TPU v7x, 128 devices: a whole 4x4x4 slice. The times are simulated.
128 devices in a mesh: band: 4 (over x), pts: 32 (over z, y, core).
Axes of the slice: x: 4, y: 4, z: 4, core: 2. Of those that a mesh axis runs over, the one named last changes fastest.
Arguments:
- spectra: float32 [16, 36, 36, 4096], P(None, 'band', None, 'pts'), may hold values from 0.05 to 1
- currents: float32 [2, 3, 16, 4096], P(None, None, 'band', 'pts'), may hold values from -4 to 4
- bathymetry: float32 [16, 4096], P('band', 'pts'), may hold values from 10 to 4000
- sea_mask: int32 [16, 4096], P('band', 'pts'), may hold values 0 or 1
Outputs:
- spectra_out: float32 [16, 36, 36, 4096], P(None, 'band', None, 'pts')
Inputs may be any that keep to these rules, and one draw needn't show every extreme that they name: `sea_mask`: 1 marks a sea point, 0 land or ice.
All inputs are finite; a program needn't handle non-finite values. No bound on the sum of `sea_mask` on one device may be relied on, other than what follows from the above.
Results may differ from a plain program's by a relative error of at most 0.0001.
Values sent between devices are 32-bit elements; how exact they have to be, the bound alone decides.
No kernel may reach another device: no remote copies, remote signals or barrier semaphores. Data moves between devices by JAX's collectives and lax.ppermute only.
A program may use at most 192 MiB of HBM per device.

v0:
```python
import math

import jax
import jax.numpy as jnp
from jax import lax
from jax.sharding import PartitionSpec as P

GRAVITY = 9.81
COURANT = 0.02
DISSIPATION = 1.0
MOMENT_FLOOR = 0.01
FREQ_FIRST = 0.035
FREQ_STEP = 1.1
BAND_WIDTH = 0.0955


def padded_2(block, sides, width):
    for axis, dim in sides:
        count = lax.axis_size(axis)
        forward = [(i, i + 1) for i in range(count - 1)]
        forward.append((count - 1, 0))
        backward = [(target, source) for source, target in forward]
        low = lax.ppermute(
            lax.slice_in_dim(block, block.shape[dim] - width, None, axis=dim), axis, forward
        )
        high = lax.ppermute(lax.slice_in_dim(block, 0, width, axis=dim), axis, backward)
        block = jnp.concatenate([low, block, high], axis=dim)
    return block


def celerity_all(frequency, water_depth):
    angular = 2.0 * math.pi * frequency[None, :, None, None]
    height = water_depth[:, None, None, :]
    deep_wavenumber = angular * angular / GRAVITY
    wavenumber = deep_wavenumber / jnp.sqrt(jnp.tanh(deep_wavenumber * height))
    scaled_depth = 2.0 * wavenumber * height
    depth_ratio = 2.0 * scaled_depth * jnp.exp(-scaled_depth) / (1.0 - jnp.exp(-2.0 * scaled_depth))
    return 0.5 * (1.0 + depth_ratio) * angular / wavenumber


def flux_parts(energy, celerity, current_along, direction_table):
    velocity = celerity * direction_table + current_along[:, None, None, :]
    return (jnp.maximum(velocity, 0.0) * energy, jnp.minimum(velocity, 0.0) * energy)


def north_south(plus_y, minus_y):
    zero_row = jnp.zeros_like(plus_y[:1])
    return (
        plus_y
        + jnp.concatenate([minus_y[1:], zero_row], 0)
        - jnp.concatenate([zero_row, plus_y[:-1]], 0)
        - minus_y
    )


def relax(energy, frequency):
    dir_count = energy.shape[2]
    weight = BAND_WIDTH * (2.0 * math.pi / dir_count) * frequency
    level = jnp.sum(energy, axis=2)
    zeroth = jnp.sum(level * weight[None, :, None], axis=1)
    first_moment = jnp.sum(level * (weight * frequency)[None, :, None], axis=1)
    zeroth, first_moment = lax.psum((zeroth, first_moment), "band")
    mean_freq = first_moment / jnp.maximum(zeroth, MOMENT_FLOOR)
    strength = DISSIPATION * zeroth * mean_freq
    return energy / (
        1.0 + strength[:, None, None, :] * (frequency * frequency)[None, :, None, None]
    )


def per_device(spectra, currents, bathymetry, sea_mask):
    substeps = currents.shape[0]
    block_rows = currents.shape[2]
    col_count = currents.shape[3]
    stacked = currents.reshape(substeps * 3, block_rows, col_count)
    forcing = jnp.concatenate([stacked, bathymetry[None], sea_mask.astype(jnp.float32)[None]], 0)
    strip_forcing = lax.all_gather(forcing, "band", axis=1, tiled=True)
    band_freqs = spectra.shape[1]
    dir_count = spectra.shape[2]
    first_index = lax.axis_index("band") * band_freqs
    frequency = FREQ_FIRST * jnp.exp(
        (first_index + jnp.arange(band_freqs, dtype=jnp.int32)).astype(jnp.float32)
        * math.log(FREQ_STEP)
    )
    angles = jnp.arange(dir_count, dtype=jnp.float32) * (2.0 * math.pi / dir_count)
    cosine_table = jnp.cos(angles)[None, None, :, None]
    sine_table = jnp.sin(angles)[None, None, :, None]
    energy = lax.all_to_all(spectra, "pts", split_axis=3, concat_axis=3, tiled=True)
    wet_mask = strip_forcing[3 * substeps + 1][:, None, None, :]
    energy = energy * wet_mask
    for substep in range(substeps):
        water_depth = strip_forcing[3 * substeps] + strip_forcing[3 * substep + 2]
        celerity = celerity_all(frequency, water_depth)
        plus_x, minus_x = flux_parts(energy, celerity, strip_forcing[3 * substep], cosine_table)
        plus_y, minus_y = flux_parts(energy, celerity, strip_forcing[3 * substep + 1], sine_table)
        boundary = jnp.concatenate([minus_x[..., :1], plus_x[..., -1:]], axis=3)
        padded = padded_2(boundary, (("pts", 3),), 1)
        inflow_low = jnp.concatenate([padded[..., :1], plus_x[..., :-1]], 3)
        inflow_high = jnp.concatenate([minus_x[..., 1:], padded[..., 3:]], 3)
        diverge_x = plus_x + inflow_high - inflow_low - minus_x
        diverge_y = north_south(plus_y, minus_y)
        energy = (energy - COURANT * (diverge_x + diverge_y)) * wet_mask
        energy = relax(energy, frequency)
    result = lax.all_to_all(energy, "pts", split_axis=3, concat_axis=3, tiled=True)
    return result


def solution(mesh):
    in_specs = (
        P(None, "band", None, "pts"),
        P(None, None, "band", "pts"),
        P("band", "pts"),
        P("band", "pts"),
    )
    out_specs = P(None, "band", None, "pts")
    return jax.shard_map(
        per_device, mesh=mesh, in_specs=in_specs, out_specs=out_specs, check_vma=False
    )
```

profile of v0, /device:TPU:0, one launch (start us, length us, event | category | flops | bytes accessed | tf_op | source)
XLA Modules:
  0.0 345.5 jit_solution(3888334856076439188)
XLA Ops:
  0.0 9.8 %copy.117 = f32[16,9,36,128]{2,0,1,3:T(8,128)} copy(f32[16,9,36,128]{3,0,2,1:T(8,128)} %param.4) | data formatting | bytes 5308416 | tf_op args[0]
  9.8 13.7 %reshape.156 = f32[32,1,20736]{2,1,0:T(1,128)} reshape(f32[128,9,16,36]{3,2,1,0:T(8,128)} %bitcast.45) | data formatting | bytes 5308416
  23.6 8.4 %all-to-all-start = ((f32[32,1,20736]{2,1,0:T(1,128)}), f32[32,1,20736]{2,1,0:T(1,128)S(1)}, u32[]{:S(2)}, u32[]{:S(2)}) async-start(f32[32,1,20736]{2,1,0:T(1,128)} %reshape.156), calls=%async_computation | async-start | bytes 5308416 | tf_op jit(solution)/shard_map/all_to_all | solution.py:87
  32.1 12.7 %all_gather.3 = f32[8,16,128]{2,0,1:T(8,128)S(1)} all-gather(f32[8,4,128]{2,0,1:T(8,128)S(1)} %copy.118), channel_id=1, replica_groups=mesh['band'=4,'pts'=32] {'band'}, dimensions={1}, use_global_device_ids=true | all-gather | bytes 81920 | tf_op jit(solution)/shard_map/all_gather | solution.py:76
  44.8 0.1 copy.119
  44.9 0.1 copy.128
  45.0 0.1 copy.123
  45.1 0.2 multiply_divide_fusion.1
  45.3 1.4 copy.122
  46.8 21.6 %all-to-all-done = f32[32,1,20736]{2,1,0:T(1,128)S(1)} async-done(((f32[32,1,20736]{2,1,0:T(1,128)}), f32[32,1,20736]{2,1,0:T(1,128)S(1)}, u32[]{:S(2)}, u32[]{:S(2)}) %all-to-all-start) | async-done | bytes 2654240 | tf_op jit(solution)/shard_map/all_to_all | solution.py:87
  68.4 0.5 broadcast.315
  68.9 9.1 %reduce = f32[32,20736]{1,0:T(8,128)} reduce(f32[32,1,20736]{2,1,0:T(1,128)S(1)} %all-to-all-done, f32[]{:T(128)} %broadcast.315), dimensions={1}, to_apply=%all_to_all.6.reduce_sub_computation | reduce | bytes 5308420 | tf_op jit(solution)/shard_map/all_to_all | solution.py:87
  78.0 14.8 %reshape.157 = f32[128,9,16,36]{3,2,1,0:T(8,128)} reshape(f32[32,20736]{1,0:T(8,128)} %reduce) | data formatting | bytes 5308416
  92.9 11.2 %minimum_multiply_fusion.3 = (f32[16,9,36,128]{2,0,1,3:T(8,128)S(1)}, f32[16,9,36,128]{2,0,1,3:T(8,128)S(1)}, f32[16,9,36,128]{2,0,1,3:T(8,128)}, f32[16,9,36,128]{2,0,1,3:T(8,128)}) fusion(f32[16,128]{0,1:T(8,128)S(1)} %copy.123, f32[36]{0:T(128)S(1)} %get-tuple-element.47, f32[16,9,128]{0,1,2:T(8,128)S(1)} %copy-done.3, f32[16,128]{0,1:T(8,128)S(1)} %copy.119, ...), kind=kLoop, calls=%fused_computation.23 | loop fusion | flops 8626176 | bytes 13369632 | tf_op jit(solution)/shard_map/mul | solution.py:43
  104.1 0.7 slice_bitcast_fusion.3
  104.7 3.0 copy-done
  107.7 1.4 slice_bitcast_fusion.2
  109.1 1.4 copy-done.1
  110.5 5.2 %collective-permute-start = (f32[16,9,36,1]{2,0,3,1:T(8,128)}, f32[16,9,36,1]{2,0,3,1:T(8,128)S(1)}, u32[]{:S(2)}, u32[]{:S(2)}) collective-permute-start(f32[16,9,36,1]{2,0,3,1:T(8,128)} %slice_bitcast_fusion.3), channel_id=1, source_target_pairs={{1,0},{2,1},{3,2},{4,3},{5,4},{6,5},{7,6},{8,7},{9,8},{10,9},{11,1... | collective-permute-start | bytes 62216 | tf_op jit(solution)/shard_map/ppermute | solution.py:26
  115.8 0.1 copy.133
  115.9 0.1 copy.138
  116.0 1.4 copy.132
  117.4 8.3 %slice.85 = f32[16,9,36,127]{2,0,1,3:T(8,128)} slice(f32[16,9,36,128]{2,0,1,3:T(8,128)} %copy-done.1), slice={[0:16], [0:9], [0:36], [1:128]} | slice | bytes 5266944 | tf_op jit(solution)/shard_map/slice | solution.py:98
  125.8 5.4 %slice.88 = f32[16,9,36,127]{2,0,1,3:T(8,128)} slice(f32[16,9,36,128]{2,0,1,3:T(8,128)S(1)} %bitcast.47), slice={[0:16], [0:9], [0:36], [0:127]} | slice | bytes 5266944 | tf_op jit(solution)/shard_map/slice | solution.py:97
  131.1 5.0 %slice.90 = f32[15,9,36,128]{2,0,1,3:T(8,128)S(1)} slice(f32[16,9,36,128]{2,0,1,3:T(8,128)} %get-tuple-element.30), slice={[1:16], [0:9], [0:36], [0:128]} | slice | bytes 4976640 | tf_op jit(solution)/shard_map/slice | solution.py:50
  136.2 20.9 %fusion.16 = (f32[16,9,128]{0,1,2:T(8,128)}, f32[16,9,36,128]{2,0,1,3:T(8,128)}) fusion(f32[15,9,36,128]{2,0,1,3:T(8,128)} %bitcast.42, f32[15,9,36,128]{2,0,1,3:T(8,128)S(1)} %slice.90, f32[16,128]{0,1:T(8,128)S(1)} %copy.128, f32[36]{0:T(128)S(1)} %get-tuple-element.46, f32[16,9,36,127]{2,0,1,3:T(8,128)} %slice.88, f32[16,9,36,1]{2,0,1,3:T(8,128)S(1)} %bitcast.48, ...), kind=kLoop, calls=%fused_computation.60 | loop fusion | flops 17233920 | bytes 15765792 | tf_op jit(solution)/shard_map/reduce_sum | solution.py:59
  157.1 1.4 copy.142
  158.7 16.9 %all-reduce.5 = (f32[16,128]{1,0:T(8,128)S(1)}, f32[16,128]{1,0:T(8,128)S(1)}) all-reduce(f32[16,128]{1,0:T(8,128)S(1)} %get-tuple-element.8, f32[16,128]{1,0:T(8,128)S(1)} %get-tuple-element.7), channel_id=1, replica_groups=mesh['band'=4,'pts'=32] {'band'}, use_global_device_ids=true, to_apply=%region_2.0 | all-reduce | flops 4096 | bytes 32768 | tf_op jit(solution)/shard_map/psum | solution.py:62
  175.6 0.1 multiply_add_fusion.5
  175.7 1.4 copy.130
  177.1 9.2 %minimum_multiply_fusion.1 = (f32[16,9,36,128]{2,0,1,3:T(8,128)S(1)}, f32[16,9,36,128]{2,0,1,3:T(8,128)S(1)}, f32[16,9,36,128]{2,0,1,3:T(8,128)}, f32[16,9,36,128]{2,0,1,3:T(8,128)S(1)}) fusion(f32[16,128]{0,1:T(8,128)S(1)} %copy.133, f32[16,9,128]{0,1,2:T(8,128)} %copy.132, f32[36]{0:T(128)S(1)} %get-tuple-element.47, ...), kind=kLoop, calls=%fused_computation.17 | loop fusion | flops 8626176 | bytes 13435168 | tf_op jit(solution)/shard_map/mul | solution.py:43
  186.4 3.7 %copy-done.2 = f32[16,9,36,128]{2,0,1,3:T(8,128)} copy-done((f32[16,9,36,128]{2,0,1,3:T(8,128)}, f32[16,9,36,128]{2,0,1,3:T(8,128)S(1)}, u32[]{:S(2)}) %copy-start.2) | copy-done | bytes 2654232
  190.1 0.6 slice_bitcast_fusion
  190.7 5.1 %collective-permute-start.2 = (f32[16,9,36,1]{2,0,3,1:T(8,128)S(1)}, f32[16,9,36,1]{2,0,3,1:T(8,128)S(1)}, u32[]{:S(2)}, u32[]{:S(2)}) collective-permute-start(f32[16,9,36,1]{2,0,3,1:T(8,128)S(1)} %slice_bitcast_fusion.1), channel_id=1, source_target_pairs={{1,0},{2,1},{3,2},{4,3},{5,4},{6,5},{7,6},{8,7},{9,8},{10,9},{11,1... | collective-permute-start | bytes 62216 | tf_op jit(solution)/shard_map/ppermute | solution.py:26
  195.8 4.2 %slice.94 = f32[16,9,36,127]{2,0,1,3:T(8,128)} slice(f32[16,9,36,128]{2,0,1,3:T(8,128)S(1)} %get-tuple-element.19), slice={[0:16], [0:9], [0:36], [1:128]} | slice | bytes 5266944 | tf_op jit(solution)/shard_map/slice | solution.py:98
  200.0 8.3 %slice.97 = f32[16,9,36,127]{2,0,1,3:T(8,128)} slice(f32[16,9,36,128]{2,0,1,3:T(8,128)} %copy-done.2), slice={[0:16], [0:9], [0:36], [0:127]} | slice | bytes 5266944 | tf_op jit(solution)/shard_map/slice | solution.py:97
  208.3 4.6 %slice.99 = f32[15,9,36,128]{2,0,1,3:T(8,128)} slice(f32[16,9,36,128]{2,0,1,3:T(8,128)S(1)} %get-tuple-element.24), slice={[1:16], [0:9], [0:36], [0:128]} | slice | bytes 4976640 | tf_op jit(solution)/shard_map/slice | solution.py:50
  213.0 19.7 %fusion.14 = (f32[16,9,128]{0,1,2:T(8,128)}, f32[16,9,36,128]{2,0,1,3:T(8,128)}) fusion(f32[16,128]{0,1:T(8,128)S(1)} %copy.119, f32[15,9,36,128]{2,0,1,3:T(8,128)} %bitcast.43, f32[15,9,36,128]{2,0,1,3:T(8,128)} %slice.99, f32[16,128]{0,1:T(8,128)S(1)} %copy.138, f32[36]{0:T(128)S(1)} %get-tuple-element.46, f32[16,9,36,127]{2,0,1,3:T(8,128)} %slice.97, ...), kind=kLoop, calls=%fused_computation.59 | loop fusion | flops 17233920 | bytes 15839520 | tf_op jit(solution)/shard_map/reduce_sum | solution.py:59
  232.7 1.4 copy.143
  234.2 14.5 %all-reduce.4 = (f32[16,128]{1,0:T(8,128)S(1)}, f32[16,128]{1,0:T(8,128)S(1)}) all-reduce(f32[16,128]{1,0:T(8,128)S(1)} %get-tuple-element.6, f32[16,128]{1,0:T(8,128)S(1)} %get-tuple-element.5), channel_id=1, replica_groups=mesh['band'=4,'pts'=32] {'band'}, use_global_device_ids=true, to_apply=%region_7.0 | all-reduce | flops 4096 | bytes 32768 | tf_op jit(solution)/shard_map/psum | solution.py:62
  248.8 0.1 multiply_add_fusion.4
  248.8 0.5 copy.140
  249.3 10.4 %fusion.19 = f32[128,9,16,36]{3,2,1,0:T(8,128)} fusion(f32[16,9,36,128]{2,0,1,3:T(8,128)} %get-tuple-element.14, f32[16,9,128]{0,1,2:T(8,128)S(1)} %copy.140), kind=kLoop, calls=%fused_computation.62 | loop fusion | flops 663552 | bytes 5382144
  259.7 13.7 %reshape.158 = f32[32,1,20736]{2,1,0:T(1,128)} reshape(f32[128,9,16,36]{3,2,1,0:T(8,128)} %fusion.19) | data formatting | bytes 5308416
  273.4 38.7 %all_to_all.10 = f32[32,1,20736]{2,1,0:T(1,128)S(1)} all-to-all(f32[32,1,20736]{2,1,0:T(1,128)} %reshape.158), channel_id=1, replica_groups=mesh['band'=4,'pts'=32] {'pts'}, dimensions={0} | all-to-all | bytes 5308416 | tf_op jit(solution)/shard_map/all_to_all | solution.py:103
  312.1 9.1 %reduce.1 = f32[32,20736]{1,0:T(8,128)} reduce(f32[32,1,20736]{2,1,0:T(1,128)S(1)} %all_to_all.10, f32[]{:T(128)} %broadcast.315), dimensions={1}, to_apply=%all_to_all.7.reduce_sub_computation | reduce | bytes 5308420 | tf_op jit(solution)/shard_map/all_to_all | solution.py:103
  321.2 14.8 %reshape.159 = f32[128,9,16,36]{3,2,1,0:T(8,128)} reshape(f32[32,20736]{1,0:T(8,128)} %reduce.1) | data formatting | bytes 5308416
  336.0 9.3 %copy.141 = f32[16,9,36,128]{3,0,2,1:T(8,128)} copy(f32[16,9,36,128]{2,0,1,3:T(8,128)} %bitcast.44) | data formatting | bytes 5308416 | tf_op jit(solution)/shard_map/all_to_all | solution.py:103
  (52 shorter events, 0.4 us)
Async XLA Ops:
  9.8 22.2 %copy-start.6 = (s32[4,128]{1,0:T(4,128)S(1)}, s32[4,128]{1,0:T(4,128)}, u32[]{:S(2)}) copy-start(s32[4,128]{1,0:T(4,128)} %param.7) | copy-start | bytes 6148
  9.8 22.2 %copy-start.4 = (f32[2,3,4,128]{3,2,1,0:T(4,128)S(1)}, f32[2,3,4,128]{3,2,1,0:T(4,128)}, u32[]{:S(2)}) copy-start(f32[2,3,4,128]{3,2,1,0:T(4,128)} %param.5) | copy-start | bytes 36868
  9.8 22.2 %copy-start.5 = (f32[4,128]{1,0:T(4,128)S(1)}, f32[4,128]{1,0:T(4,128)}, u32[]{:S(2)}) copy-start(f32[4,128]{1,0:T(4,128)} %param.6) | copy-start | bytes 6148
  23.6 44.8 %all-to-all-start = ((f32[32,1,20736]{2,1,0:T(1,128)}), f32[32,1,20736]{2,1,0:T(1,128)S(1)}, u32[]{:S(2)}, u32[]{:S(2)}) async-start(f32[32,1,20736]{2,1,0:T(1,128)} %reshape.156), calls=%async_computation | async-start | bytes 5308416 | tf_op jit(solution)/shard_map/all_to_all | solution.py:87
  78.0 14.8 %copy-start.3 = (f32[16,9,128]{0,1,2:T(8,128)S(1)}, f32[16,9,128]{0,1,2:T(8,128)}, u32[]{:S(2)}) copy-start(f32[16,9,128]{0,1,2:T(8,128)} %copy.122) | copy-start | bytes 221188
  104.0 3.7 %copy-start = (f32[16,9,36,128]{2,0,1,3:T(8,128)}, f32[16,9,36,128]{2,0,1,3:T(8,128)S(1)}, u32[]{:S(2)}) copy-start(f32[16,9,36,128]{2,0,1,3:T(8,128)S(1)} %get-tuple-element.26) | copy-start | bytes 7962628
  104.0 6.5 %copy-start.1 = (f32[16,9,36,128]{2,0,1,3:T(8,128)}, f32[16,9,36,128]{2,0,1,3:T(8,128)S(1)}, u32[]{:S(2)}) copy-start(f32[16,9,36,128]{2,0,1,3:T(8,128)S(1)} %get-tuple-element.25) | copy-start | bytes 7962628
  110.5 25.6 %collective-permute-start.1 = (f32[16,9,36,1]{2,0,3,1:T(8,128)}, f32[16,9,36,1]{2,0,3,1:T(8,128)S(1)}, u32[]{:S(2)}, u32[]{:S(2)}) collective-permute-start(f32[16,9,36,1]{2,0,3,1:T(8,128)} %slice_bitcast_fusion.2), channel_id=1, source_target_pairs={{0,1},{1,2},{2,3},{3,4},{4,5},{5,6},{6,7},{7,8},{8,9},{9,10},{10,1... | collective-permute-start | bytes 62216 | tf_op jit(solution)/shard_map/ppermute | solution.py:23
  110.5 25.6 %collective-permute-start = (f32[16,9,36,1]{2,0,3,1:T(8,128)}, f32[16,9,36,1]{2,0,3,1:T(8,128)S(1)}, u32[]{:S(2)}, u32[]{:S(2)}) collective-permute-start(f32[16,9,36,1]{2,0,3,1:T(8,128)} %slice_bitcast_fusion.3), channel_id=1, source_target_pairs={{1,0},{2,1},{3,2},{4,3},{5,4},{6,5},{7,6},{8,7},{9,8},{10,9},{11,1... | collective-permute-start | bytes 62216 | tf_op jit(solution)/shard_map/ppermute | solution.py:26
  116.0 9.7 %slice-start.6 = ((s8[9437184]{0:T(1024)(128)(4,1)}), s8[1048576]{0:T(1024)(128)(4,1)S(1)}, s32[]{:S(2)}) async-start(s8[9437184]{0:T(1024)(128)(4,1)} %bitcast.46), calls=%async_computation.8 | async-start | bytes 2097152
  117.4 8.3 %slice-start.7 = ((s8[9437184]{0:T(1024)(128)(4,1)}), s8[4194304]{0:T(1024)(128)(4,1)S(1)}, s32[]{:S(2)}) async-start(s8[9437184]{0:T(1024)(128)(4,1)} %bitcast.46), calls=%async_computation.9 | async-start | bytes 8388608
  117.4 8.3 %slice-start.8 = ((s8[9437184]{0:T(1024)(128)(4,1)}), s8[4194304]{0:T(1024)(128)(4,1)S(1)}, s32[]{:S(2)}) async-start(s8[9437184]{0:T(1024)(128)(4,1)} %bitcast.46), calls=%async_computation.10 | async-start | bytes 8388608
  125.7 10.4 %slice-start.3 = ((s8[9437184]{0:T(1024)(128)(4,1)}), s8[4194304]{0:T(1024)(128)(4,1)S(1)}, s32[]{:S(2)}) async-start(s8[9437184]{0:T(1024)(128)(4,1)} %bitcast.40), calls=%async_computation.5 | async-start | bytes 8388608
  125.7 10.4 %slice-start.4 = ((s8[9437184]{0:T(1024)(128)(4,1)}), s8[4194304]{0:T(1024)(128)(4,1)S(1)}, s32[]{:S(2)}) async-start(s8[9437184]{0:T(1024)(128)(4,1)} %bitcast.40), calls=%async_computation.6 | async-start | bytes 8388608
  131.1 5.0 %slice-start.5 = ((s8[9437184]{0:T(1024)(128)(4,1)}), s8[1048576]{0:T(1024)(128)(4,1)S(1)}, s32[]{:S(2)}) async-start(s8[9437184]{0:T(1024)(128)(4,1)} %bitcast.40), calls=%async_computation.7 | async-start | bytes 2097152
  186.4 3.7 %copy-start.2 = (f32[16,9,36,128]{2,0,1,3:T(8,128)}, f32[16,9,36,128]{2,0,1,3:T(8,128)S(1)}, u32[]{:S(2)}) copy-start(f32[16,9,36,128]{2,0,1,3:T(8,128)S(1)} %get-tuple-element.20) | copy-start | bytes 7962628
  190.7 22.2 %collective-permute-start.3 = (f32[16,9,36,1]{2,0,3,1:T(8,128)}, f32[16,9,36,1]{2,0,3,1:T(8,128)S(1)}, u32[]{:S(2)}, u32[]{:S(2)}) collective-permute-start(f32[16,9,36,1]{2,0,3,1:T(8,128)} %slice_bitcast_fusion), channel_id=1, source_target_pairs={{0,1},{1,2},{2,3},{3,4},{4,5},{5,6},{6,7},{7,8},{8,9},{9,10},{10,1... | collective-permute-start | bytes 62216 | tf_op jit(solution)/shard_map/ppermute | solution.py:23
  190.7 22.2 %collective-permute-start.2 = (f32[16,9,36,1]{2,0,3,1:T(8,128)S(1)}, f32[16,9,36,1]{2,0,3,1:T(8,128)S(1)}, u32[]{:S(2)}, u32[]{:S(2)}) collective-permute-start(f32[16,9,36,1]{2,0,3,1:T(8,128)S(1)} %slice_bitcast_fusion.1), channel_id=1, source_target_pairs={{1,0},{2,1},{3,2},{4,3},{5,4},{6,5},{7,6},{8,7},{9,8},{10,9},{11,1... | collective-permute-start | bytes 62216 | tf_op jit(solution)/shard_map/ppermute | solution.py:26
  200.0 13.0 %slice-start = ((s8[9437184]{0:T(1024)(128)(4,1)}), s8[4194304]{0:T(1024)(128)(4,1)S(1)}, s32[]{:S(2)}) async-start(s8[9437184]{0:T(1024)(128)(4,1)} %bitcast.38), calls=%async_computation.2 | async-start | bytes 8388608
  200.0 13.0 %slice-start.1 = ((s8[9437184]{0:T(1024)(128)(4,1)}), s8[4194304]{0:T(1024)(128)(4,1)S(1)}, s32[]{:S(2)}) async-start(s8[9437184]{0:T(1024)(128)(4,1)} %bitcast.38), calls=%async_computation.3 | async-start | bytes 8388608
  208.3 4.6 %slice-start.2 = ((s8[9437184]{0:T(1024)(128)(4,1)}), s8[1048576]{0:T(1024)(128)(4,1)S(1)}, s32[]{:S(2)}) async-start(s8[9437184]{0:T(1024)(128)(4,1)} %bitcast.38), calls=%async_computation.4 | async-start | bytes 2097152
where the time goes:
time: 351 us; the launch traced here: 346 us
  local copies, waits for them, and re-layouts  132 us (38%)
  other arithmetic  90.3 us (26%)
  blocking collectives  82.8 us (24%)
  waiting for transfers between devices  21.6 us (6%)
  starting transfers between devices  18.7 us (5%)
    unnamed x39, local copies, waits for them, and re-layouts  78 us
    reduce_sum x2, other arithmetic, relax(): level = jnp.sum(energy, axis=2)  40.7 us
    all_to_all x1, blocking collectives, per_device(): lax.all_to_all(energy, 'pts', split_axis=3, concat_axis=3, tiled=True)  38.7 us
    psum x2, blocking collectives, relax(): zeroth, first_moment = lax.psum((zeroth, first_moment), 'band')  31.4 us
    all_to_all x1, waiting for transfers between devices, per_device(): lax.all_to_all(spectra, 'pts', split_axis=3, concat_axis=3, tiled=True)  21.6 us
    mul x2, other arithmetic, flux_parts(): jnp.minimum(velocity, 0.0) * energy  20.4 us
    slice x2, local copies, waits for them, and re-layouts, per_device(): inflow_low = jnp.concatenate([padded[..., :1], plus_x[..., :-1]], 3)  13.7 us
    all_gather x1, blocking collectives, per_device(): strip_forcing = lax.all_gather(forcing, 'band', axis=1, tiled=True)  12.7 us
  transfers between devices with their start and end apart: 5, of which 1 were waited for; matrix products, arithmetic and copies ran while one was open for 11% of the time, Pallas kernels for 0%

commit v1 on v0

v1 whole, which is shorter than its diff:
```python
import math

import jax
import jax.numpy as jnp
from jax import lax
from jax.experimental import pallas as pl
from jax.experimental.pallas import tpu as pltpu
from jax.sharding import PartitionSpec as P

GRAVITY = 9.81
COURANT = 0.02
DISSIPATION = 1.0
MOMENT_FLOOR = 0.01
FREQ_FIRST = 0.035
FREQ_STEP = 1.1
BAND_WIDTH = 0.0955
ND = 36
NQ = 9
NFB = 9
ROWS = 16
BANDS = 4
PTS = 32
SUBSTEPS = 2
FIELDS = 8
LANES = 128
F32 = jnp.float32
VMEM_LIMIT = 40 * 1024 * 1024
VM = pl.BlockSpec(memory_space=pltpu.VMEM)
SM = pl.BlockSpec(memory_space=pltpu.SMEM)
PARAMS = pltpu.CompilerParams(vmem_limit_bytes=VMEM_LIMIT)


def lane_group():
    return lax.broadcasted_iota(jnp.int32, (ROWS, LANES), 1) & 3


def lroll(x, shift):
    return pltpu.roll(x, shift % LANES, 1)


def quad_transpose(a):
    lane = lane_group()
    low = lane < 2
    even = (lane & 1) == 0
    b0 = jnp.where(low, a[0], lroll(a[2], 2))
    b2 = jnp.where(low, lroll(a[0], -2), a[2])
    b1 = jnp.where(low, a[1], lroll(a[3], 2))
    b3 = jnp.where(low, lroll(a[1], -2), a[3])
    return (
        jnp.where(even, b0, lroll(b1, 1)),
        jnp.where(even, lroll(b0, -1), b1),
        jnp.where(even, b2, lroll(b3, 1)),
        jnp.where(even, lroll(b2, -1), b3),
    )


def quad_spread(x):
    lane = lane_group()
    low = lane < 2
    even = (lane & 1) == 0
    b0 = jnp.where(low, x, lroll(x, 2))
    b2 = jnp.where(low, lroll(x, -2), x)
    return (
        jnp.where(even, b0, lroll(b0, 1)),
        jnp.where(even, lroll(b0, -1), b0),
        jnp.where(even, b2, lroll(b2, 1)),
        jnp.where(even, lroll(b2, -1), b2),
    )


def quad_sum(x):
    lane = lane_group()
    x = x + jnp.where((lane & 1) == 0, lroll(x, -1), lroll(x, 1))
    return x + jnp.where(lane < 2, lroll(x, -2), lroll(x, 2))


def select4(x):
    lane = lane_group()
    return jnp.where(
        lane < 2, jnp.where(lane == 0, x[0], x[1]), jnp.where(lane == 2, x[2], x[3])
    )


def frequency_of(index):
    return FREQ_FIRST * jnp.exp(
        jnp.full((ROWS, LANES), index, jnp.int32).astype(F32) * math.log(FREQ_STEP)
    )


def edge_shifts(pts):
    left = jnp.where(pts == 0, 4, 0)
    right = jnp.where(pts == PTS - 1, LANES - 4, 0)
    return left, right


def pack_kernel(e_ref, ml_ref, mr_ref):
    for f in range(e_ref.shape[0]):
        for d in range(NQ):
            out = quad_transpose([e_ref[f, d + NQ * q] for q in range(4)])
            ml_ref[0, f, d] = out[0]
            ml_ref[1, f, d] = out[1]
            mr_ref[0, f, d] = out[2]
            mr_ref[1, f, d] = out[3]


def pack(spectra):
    fb = 3
    shape = jax.ShapeDtypeStruct((2, NFB, NQ, ROWS, LANES), F32)
    spec = pl.BlockSpec((2, fb, NQ, ROWS, LANES), lambda i: (0, i, 0, 0, 0))
    return pl.pallas_call(
        pack_kernel,
        grid=(NFB // fb,),
        in_specs=[pl.BlockSpec((fb, ND, ROWS, LANES), lambda i: (i, 0, 0, 0))],
        out_specs=[spec, spec],
        out_shape=[shape, shape],
        compiler_params=PARAMS,
        name="pack",
    )(spectra)


def exact_dot(a, b, dims):
    return lax.dot_general(
        a, b, (dims, ((), ())), precision=lax.Precision.HIGHEST, preferred_element_type=F32
    )


def forcing_kernel(at, f0, f1, f2, f3, out_ref, scr, full):
    band = at[0]
    for k, ref in enumerate((f0, f1, f2, f3)):
        scr[band ^ k] = ref[...]
    for q in range(BANDS):
        full[:, 4 * q : 4 * q + 4, :] = scr[q]
    shape = (8 * PTS, LANES)
    place = lax.broadcasted_iota(jnp.int32, shape, 0)
    wanted = (4 * (place >> 3) + (place & 7) + (LANES - 2)) & (LANES - 1)
    pick = (lax.broadcasted_iota(jnp.int32, shape, 1) == wanted).astype(F32)
    windows = exact_dot(pick, full[...].reshape(LANES, LANES), ((1,), (1,)))
    out_ref[...] = windows.reshape(PTS, 8, LANES)


def forcing_windows(at, parts):
    return pl.pallas_call(
        forcing_kernel,
        in_specs=[SM] + [VM] * 4,
        out_specs=VM,
        out_shape=jax.ShapeDtypeStruct((PTS, 8, LANES), F32),
        scratch_shapes=[
            pltpu.VMEM((BANDS, FIELDS, 4, LANES), F32),
            pltpu.VMEM((FIELDS, ROWS, LANES), F32),
        ],
        compiler_params=PARAMS,
        name="forcing",
    )(at, *parts)


def speed_kernel(at, win, c_ref, u_ref, v_ref, w_ref, t_ref, h_scr, f_scr):
    left, right = edge_shifts(at[1])
    shape = (PTS, LANES)
    place = lax.broadcasted_iota(jnp.int32, shape, 0)
    spread = ((lax.broadcasted_iota(jnp.int32, shape, 1) >> 2) == place).astype(F32)
    for i in range(8):
        fields = exact_dot(win[:, i, :], spread, ((0,), (0,)))
        if i < 2:
            fields = pltpu.roll(fields, left, 1)
        if i >= 6:
            fields = pltpu.roll(fields, right, 1)
        f_scr[i] = fields.reshape(FIELDS, ROWS, LANES)
    for i in range(8):
        w_ref[i] = f_scr[i, 7]
        for s in range(SUBSTEPS):
            u_ref[s, i] = COURANT * f_scr[i, 3 * s]
            v_ref[s, i] = COURANT * f_scr[i, 3 * s + 1]
    for s in range(SUBSTEPS):
        depth = [f_scr[i, 6] + f_scr[i, 3 * s + 2] for i in range(8)]
        h_scr[s, 0] = select4(depth[2:6])
        h_scr[s, 1] = select4([depth[6], depth[7], depth[0], depth[1]])

    def columns(x, y):
        a, b = quad_spread(x), quad_spread(y)
        return (b[2], b[3]) + a + (b[0], b[1])

    for d in range(NQ):
        angle = (d + NQ * lane_group()[0:8]).astype(F32) * (2.0 * math.pi / ND)
        t_ref[0, d] = jnp.cos(angle)
        t_ref[1, d] = jnp.sin(angle)
    first = at[0] * NFB

    def body(f, carry):
        angular = (2.0 * math.pi) * frequency_of(first + f)
        deep = angular * angular / GRAVITY
        for s in range(SUBSTEPS):
            speed = []
            for part in range(2):
                height = h_scr[s, part]
                wavenumber = deep / jnp.sqrt(jnp.tanh(deep * height))
                q = 2.0 * wavenumber * height
                ratio = 2.0 * q * jnp.exp(-q) / (1.0 - jnp.exp(-2.0 * q))
                speed.append((0.5 * COURANT) * (1.0 + ratio) * angular / wavenumber)
            for i, x in enumerate(columns(*speed)):
                c_ref[s, f, i] = x
        return carry

    lax.fori_loop(0, NFB, body, 0)


def speeds(at, windows):
    return pl.pallas_call(
        speed_kernel,
        in_specs=[SM, VM],
        out_specs=[VM] * 5,
        out_shape=[
            jax.ShapeDtypeStruct((SUBSTEPS, NFB, 8, ROWS, LANES), F32),
            jax.ShapeDtypeStruct((SUBSTEPS, 8, ROWS, LANES), F32),
            jax.ShapeDtypeStruct((SUBSTEPS, 8, ROWS, LANES), F32),
            jax.ShapeDtypeStruct((8, ROWS, LANES), F32),
            jax.ShapeDtypeStruct((2, NQ, 8, LANES), F32),
        ],
        scratch_shapes=[
            pltpu.VMEM((SUBSTEPS, 2, ROWS, LANES), F32),
            pltpu.VMEM((8, FIELDS, ROWS, LANES), F32),
        ],
        compiler_params=PARAMS,
        name="speeds",
    )(at, windows)


def row_below(x):
    first = lax.broadcasted_iota(jnp.int32, (8, LANES), 0) == 0
    t0, t1 = pltpu.roll(x[0:8], 1, 0), pltpu.roll(x[8:16], 1, 0)
    return jnp.concatenate([jnp.where(first, 0.0, t0), jnp.where(first, t0, t1)], axis=0)


def row_above(x):
    last = lax.broadcasted_iota(jnp.int32, (8, LANES), 0) == 7
    t0, t1 = pltpu.roll(x[0:8], 7, 0), pltpu.roll(x[8:16], 7, 0)
    return jnp.concatenate([jnp.where(last, t1, t0), jnp.where(last, 0.0, t1)], axis=0)


def advance(count, energy, speed, current_x, current_y, wet, cos, sin, store):
    inflow = None
    part = None
    for i in range(count):
        e = energy(i)
        c = speed(i)
        a = (c * cos + current_x(i)) * e
        if part is not None:
            store(i - 1, (part - jnp.minimum(a, 0.0)) * wet(i - 1))
        if 0 < i < count - 1:
            b = (c * sin + current_y(i)) * e
            turn = row_below(jnp.maximum(b, 0.0)) - row_above(jnp.minimum(b, 0.0))
            part = e - (jnp.abs(a) + jnp.abs(b)) + (inflow + turn)
        inflow = jnp.maximum(a, 0.0)


def twice(x):
    return jnp.concatenate([x, x], axis=0)


def add_moments(acc, levels, freq):
    weight = (BAND_WIDTH * (2.0 * math.pi / ND)) * freq
    for i, level in enumerate(levels):
        t = level * weight
        acc[0, i] = acc[0, i] + t
        acc[1, i] = acc[1, i] + t * freq


def first_kernel(at, lh, ml, mr, rh, c_ref, u_ref, v_ref, w_ref, t_ref, out_ref, mom_ref, acc):
    left, right = edge_shifts(at[1])
    first = at[0] * NFB
    acc[...] = jnp.zeros_like(acc)

    def body(f, carry):
        levels = [None] * 6
        for d in range(NQ):

            def energy(i):
                e = (lh, ml, mr, rh)[i // 2][i % 2, f, d]
                if i < 2:
                    e = pltpu.roll(e, left, 1)
                if i >= 6:
                    e = pltpu.roll(e, right, 1)
                return e * w_ref[i]

            def store(i, value):
                out_ref[i - 1, f, d] = value
                old = levels[i - 1]
                levels[i - 1] = value if old is None else old + value

            advance(
                8,
                energy,
                lambda i: c_ref[0, f, i],
                lambda i: u_ref[0, i],
                lambda i: v_ref[0, i],
                lambda i: w_ref[i],
                twice(t_ref[0, d]),
                twice(t_ref[1, d]),
                store,
            )
        add_moments(acc, levels, frequency_of(first + f))
        return carry

    lax.fori_loop(0, NFB, body, 0)
    for m in range(2):
        sums = [quad_sum(acc[m, i]) for i in range(6)]
        mom_ref[m, 0] = select4(sums[1:5])
        mom_ref[m, 1] = jnp.where(lane_group() < 2, sums[0], sums[5])


def first_step(at, lh, ml, mr, rh, c, u, v, w, t):
    return pl.pallas_call(
        first_kernel,
        in_specs=[SM] + [VM] * 9,
        out_specs=[VM] * 2,
        out_shape=[
            jax.ShapeDtypeStruct((6, NFB, NQ, ROWS, LANES), F32),
            jax.ShapeDtypeStruct((2, 2, ROWS, LANES), F32),
        ],
        scratch_shapes=[pltpu.VMEM((2, 6, ROWS, LANES), F32)],
        compiler_params=PARAMS,
        name="first_step",
    )(at, lh, ml, mr, rh, c, u, v, w, t)


def strength_of(parts, k):
    def total(m):
        a = [p[(m,) + k] for p in parts]
        return (a[0] + a[1]) + (a[2] + a[3])

    zeroth, first_moment = total(0), total(1)
    return DISSIPATION * zeroth * (first_moment / jnp.maximum(zeroth, MOMENT_FLOOR))


def second_kernel(
    at, e_ref, m0, m1, m2, m3, c_ref, u_ref, v_ref, w_ref, t_ref, out_ref, mom_ref, acc, s_scr, d_scr
):
    first = at[0] * NFB
    acc[...] = jnp.zeros_like(acc)
    own = quad_spread(strength_of((m0, m1, m2, m3), (0,)))
    edge = quad_spread(strength_of((m0, m1, m2, m3), (1,)))
    for i, x in enumerate((edge[0],) + own + (edge[2],)):
        s_scr[i] = x

    def body(f, carry):
        freq = frequency_of(first + f)
        square = freq * freq
        for i in range(6):
            d_scr[i] = 1.0 / (1.0 + s_scr[i] * square)
        levels = [None] * 4
        for d in range(NQ):

            def store(i, value):
                out_ref[i - 1, f, d] = value
                old = levels[i - 1]
                levels[i - 1] = value if old is None else old + value

            advance(
                6,
                lambda i: e_ref[i, f, d] * d_scr[i],
                lambda i: c_ref[1, f, i + 1],
                lambda i: u_ref[1, i + 1],
                lambda i: v_ref[1, i + 1],
                lambda i: w_ref[i + 1],
                twice(t_ref[0, d]),
                twice(t_ref[1, d]),
                store,
            )
        add_moments(acc, levels, freq)
        return carry

    lax.fori_loop(0, NFB, body, 0)
    for m in range(2):
        mom_ref[m] = select4([quad_sum(acc[m, i]) for i in range(4)])


def second_step(at, e, moments, c, u, v, w, t):
    return pl.pallas_call(
        second_kernel,
        in_specs=[SM] + [VM] * 10,
        out_specs=[VM] * 2,
        out_shape=[
            jax.ShapeDtypeStruct((4, NFB, NQ, ROWS, LANES), F32),
            jax.ShapeDtypeStruct((2, ROWS, LANES), F32),
        ],
        scratch_shapes=[
            pltpu.VMEM((2, 4, ROWS, LANES), F32),
            pltpu.VMEM((6, ROWS, LANES), F32),
            pltpu.VMEM((6, ROWS, LANES), F32),
        ],
        compiler_params=PARAMS,
        name="second_step",
    )(at, e, *moments, c, u, v, w, t)


def last_kernel(at, e_ref, m0, m1, m2, m3, out_ref):
    fb = e_ref.shape[1]
    first = at[0] * NFB + pl.program_id(0) * fb
    strength = strength_of((m0, m1, m2, m3), ())
    for f in range(fb):
        freq = frequency_of(first + f)
        damp = 1.0 / (1.0 + strength * (freq * freq))
        for d in range(NQ):
            out = quad_transpose([e_ref[c, f, d] for c in range(4)])
            for q in range(4):
                out_ref[f, d + NQ * q] = out[q] * damp


def last_step(at, e, moments):
    fb = 3
    small = pl.BlockSpec((2, ROWS, LANES), lambda i: (0, 0, 0))
    return pl.pallas_call(
        last_kernel,
        grid=(NFB // fb,),
        in_specs=[SM, pl.BlockSpec((4, fb, NQ, ROWS, LANES), lambda i: (0, i, 0, 0, 0))]
        + [small] * 4,
        out_specs=pl.BlockSpec((fb, ND, ROWS, LANES), lambda i: (i, 0, 0, 0)),
        out_shape=jax.ShapeDtypeStruct((NFB, ND, ROWS, LANES), F32),
        compiler_params=PARAMS,
        name="last_step",
    )(at, e, *moments)


RIGHT = [(i, (i + 1) % PTS) for i in range(PTS)]
LEFT = [(b, a) for a, b in RIGHT]


def band_parts(x):
    return [x] + [
        lax.ppermute(x, "band", [(i, i ^ k) for i in range(BANDS)]) for k in range(1, BANDS)
    ]


def per_device(spectra, currents, bathymetry, sea_mask):
    forcing = jnp.concatenate(
        [
            currents.reshape(3 * SUBSTEPS, 4, LANES),
            bathymetry[None],
            sea_mask.astype(F32)[None],
        ],
        0,
    )
    at = jnp.stack([lax.axis_index("band"), lax.axis_index("pts")]).astype(jnp.int32)
    ml, mr = pack(jnp.transpose(spectra, (1, 2, 0, 3)))
    lh = lax.ppermute(mr, "pts", RIGHT)
    rh = lax.ppermute(ml, "pts", LEFT)
    windows = forcing_windows(at, band_parts(forcing))
    windows = lax.all_to_all(windows, "pts", 0, 0, tiled=True)
    tables = speeds(at, windows)
    e, moments = first_step(at, lh, ml, mr, rh, *tables)
    e, moments = second_step(at, e, band_parts(moments), *tables)
    return jnp.transpose(last_step(at, e, band_parts(moments)), (2, 0, 1, 3))


def solution(mesh):
    in_specs = (
        P(None, "band", None, "pts"),
        P(None, None, "band", "pts"),
        P("band", "pts"),
        P("band", "pts"),
    )
    out_specs = P(None, "band", None, "pts")
    return jax.shard_map(
        per_device, mesh=mesh, in_specs=in_specs, out_specs=out_specs, check_vma=False
    )
```

time: 351 us -> 68.2 us (0.19); the launches traced: 346 us -> 67.9 us
  local copies, waits for them, and re-layouts: 132 us -> 1.76 us
  other arithmetic: 90.3 us -> 0.08 us
  blocking collectives: 82.8 us -> 11.7 us
  Pallas kernels: 0 us -> 26.1 us
  waiting for transfers between devices: 21.6 us -> 9.55 us
    unnamed x39 -> x8, local copies, waits for them, and re-layouts: 78 us -> 1.76 us
    reduce_sum x4 -> x0, other arithmetic: 40.8 us -> none  [the longest x2 40.7 us: relax(): level = jnp.sum(energy, axis=2)]
    slice x10 -> x0, local copies, waits for them, and re-layouts: 38.6 us -> none  [the longest x2 13.7 us: per_device(): inflow_low = jnp.concatenate([padded[..., :1], plus_x[..., :-1]], 3)]
    psum x2 -> x0, blocking collectives: 31.4 us -> none  [relax(): zeroth, first_moment = lax.psum((zeroth, first_moment), 'band')]
    all_to_all x1, blocking collectives: 38.7 us -> 11.7 us  [per_device(): windows = lax.all_to_all(windows, 'pts', 0, 0, tiled=True)]
    pallas_call x0 -> x6, Pallas kernels: none -> 26.1 us  [the longest x1 7.05 us: last_step(): pl.pallas_call(last_kernel, grid=(NFB // fb,), in_specs=[SM, pl.BlockSpec...]
    all_to_all x1 -> x0, waiting for transfers between devices: 21.6 us -> none  [per_device(): lax.all_to_all(spectra, 'pts', split_axis=3, concat_axis=3, tiled=True)]
    mul x7 -> x0, other arithmetic: 20.5 us -> none  [the longest x2 20.4 us: flux_parts(): jnp.minimum(velocity, 0.0) * energy]
  transfers between devices with their start and end apart: 5 -> 11, of which waited for: 1 -> 6; matrix products, arithmetic and copies ran while one was open for 11% -> 0% of each run, Pallas kernels for 0% -> 6%
where the time goes in v1:
time: 68.2 us; the launch traced here: 67.9 us
  Pallas kernels  26.1 us (38%)
  starting transfers between devices  18.7 us (27%)
  blocking collectives  11.7 us (17%)
  waiting for transfers between devices  9.55 us (14%)
  local copies, waits for them, and re-layouts  1.76 us (3%)
    ppermute x9, starting transfers between devices, band_parts(): lax.ppermute(x, 'band', [(i, i ^ k) for i in range(BANDS)])  12.5 us
    all_to_all x1, blocking collectives, per_device(): windows = lax.all_to_all(windows, 'pts', 0, 0, tiled=True)  11.7 us
    ppermute x9, waiting for transfers between devices, band_parts(): lax.ppermute(x, 'band', [(i, i ^ k) for i in range(BANDS)])  9.55 us
    pallas_call x1, Pallas kernels, last_step(): pl.pallas_call(last_kernel, grid=(NFB // fb,), in_specs=[SM, pl.BlockSpec...  7.05 us
    ppermute x1, starting transfers between devices, per_device(): rh = lax.ppermute(ml, 'pts', LEFT)  6.08 us
    pallas_call x1, Pallas kernels, first_step(): pl.pallas_call(first_kernel, in_specs=[SM] + [VM] * 9, out_specs=[VM] * 2...  5.85 us
    pallas_call x1, Pallas kernels, pack(): pl.pallas_call(pack_kernel, grid=(NFB // fb,), in_specs=[pl.BlockSpec((fb...  5.56 us
    pallas_call x1, Pallas kernels, second_step(): pl.pallas_call(second_kernel, in_specs=[SM] + [VM] * 10, out_specs=[VM] *...  3.45 us
  transfers between devices with their start and end apart: 11, of which 6 were waited for; matrix products, arithmetic and copies ran while one was open for 0% of the time, Pallas kernels for 6%

profile of v1, /device:TPU:0, one launch (start us, length us, event | category | flops | bytes accessed | tf_op | source)
XLA Modules:
  0.0 67.9 jit_solution(5665889840873120218)
XLA Ops:
  0.0 0.0 copy-start
  0.0 1.7 %copy-done = f32[16,9,36,128]{3,0,2,1:T(8,128)S(1)} copy-done((f32[16,9,36,128]{3,0,2,1:T(8,128)S(1)}, f32[16,9,36,128]{3,0,2,1:T(8,128)}, u32[]{:S(2)}) %copy-start) | copy-done | bytes 2654232
  1.8 0.0 copy-start.3
  1.8 0.0 copy-start.1
  1.8 0.0 copy-start.2
  1.8 5.6 %pack.1 = (f32[2,9,9,16,128]{4,3,2,1,0:T(8,128)S(1)}, f32[2,9,9,16,128]{4,3,2,1,0:T(8,128)S(1)}) custom-call(f32[9,36,16,128]{3,2,1,0:T(8,128)S(1)} %bitcast.8), custom_call_target="tpu_custom_call" | custom-call | tf_op jit(solution)/shard_map/pack/pallas_call | solution.py:110
  7.3 0.1 collective-permute-start
  7.4 6.1 %collective-permute-start.1 = (f32[2,9,9,16,128]{4,3,2,1,0:T(8,128)S(1)}, f32[2,9,9,16,128]{4,3,2,1,0:T(8,128)}, u32[]{:S(2)}, u32[]{:S(2)}) collective-permute-start(f32[2,9,9,16,128]{4,3,2,1,0:T(8,128)S(1)} %get-tuple-element.17.ml), channel_id=1, source_target_pairs={{1,0},{2,1},{3,2},{4,3},{5,4},{6,5},{7,6},{8,7},{9,8},{10,9},{11,1... | collective-permute-start | bytes 3981320 | tf_op jit(solution)/shard_map/ppermute | solution.py:445
  13.5 0.0 copy-done.3
  13.5 0.0 copy-done.1
  13.5 0.0 copy-done.2
  13.5 2.8 %collective-permute-start.4 = (f32[8,4,128]{2,1,0:T(4,128)S(1)}, f32[8,4,128]{2,1,0:T(4,128)S(1)}, u32[]{:S(2)}, u32[]{:S(2)}) collective-permute-start(f32[8,4,128]{2,1,0:T(4,128)S(1)} %pad_maximum_fusion.f0), channel_id=1, source_target_pairs={{0,96},{32,64},{64,32},{96,0},{1,97},{33,65},{65,33},{97,1},{2,98}... | collective-permute-start | bytes 49160 | tf_op jit(solution)/shard_map/ppermute | solution.py:429
  16.4 0.8 %collective-permute-start.3 = (f32[8,4,128]{2,1,0:T(4,128)S(1)}, f32[8,4,128]{2,1,0:T(4,128)S(1)}, u32[]{:S(2)}, u32[]{:S(2)}) collective-permute-start(f32[8,4,128]{2,1,0:T(4,128)S(1)} %pad_maximum_fusion.f0), channel_id=1, source_target_pairs={{0,64},{32,96},{64,0},{96,32},{1,65},{33,97},{65,1},{97,33},{2,66}... | collective-permute-start | bytes 49160 | tf_op jit(solution)/shard_map/ppermute | solution.py:429
  17.2 0.5 collective-permute-start.2
  17.7 0.1 pad_add_fusion.at
  17.8 0.8 %collective-permute-done.4.f3 = f32[8,4,128]{2,1,0:T(4,128)S(1)} collective-permute-done((f32[8,4,128]{2,1,0:T(4,128)S(1)}, f32[8,4,128]{2,1,0:T(4,128)S(1)}, u32[]{:S(2)}, u32[]{:S(2)}) %collective-permute-start.4) | collective-permute-done | bytes 16416 | tf_op jit(solution)/shard_map/ppermute | solution.py:429
  18.5 3.1 %collective-permute-done.3.f2 = f32[8,4,128]{2,1,0:T(4,128)S(1)} collective-permute-done((f32[8,4,128]{2,1,0:T(4,128)S(1)}, f32[8,4,128]{2,1,0:T(4,128)S(1)}, u32[]{:S(2)}, u32[]{:S(2)}) %collective-permute-start.3) | collective-permute-done | bytes 16416 | tf_op jit(solution)/shard_map/ppermute | solution.py:429
  21.6 0.0 collective-permute-done.2.f1
  21.6 0.8 %forcing.1 = f32[32,8,128]{2,1,0:T(8,128)S(1)} custom-call(s32[2]{0:T(128)S(1)} %pad_add_fusion.at, f32[8,4,128]{2,1,0:T(4,128)S(1)} %pad_maximum_fusion.f0, f32[8,4,128]{2,1,0:T(4,128)S(1)} %collective-permute-done.2.f1, f32[8,4,128]{2,1,0:T(4,128)S(1)} %collective-permute-done.3.f2, f32[8,4,128]{2,1,0:T(4,128)S(1)} %collective-permute-done.4.f3), custom_call_target="tpu_custom_call" | custom-call | tf_op jit(solution)/shard_map/forcing/pallas_call | solution.py:142
  22.4 11.7 %all_to_all.5.win = f32[32,8,128]{2,1,0:T(8,128)S(1)} all-to-all(f32[32,8,128]{2,1,0:T(8,128)S(1)} %forcing.1), channel_id=1, replica_groups=mesh['band'=4,'pts'=32] {'pts'}, dimensions={0} | all-to-all | bytes 262144 | tf_op jit(solution)/shard_map/all_to_all | solution.py:447
  34.1 3.4 %speeds.1 = (f32[2,9,8,16,128]{4,3,2,1,0:T(8,128)S(1)}, f32[2,8,16,128]{3,2,1,0:T(8,128)S(1)}, f32[2,8,16,128]{3,2,1,0:T(8,128)S(1)}, f32[8,16,128]{2,1,0:T(8,128)S(1)}, f32[2,9,8,128]{3,2,1,0:T(8,128)S(1)}) custom-call(s32[2]{0:T(128)S(1)} %pad_add_fusion.at, f32[32,8,128]{2,1,0:T(8,128)S(1)} %all_to_all.5.win), custom_call_target="tpu_custom_call" | custom-call | tf_op jit(solution)/shard_map/speeds/pallas_call | solution.py:207
  37.5 0.0 collective-permute-done.lh
  37.5 0.0 collective-permute-done.1.rh
  37.5 5.8 %first_step.1 = (f32[6,9,9,16,128]{4,3,2,1,0:T(8,128)S(1)}, f32[2,2,16,128]{3,2,1,0:T(8,128)S(1)}) custom-call(s32[2]{0:T(128)S(1)} %pad_add_fusion.at, f32[2,9,9,16,128]{4,3,2,1,0:T(8,128)} %collective-permute-done.lh, f32[2,9,9,16,128]{4,3,2,1,0:T(8,128)S(1)} %get-tuple-element.17.ml, f32[2,9,9,16,128]{4,3,2,1,0:T(8,128)S(1)} %get-tuple-element.16.mr, ...), custom_call_target="tpu_custom_call" | custom-call | tf_op jit(solution)/shard_map/first_step/pallas_call | solution.py:311
  43.4 1.5 %collective-permute-start.7 = (f32[2,2,16,128]{3,2,1,0:T(8,128)S(1)}, f32[2,2,16,128]{3,2,1,0:T(8,128)S(1)}, u32[]{:S(2)}, u32[]{:S(2)}) collective-permute-start(f32[2,2,16,128]{3,2,1,0:T(8,128)S(1)} %get-tuple-element.24.m0), channel_id=1, source_target_pairs={{0,96},{32,64},{64,32},{96,0},{1,97},{33,65},{65,33},{97,1},{2,98}... | collective-permute-start | bytes 98312 | tf_op jit(solution)/shard_map/ppermute | solution.py:429
  44.8 0.9 %collective-permute-start.6 = (f32[2,2,16,128]{3,2,1,0:T(8,128)S(1)}, f32[2,2,16,128]{3,2,1,0:T(8,128)S(1)}, u32[]{:S(2)}, u32[]{:S(2)}) collective-permute-start(f32[2,2,16,128]{3,2,1,0:T(8,128)S(1)} %get-tuple-element.24.m0), channel_id=1, source_target_pairs={{0,64},{32,96},{64,0},{96,32},{1,65},{33,97},{65,1},{97,33},{2,66}... | collective-permute-start | bytes 98312 | tf_op jit(solution)/shard_map/ppermute | solution.py:429
  45.7 1.8 %collective-permute-start.5 = (f32[2,2,16,128]{3,2,1,0:T(8,128)S(1)}, f32[2,2,16,128]{3,2,1,0:T(8,128)S(1)}, u32[]{:S(2)}, u32[]{:S(2)}) collective-permute-start(f32[2,2,16,128]{3,2,1,0:T(8,128)S(1)} %get-tuple-element.24.m0), channel_id=1, source_target_pairs={{0,32},{32,0},{64,96},{96,64},{1,33},{33,1},{65,97},{97,65},{2,34}... | collective-permute-start | bytes 98312 | tf_op jit(solution)/shard_map/ppermute | solution.py:429
  47.5 1.0 %collective-permute-done.7.m3 = f32[2,2,16,128]{3,2,1,0:T(8,128)S(1)} collective-permute-done((f32[2,2,16,128]{3,2,1,0:T(8,128)S(1)}, f32[2,2,16,128]{3,2,1,0:T(8,128)S(1)}, u32[]{:S(2)}, u32[]{:S(2)}) %collective-permute-start.7) | collective-permute-done | bytes 32800 | tf_op jit(solution)/shard_map/ppermute | solution.py:429
  48.6 1.8 %collective-permute-done.6.m2 = f32[2,2,16,128]{3,2,1,0:T(8,128)S(1)} collective-permute-done((f32[2,2,16,128]{3,2,1,0:T(8,128)S(1)}, f32[2,2,16,128]{3,2,1,0:T(8,128)S(1)}, u32[]{:S(2)}, u32[]{:S(2)}) %collective-permute-start.6) | collective-permute-done | bytes 32800 | tf_op jit(solution)/shard_map/ppermute | solution.py:429
  50.4 0.0 collective-permute-done.5.m1
  50.4 3.5 %second_step.1 = (f32[4,9,9,16,128]{4,3,2,1,0:T(8,128)S(1)}, f32[2,16,128]{2,1,0:T(8,128)S(1)}) custom-call(s32[2]{0:T(128)S(1)} %pad_add_fusion.at, f32[6,9,9,16,128]{4,3,2,1,0:T(8,128)S(1)} %get-tuple-element.23.e_ref, f32[2,2,16,128]{3,2,1,0:T(8,128)S(1)} %get-tuple-element.24.m0, f32[2,2,16,128]{3,2,1,0:T(8,128)S(1)} %collective-permute-done.5.m1, ...), custom_call_target="tpu_custom_call" | custom-call | tf_op jit(solution)/shard_map/second_step/pallas_call | solution.py:377
  53.8 1.8 %collective-permute-start.10 = (f32[2,16,128]{2,1,0:T(8,128)S(1)}, f32[2,16,128]{2,1,0:T(8,128)S(1)}, u32[]{:S(2)}, u32[]{:S(2)}) collective-permute-start(f32[2,16,128]{2,1,0:T(8,128)S(1)} %get-tuple-element.26.m0), channel_id=1, source_target_pairs={{0,96},{32,64},{64,32},{96,0},{1,97},{33,65},{65,33},{97,1},{2,98}... | collective-permute-start | bytes 49160 | tf_op jit(solution)/shard_map/ppermute | solution.py:429
  55.7 1.4 %collective-permute-start.9 = (f32[2,16,128]{2,1,0:T(8,128)S(1)}, f32[2,16,128]{2,1,0:T(8,128)S(1)}, u32[]{:S(2)}, u32[]{:S(2)}) collective-permute-start(f32[2,16,128]{2,1,0:T(8,128)S(1)} %get-tuple-element.26.m0), channel_id=1, source_target_pairs={{0,64},{32,96},{64,0},{96,32},{1,65},{33,97},{65,1},{97,33},{2,66}... | collective-permute-start | bytes 49160 | tf_op jit(solution)/shard_map/ppermute | solution.py:429
  57.1 0.9 %collective-permute-start.8 = (f32[2,16,128]{2,1,0:T(8,128)S(1)}, f32[2,16,128]{2,1,0:T(8,128)S(1)}, u32[]{:S(2)}, u32[]{:S(2)}) collective-permute-start(f32[2,16,128]{2,1,0:T(8,128)S(1)} %get-tuple-element.26.m0), channel_id=1, source_target_pairs={{0,32},{32,0},{64,96},{96,64},{1,33},{33,1},{65,97},{97,65},{2,34}... | collective-permute-start | bytes 49160 | tf_op jit(solution)/shard_map/ppermute | solution.py:429
  58.0 0.9 %collective-permute-done.10.m3 = f32[2,16,128]{2,1,0:T(8,128)S(1)} collective-permute-done((f32[2,16,128]{2,1,0:T(8,128)S(1)}, f32[2,16,128]{2,1,0:T(8,128)S(1)}, u32[]{:S(2)}, u32[]{:S(2)}) %collective-permute-start.10) | collective-permute-done | bytes 16416 | tf_op jit(solution)/shard_map/ppermute | solution.py:429
  58.9 2.0 %collective-permute-done.9.m2 = f32[2,16,128]{2,1,0:T(8,128)S(1)} collective-permute-done((f32[2,16,128]{2,1,0:T(8,128)S(1)}, f32[2,16,128]{2,1,0:T(8,128)S(1)}, u32[]{:S(2)}, u32[]{:S(2)}) %collective-permute-start.9) | collective-permute-done | bytes 16416 | tf_op jit(solution)/shard_map/ppermute | solution.py:429
  60.9 0.0 collective-permute-done.8.m1
  60.9 7.0 %last_step.1 = f32[9,36,16,128]{3,2,1,0:T(8,128)} custom-call(s32[2]{0:T(128)S(1)} %pad_add_fusion.at, f32[4,9,9,16,128]{4,3,2,1,0:T(8,128)S(1)} %get-tuple-element.25.e_ref, f32[2,16,128]{2,1,0:T(8,128)S(1)} %get-tuple-element.26.m0, f32[2,16,128]{2,1,0:T(8,128)S(1)} %collective-permute-done.8.m1, f32[2,16,128]{2,1,0:T(8,128)S(1)} %collective-permute-done.9.m2, ...), custom_call_target="tpu_custom_call" | custom-call | tf_op jit(solution)/shard_map/last_step/pallas_call | solution.py:411
  (2 shorter events, 0.0 us)
Async XLA Ops:
  0.0 1.7 %copy-start = (f32[16,9,36,128]{3,0,2,1:T(8,128)S(1)}, f32[16,9,36,128]{3,0,2,1:T(8,128)}, u32[]{:S(2)}) copy-start(f32[16,9,36,128]{3,0,2,1:T(8,128)} %param.4) | copy-start | bytes 7962628
  1.8 11.7 %copy-start.3 = (s32[4,128]{1,0:T(4,128)S(1)}, s32[4,128]{1,0:T(4,128)}, u32[]{:S(2)}) copy-start(s32[4,128]{1,0:T(4,128)} %param.7) | copy-start | bytes 6148
  1.8 11.7 %copy-start.1 = (f32[2,3,4,128]{3,2,1,0:T(4,128)S(1)}, f32[2,3,4,128]{3,2,1,0:T(4,128)}, u32[]{:S(2)}) copy-start(f32[2,3,4,128]{3,2,1,0:T(4,128)} %param.5) | copy-start | bytes 36868
  1.8 11.7 %copy-start.2 = (f32[4,128]{1,0:T(4,128)S(1)}, f32[4,128]{1,0:T(4,128)}, u32[]{:S(2)}) copy-start(f32[4,128]{1,0:T(4,128)} %param.6) | copy-start | bytes 6148
  7.3 30.2 %collective-permute-start = (f32[2,9,9,16,128]{4,3,2,1,0:T(8,128)S(1)}, f32[2,9,9,16,128]{4,3,2,1,0:T(8,128)}, u32[]{:S(2)}, u32[]{:S(2)}) collective-permute-start(f32[2,9,9,16,128]{4,3,2,1,0:T(8,128)S(1)} %get-tuple-element.16.mr), channel_id=1, source_target_pairs={{0,1},{1,2},{2,3},{3,4},{4,5},{5,6},{6,7},{7,8},{8,9},{9,10},{10,1... | collective-permute-start | bytes 3981320 | tf_op jit(solution)/shard_map/ppermute | solution.py:444
  7.4 30.1 %collective-permute-start.1 = (f32[2,9,9,16,128]{4,3,2,1,0:T(8,128)S(1)}, f32[2,9,9,16,128]{4,3,2,1,0:T(8,128)}, u32[]{:S(2)}, u32[]{:S(2)}) collective-permute-start(f32[2,9,9,16,128]{4,3,2,1,0:T(8,128)S(1)} %get-tuple-element.17.ml), channel_id=1, source_target_pairs={{1,0},{2,1},{3,2},{4,3},{5,4},{6,5},{7,6},{8,7},{9,8},{10,9},{11,1... | collective-permute-start | bytes 3981320 | tf_op jit(solution)/shard_map/ppermute | solution.py:445
  13.5 5.0 %collective-permute-start.4 = (f32[8,4,128]{2,1,0:T(4,128)S(1)}, f32[8,4,128]{2,1,0:T(4,128)S(1)}, u32[]{:S(2)}, u32[]{:S(2)}) collective-permute-start(f32[8,4,128]{2,1,0:T(4,128)S(1)} %pad_maximum_fusion.f0), channel_id=1, source_target_pairs={{0,96},{32,64},{64,32},{96,0},{1,97},{33,65},{65,33},{97,1},{2,98}... | collective-permute-start | bytes 49160 | tf_op jit(solution)/shard_map/ppermute | solution.py:429
  16.4 5.2 %collective-permute-start.3 = (f32[8,4,128]{2,1,0:T(4,128)S(1)}, f32[8,4,128]{2,1,0:T(4,128)S(1)}, u32[]{:S(2)}, u32[]{:S(2)}) collective-permute-start(f32[8,4,128]{2,1,0:T(4,128)S(1)} %pad_maximum_fusion.f0), channel_id=1, source_target_pairs={{0,64},{32,96},{64,0},{96,32},{1,65},{33,97},{65,1},{97,33},{2,66}... | collective-permute-start | bytes 49160 | tf_op jit(solution)/shard_map/ppermute | solution.py:429
  17.2 4.4 %collective-permute-start.2 = (f32[8,4,128]{2,1,0:T(4,128)S(1)}, f32[8,4,128]{2,1,0:T(4,128)S(1)}, u32[]{:S(2)}, u32[]{:S(2)}) collective-permute-start(f32[8,4,128]{2,1,0:T(4,128)S(1)} %pad_maximum_fusion.f0), channel_id=1, source_target_pairs={{0,32},{32,0},{64,96},{96,64},{1,33},{33,1},{65,97},{97,65},{2,34}... | collective-permute-start | bytes 49160 | tf_op jit(solution)/shard_map/ppermute | solution.py:429
  43.4 5.2 %collective-permute-start.7 = (f32[2,2,16,128]{3,2,1,0:T(8,128)S(1)}, f32[2,2,16,128]{3,2,1,0:T(8,128)S(1)}, u32[]{:S(2)}, u32[]{:S(2)}) collective-permute-start(f32[2,2,16,128]{3,2,1,0:T(8,128)S(1)} %get-tuple-element.24.m0), channel_id=1, source_target_pairs={{0,96},{32,64},{64,32},{96,0},{1,97},{33,65},{65,33},{97,1},{2,98}... | collective-permute-start | bytes 98312 | tf_op jit(solution)/shard_map/ppermute | solution.py:429
  44.8 5.5 %collective-permute-start.6 = (f32[2,2,16,128]{3,2,1,0:T(8,128)S(1)}, f32[2,2,16,128]{3,2,1,0:T(8,128)S(1)}, u32[]{:S(2)}, u32[]{:S(2)}) collective-permute-start(f32[2,2,16,128]{3,2,1,0:T(8,128)S(1)} %get-tuple-element.24.m0), channel_id=1, source_target_pairs={{0,64},{32,96},{64,0},{96,32},{1,65},{33,97},{65,1},{97,33},{2,66}... | collective-permute-start | bytes 98312 | tf_op jit(solution)/shard_map/ppermute | solution.py:429
  45.7 4.6 %collective-permute-start.5 = (f32[2,2,16,128]{3,2,1,0:T(8,128)S(1)}, f32[2,2,16,128]{3,2,1,0:T(8,128)S(1)}, u32[]{:S(2)}, u32[]{:S(2)}) collective-permute-start(f32[2,2,16,128]{3,2,1,0:T(8,128)S(1)} %get-tuple-element.24.m0), channel_id=1, source_target_pairs={{0,32},{32,0},{64,96},{96,64},{1,33},{33,1},{65,97},{97,65},{2,34}... | collective-permute-start | bytes 98312 | tf_op jit(solution)/shard_map/ppermute | solution.py:429
  53.8 5.0 %collective-permute-start.10 = (f32[2,16,128]{2,1,0:T(8,128)S(1)}, f32[2,16,128]{2,1,0:T(8,128)S(1)}, u32[]{:S(2)}, u32[]{:S(2)}) collective-permute-start(f32[2,16,128]{2,1,0:T(8,128)S(1)} %get-tuple-element.26.m0), channel_id=1, source_target_pairs={{0,96},{32,64},{64,32},{96,0},{1,97},{33,65},{65,33},{97,1},{2,98}... | collective-permute-start | bytes 49160 | tf_op jit(solution)/shard_map/ppermute | solution.py:429
  55.7 5.2 %collective-permute-start.9 = (f32[2,16,128]{2,1,0:T(8,128)S(1)}, f32[2,16,128]{2,1,0:T(8,128)S(1)}, u32[]{:S(2)}, u32[]{:S(2)}) collective-permute-start(f32[2,16,128]{2,1,0:T(8,128)S(1)} %get-tuple-element.26.m0), channel_id=1, source_target_pairs={{0,64},{32,96},{64,0},{96,32},{1,65},{33,97},{65,1},{97,33},{2,66}... | collective-permute-start | bytes 49160 | tf_op jit(solution)/shard_map/ppermute | solution.py:429
  57.1 3.8 %collective-permute-start.8 = (f32[2,16,128]{2,1,0:T(8,128)S(1)}, f32[2,16,128]{2,1,0:T(8,128)S(1)}, u32[]{:S(2)}, u32[]{:S(2)}) collective-permute-start(f32[2,16,128]{2,1,0:T(8,128)S(1)} %get-tuple-element.26.m0), channel_id=1, source_target_pairs={{0,32},{32,0},{64,96},{96,64},{1,33},{33,1},{65,97},{97,65},{2,34}... | collective-permute-start | bytes 49160 | tf_op jit(solution)/shard_map/ppermute | solution.py:429

commit v2 on v1

v2 whole, which is shorter than its diff:
```python
import math

import jax
import jax.numpy as jnp
from jax import lax
from jax.experimental import pallas as pl
from jax.experimental.pallas import tpu as pltpu
from jax.sharding import PartitionSpec as P

GRAVITY = 9.81
COURANT = 0.02
DISSIPATION = 1.0
MOMENT_FLOOR = 0.01
FREQ_FIRST = 0.035
FREQ_STEP = 1.1
BAND_WIDTH = 0.0955
ND = 36
NQ = 9
NFB = 9
ROWS = 16
BANDS = 4
PTS = 32
SUBSTEPS = 2
FIELDS = 8
LANES = 128
F32 = jnp.float32
VMEM_LIMIT = 40 * 1024 * 1024
VM = pl.BlockSpec(memory_space=pltpu.VMEM)
SM = pl.BlockSpec(memory_space=pltpu.SMEM)
HB = pl.BlockSpec(memory_space=pltpu.HBM)
PARAMS = pltpu.CompilerParams(vmem_limit_bytes=VMEM_LIMIT)


def lane_group():
    return lax.broadcasted_iota(jnp.int32, (ROWS, LANES), 1) & 3


def lroll(x, shift):
    return pltpu.roll(x, shift % LANES, 1)


def lane_swap(x, distance):
    index = lax.broadcasted_iota(jnp.int32, x.shape, 1) ^ distance
    return jnp.take_along_axis(x, index, axis=1)


def quad_transpose(a):
    lane = lane_group()

    def exchange(x, y, distance):
        low = (lane & distance) == 0
        t = lane_swap(jnp.where(low, y, x), distance)
        return jnp.where(low, x, t), jnp.where(low, t, y)

    b0, b2 = exchange(a[0], a[2], 2)
    b1, b3 = exchange(a[1], a[3], 2)
    o0, o1 = exchange(b0, b1, 1)
    o2, o3 = exchange(b2, b3, 1)
    return o0, o1, o2, o3


def quad_spread(x):
    lane = lax.broadcasted_iota(jnp.int32, x.shape, 1)
    return tuple(jnp.take_along_axis(x, (lane & ~3) + k, axis=1) for k in range(4))


def quad_sum(x):
    x = x + lane_swap(x, 1)
    return x + lane_swap(x, 2)


def select4(x):
    lane = lane_group()
    return jnp.where(
        lane < 2, jnp.where(lane == 0, x[0], x[1]), jnp.where(lane == 2, x[2], x[3])
    )


def frequency_of(index):
    return FREQ_FIRST * jnp.exp(
        jnp.full((ROWS, LANES), index, jnp.int32).astype(F32) * math.log(FREQ_STEP)
    )


def edge_shifts(pts):
    left = jnp.where(pts == 0, 4, 0)
    right = jnp.where(pts == PTS - 1, LANES - 4, 0)
    return left, right


def cost(microseconds):
    return pl.CostEstimate(
        flops=0, transcendentals=0, bytes_accessed=int(microseconds * 3.0e6)
    )


def loop(count, body):
    lax.fori_loop(0, count, lambda i, carry: (body(i), carry)[1], 0)


def pack_kernel(e_ref, ml_ref, mr_ref):
    def body(f):
        def over(d, carry):
            out = quad_transpose([e_ref[f, d + NQ * q] for q in range(4)])
            ml_ref[0, f, d] = out[0]
            ml_ref[1, f, d] = out[1]
            mr_ref[0, f, d] = out[2]
            mr_ref[1, f, d] = out[3]
            return carry

        lax.fori_loop(0, NQ, over, 0, unroll=3)

    loop(NFB, body)


def pack(spectra):
    shape = jax.ShapeDtypeStruct((2, NFB, NQ, ROWS, LANES), F32)
    return pl.pallas_call(
        pack_kernel,
        in_specs=[VM],
        out_specs=[VM, VM],
        out_shape=[shape, shape],
        compiler_params=PARAMS,
        cost_estimate=cost(2.0),
        name="pack",
    )(spectra)


def exact_dot(a, b, dims):
    return lax.dot_general(
        a, b, (dims, ((), ())), precision=lax.Precision.HIGHEST, preferred_element_type=F32
    )


def forcing_kernel(own, out_ref):
    shape = (8 * PTS, LANES)
    place = lax.broadcasted_iota(jnp.int32, shape, 0)
    wanted = (4 * (place & (PTS - 1)) + (place >> 5) + (LANES - 2)) & (LANES - 1)
    pick = (lax.broadcasted_iota(jnp.int32, shape, 1) == wanted).astype(F32)
    x = exact_dot(pick, own[...], ((1,), (1,)))
    for h in range(2):
        row = jnp.concatenate(
            [x[PTS * (4 * h + k) : PTS * (4 * h + k) + PTS] for k in range(4)], axis=1
        )
        for band in range(BANDS):
            out_ref[PTS * band : PTS * band + PTS, h, :] = row


def forcing_windows(forcing):
    return pl.pallas_call(
        forcing_kernel,
        in_specs=[VM],
        out_specs=VM,
        out_shape=jax.ShapeDtypeStruct((BANDS * PTS, 2, LANES), F32),
        compiler_params=PARAMS,
        cost_estimate=cost(0.8),
        name="forcing",
    )(forcing)


def spread_columns(x, y):
    a, b = quad_spread(x), quad_spread(y)
    return (b[2], b[3]) + a + (b[0], b[1])


def celerities(first, h_ref, c_ref):
    def body(f):
        angular = (2.0 * math.pi) * frequency_of(first + f)
        deep = angular * angular / GRAVITY
        speed = []
        for part in range(2):
            height = h_ref[part]
            wavenumber = deep / jnp.sqrt(jnp.tanh(deep * height))
            q = 2.0 * wavenumber * height
            ratio = 2.0 * q * jnp.exp(-q) / (1.0 - jnp.exp(-2.0 * q))
            speed.append((0.5 * COURANT) * (1.0 + ratio) * angular / wavenumber)
        for i, x in enumerate(spread_columns(*speed)):
            c_ref[f, i] = x

    loop(NFB, body)


def speed_kernel(at, win, c_ref, u_ref, v_ref, w_ref, t_ref, h_ref, f_scr, h_scr):
    left, right = edge_shifts(at[1])
    shape = (PTS, LANES)
    place = lax.broadcasted_iota(jnp.int32, shape, 0)
    spread = ((lax.broadcasted_iota(jnp.int32, shape, 1) >> 2) == place).astype(F32)
    for band in range(BANDS):
        for h in range(2):
            block = win[PTS * band : PTS * band + PTS, h, :]
            fields = exact_dot(block, spread, ((0,), (0,)))
            for k in range(4):
                i = 4 * h + k
                part = fields[32 * k : 32 * k + 32]
                if i < 2:
                    part = pltpu.roll(part, left, 1)
                if i >= 6:
                    part = pltpu.roll(part, right, 1)
                for n in range(FIELDS):
                    f_scr[i, n, 4 * band : 4 * band + 4, :] = part[4 * n : 4 * n + 4]
    for i in range(8):
        w_ref[i] = f_scr[i, 7]
        for s in range(SUBSTEPS):
            u_ref[s, i] = COURANT * f_scr[i, 3 * s]
            v_ref[s, i] = COURANT * f_scr[i, 3 * s + 1]
    for s, ref in ((0, h_scr), (1, h_ref)):
        depth = [f_scr[i, 6] + f_scr[i, 3 * s + 2] for i in range(8)]
        ref[0] = select4(depth[2:6])
        ref[1] = select4([depth[6], depth[7], depth[0], depth[1]])
    for d in range(NQ):
        angle = (d + NQ * lane_group()[0:8]).astype(F32) * (2.0 * math.pi / ND)
        t_ref[0, d] = jnp.cos(angle)
        t_ref[1, d] = jnp.sin(angle)
    celerities(at[0] * NFB, h_scr, c_ref)


def speeds(at, windows):
    return pl.pallas_call(
        speed_kernel,
        in_specs=[SM, VM],
        out_specs=[VM] * 6,
        out_shape=[
            jax.ShapeDtypeStruct((NFB, 8, ROWS, LANES), F32),
            jax.ShapeDtypeStruct((SUBSTEPS, 8, ROWS, LANES), F32),
            jax.ShapeDtypeStruct((SUBSTEPS, 8, ROWS, LANES), F32),
            jax.ShapeDtypeStruct((8, ROWS, LANES), F32),
            jax.ShapeDtypeStruct((2, NQ, 8, LANES), F32),
            jax.ShapeDtypeStruct((2, ROWS, LANES), F32),
        ],
        scratch_shapes=[
            pltpu.VMEM((8, FIELDS, ROWS, LANES), F32),
            pltpu.VMEM((2, ROWS, LANES), F32),
        ],
        compiler_params=PARAMS,
        cost_estimate=cost(2.0),
        name="speeds",
    )(at, windows)


def second_speed_kernel(at, h_ref, c_ref):
    celerities(at[0] * NFB, h_ref, c_ref)


def second_speeds(at, h):
    return pl.pallas_call(
        second_speed_kernel,
        in_specs=[SM, VM],
        out_specs=VM,
        out_shape=jax.ShapeDtypeStruct((NFB, 8, ROWS, LANES), F32),
        compiler_params=PARAMS,
        cost_estimate=cost(1.5),
        name="second_speeds",
    )(at, h)


def row_below(x):
    first = lax.broadcasted_iota(jnp.int32, (8, LANES), 0) == 0
    t0, t1 = pltpu.roll(x[0:8], 1, 0), pltpu.roll(x[8:16], 1, 0)
    return jnp.concatenate([jnp.where(first, 0.0, t0), jnp.where(first, t0, t1)], axis=0)


def row_above(x):
    last = lax.broadcasted_iota(jnp.int32, (8, LANES), 0) == 7
    t0, t1 = pltpu.roll(x[0:8], 7, 0), pltpu.roll(x[8:16], 7, 0)
    return jnp.concatenate([jnp.where(last, t1, t0), jnp.where(last, 0.0, t1)], axis=0)


def advance(count, energy, speed, current_x, current_y, wet, cos, sin, store):
    inflow = None
    part = None
    for i in range(count):
        e = energy(i)
        c = speed(i)
        a = (c * cos + current_x(i)) * e
        if part is not None:
            store(i - 1, (part - jnp.minimum(a, 0.0)) * wet(i - 1))
        if 0 < i < count - 1:
            b = (c * sin + current_y(i)) * e
            turn = row_below(jnp.maximum(b, 0.0)) - row_above(jnp.minimum(b, 0.0))
            part = e - (jnp.abs(a) + jnp.abs(b)) + (inflow + turn)
        inflow = jnp.maximum(a, 0.0)


UNROLL = 9


def zeros(count):
    return tuple(jnp.zeros((ROWS, LANES), F32) for _ in range(count))


def twice(x):
    return jnp.concatenate([x, x], axis=0)


def add_moments(acc, levels, freq):
    weight = (BAND_WIDTH * (2.0 * math.pi / ND)) * freq
    for i, level in enumerate(levels):
        t = level * weight
        acc[0, i] = acc[0, i] + t
        acc[1, i] = acc[1, i] + t * freq


def inner_kernel(
    at, ml, mr, c_ref, u_ref, v_ref, w_ref, t_ref, out_ref, left_ref, right_ref, acc_ref
):
    first = at[0] * NFB
    acc_ref[...] = jnp.zeros_like(acc_ref)

    def body(f, carry):
        def over(d, levels):
            levels = list(levels)
            cos, sin = twice(t_ref[0, d]), twice(t_ref[1, d])
            inflow = None
            part = None
            for i in range(4):
                e = (ml, mr)[i // 2][i % 2, f, d] * w_ref[i + 2]
                c = c_ref[f, i + 2]
                a = (c * cos + u_ref[0, i + 2]) * e
                minus = jnp.minimum(a, 0.0)
                if i == 0:
                    left_ref[f, d] = minus
                if i == 1:
                    out_ref[0, f, d] = part - minus
                if i > 1:
                    value = (part - minus) * w_ref[i + 1]
                    out_ref[i - 1, f, d] = value
                    levels[i - 2] = levels[i - 2] + value
                b = (c * sin + v_ref[0, i + 2]) * e
                turn = row_below(jnp.maximum(b, 0.0)) - row_above(jnp.minimum(b, 0.0))
                part = e - (jnp.abs(a) + jnp.abs(b))
                part = part + (turn if inflow is None else inflow + turn)
                inflow = jnp.maximum(a, 0.0)
            out_ref[3, f, d] = part
            right_ref[f, d] = inflow
            return tuple(levels)

        levels = lax.fori_loop(0, NQ, over, zeros(2), unroll=UNROLL)
        add_moments(acc_ref, levels, frequency_of(first + f))
        return carry

    lax.fori_loop(0, NFB, body, 0)


def inner_step(at, ml, mr, c, u, v, w, t):
    edge = jax.ShapeDtypeStruct((NFB, NQ, ROWS, LANES), F32)
    return pl.pallas_call(
        inner_kernel,
        in_specs=[SM] + [VM] * 7,
        out_specs=[VM] * 4,
        out_shape=[
            jax.ShapeDtypeStruct((4, NFB, NQ, ROWS, LANES), F32),
            edge,
            edge,
            jax.ShapeDtypeStruct((2, 2, ROWS, LANES), F32),
        ],
        compiler_params=PARAMS,
        cost_estimate=cost(4.0),
        name="inner_step",
    )(at, ml, mr, c, u, v, w, t)


def outer_kernel(
    at, lh, rh, e_ref, l_ref, r_ref, a_ref, c_ref, u_ref, v_ref, w_ref, t_ref, out_ref, mom_ref, acc
):
    left, right = edge_shifts(at[1])
    first = at[0] * NFB
    acc[...] = jnp.zeros_like(acc)

    def body(f, carry):
        def over(d, levels):
            levels = list(levels)
            cos, sin = twice(t_ref[0, d]), twice(t_ref[1, d])

            def load(i):
                if i < 2:
                    e = pltpu.roll(lh[i, f, d], left, 1)
                else:
                    e = pltpu.roll(rh[i - 6, f, d], right, 1)
                e = e * w_ref[i]
                return e, (c_ref[f, i] * cos + u_ref[0, i]) * e

            def stay(i, e, a):
                b = (c_ref[f, i] * sin + v_ref[0, i]) * e
                turn = row_below(jnp.maximum(b, 0.0)) - row_above(jnp.minimum(b, 0.0))
                return e - (jnp.abs(a) + jnp.abs(b)) + turn

            def store(k, i, value):
                value = value * w_ref[i]
                out_ref[k, f, d] = value
                levels[k] = levels[k] + value

            _, a0 = load(0)
            e1, a1 = load(1)
            store(0, 1, stay(1, e1, a1) + jnp.maximum(a0, 0.0) - l_ref[f, d])
            store(1, 2, e_ref[0, f, d] + jnp.maximum(a1, 0.0))
            e6, a6 = load(6)
            _, a7 = load(7)
            store(2, 5, e_ref[3, f, d] - jnp.minimum(a6, 0.0))
            store(3, 6, stay(6, e6, a6) + r_ref[f, d] - jnp.minimum(a7, 0.0))
            return tuple(levels)

        levels = lax.fori_loop(0, NQ, over, zeros(4), unroll=UNROLL)
        add_moments(acc, levels, frequency_of(first + f))
        return carry

    lax.fori_loop(0, NFB, body, 0)
    for m in range(2):
        parts = [acc[m, 1], a_ref[m, 0], a_ref[m, 1], acc[m, 2]]
        mom_ref[m, 0] = select4([quad_sum(x) for x in parts])
        mom_ref[m, 1] = jnp.where(lane_group() < 2, quad_sum(acc[m, 0]), quad_sum(acc[m, 3]))


def outer_step(at, lh, rh, inner, tables):
    return pl.pallas_call(
        outer_kernel,
        in_specs=[SM] + [VM] * 11,
        out_specs=[VM] * 2,
        out_shape=[
            jax.ShapeDtypeStruct((4, NFB, NQ, ROWS, LANES), F32),
            jax.ShapeDtypeStruct((2, 2, ROWS, LANES), F32),
        ],
        scratch_shapes=[pltpu.VMEM((2, 4, ROWS, LANES), F32)],
        compiler_params=PARAMS,
        cost_estimate=cost(3.0),
        name="outer_step",
    )(at, lh, rh, *inner, *tables)


def strength_of(parts, k):
    def total(m):
        a = [p[(m,) + k] for p in parts]
        return (a[0] + a[1]) + (a[2] + a[3])

    zeroth, first_moment = total(0), total(1)
    return DISSIPATION * zeroth * (first_moment / jnp.maximum(zeroth, MOMENT_FLOOR))


def second_kernel(
    at, in_ref, edge_ref, m0, m1, m2, m3, c_ref, u_ref, v_ref, w_ref, t_ref,
    out_ref, mom_ref, acc, s_scr, d_scr,
):
    first = at[0] * NFB
    acc[...] = jnp.zeros_like(acc)
    own = quad_spread(strength_of((m0, m1, m2, m3), (0,)))
    edge = quad_spread(strength_of((m0, m1, m2, m3), (1,)))
    for i, x in enumerate((edge[0],) + own + (edge[2],)):
        s_scr[i] = x

    def body(f, carry):
        freq = frequency_of(first + f)
        square = freq * freq
        for i in range(6):
            d_scr[i] = 1.0 / (1.0 + s_scr[i] * square)
        def over(d, levels):
            levels = list(levels)

            def store(i, value):
                out_ref[i - 1, f, d] = value
                levels[i - 1] = levels[i - 1] + value

            def energy(i):
                if i in (2, 3):
                    return in_ref[i - 1, f, d] * d_scr[i]
                return edge_ref[(0, 1, 0, 0, 2, 3)[i], f, d] * d_scr[i]

            advance(
                6,
                energy,
                lambda i: c_ref[f, i + 1],
                lambda i: u_ref[1, i + 1],
                lambda i: v_ref[1, i + 1],
                lambda i: w_ref[i + 1],
                twice(t_ref[0, d]),
                twice(t_ref[1, d]),
                store,
            )
            return tuple(levels)

        levels = lax.fori_loop(0, NQ, over, zeros(4), unroll=UNROLL)
        add_moments(acc, levels, freq)
        return carry

    lax.fori_loop(0, NFB, body, 0)
    for m in range(2):
        mom_ref[m] = select4([quad_sum(acc[m, i]) for i in range(4)])


def second_step(at, e, edges, moments, c, u, v, w, t):
    return pl.pallas_call(
        second_kernel,
        in_specs=[SM] + [VM] * 11,
        out_specs=[VM] * 2,
        out_shape=[
            jax.ShapeDtypeStruct((4, NFB, NQ, ROWS, LANES), F32),
            jax.ShapeDtypeStruct((2, ROWS, LANES), F32),
        ],
        scratch_shapes=[
            pltpu.VMEM((2, 4, ROWS, LANES), F32),
            pltpu.VMEM((6, ROWS, LANES), F32),
            pltpu.VMEM((6, ROWS, LANES), F32),
        ],
        compiler_params=PARAMS,
        cost_estimate=cost(3.5),
        name="second_step",
    )(at, e, edges, *moments, c, u, v, w, t)


def unpack_kernel(e_ref, out_ref):
    def body(f, carry):
        for d in range(NQ):
            out = quad_transpose([e_ref[c, f, d] for c in range(4)])
            for q in range(4):
                out_ref[f, d + NQ * q] = out[q]
        return carry

    lax.fori_loop(0, NFB, body, 0)


def unpack(e):
    return pl.pallas_call(
        unpack_kernel,
        in_specs=[VM],
        out_specs=VM,
        out_shape=jax.ShapeDtypeStruct((NFB, ND, ROWS, LANES), F32),
        compiler_params=PARAMS,
        cost_estimate=cost(2.0),
        name="unpack",
    )(e)


def last_kernel(at, e_ref, m0, m1, m2, m3, out_hbm, buf, sem):
    first = at[0] * NFB
    strength = strength_of((m0, m1, m2, m3), ())

    def save(f):
        return pltpu.make_async_copy(buf.at[f], out_hbm.at[f], sem.at[f])

    def body(f, carry):
        freq = frequency_of(first + f)
        damp = 1.0 / (1.0 + strength * (freq * freq))
        for d in range(ND):
            buf[f, d] = e_ref[f, d] * damp
        save(f).start()
        return carry

    lax.fori_loop(0, NFB, body, 0)
    for f in range(NFB):
        save(f).wait()


def last_step(at, e, moments):
    return pl.pallas_call(
        last_kernel,
        in_specs=[SM] + [VM] * 5,
        out_specs=HB,
        out_shape=jax.ShapeDtypeStruct((NFB, ND, ROWS, LANES), F32),
        scratch_shapes=[
            pltpu.VMEM((NFB, ND, ROWS, LANES), F32),
            pltpu.SemaphoreType.DMA((NFB,)),
        ],
        compiler_params=PARAMS,
        cost_estimate=cost(1.5),
        name="last_step",
    )(at, e, *moments)


RIGHT = [(i, (i + 1) % PTS) for i in range(PTS)]
LEFT = [(b, a) for a, b in RIGHT]


def band_parts(x):
    return [x] + [
        lax.ppermute(x, "band", [(i, i ^ k) for i in range(BANDS)]) for k in range(1, BANDS)
    ]


def per_device(spectra, currents, bathymetry, sea_mask):
    forcing = jnp.concatenate(
        [
            currents.reshape(3 * SUBSTEPS, 4, LANES),
            bathymetry[None],
            sea_mask.astype(F32)[None],
        ],
        0,
    ).reshape(4 * FIELDS, LANES)
    at = jnp.stack([lax.axis_index("band"), lax.axis_index("pts")]).astype(jnp.int32)
    windows = forcing_windows(forcing)
    windows = lax.all_to_all(windows, ("band", "pts"), 0, 0, tiled=True)
    ml, mr = pack(jnp.transpose(spectra, (1, 2, 0, 3)))
    lh = lax.ppermute(mr, "pts", RIGHT)
    rh = lax.ppermute(ml, "pts", LEFT)
    *tables, depth = speeds(at, windows)
    inner = inner_step(at, ml, mr, *tables)
    edges, moments = outer_step(at, lh, rh, inner, tables)
    tables[0] = second_speeds(at, depth)
    e, moments = second_step(at, inner[0], edges, band_parts(moments), *tables)
    return jnp.transpose(last_step(at, unpack(e), band_parts(moments)), (2, 0, 1, 3))


def solution(mesh):
    in_specs = (
        P(None, "band", None, "pts"),
        P(None, None, "band", "pts"),
        P("band", "pts"),
        P("band", "pts"),
    )
    out_specs = P(None, "band", None, "pts")
    return jax.shard_map(
        per_device, mesh=mesh, in_specs=in_specs, out_specs=out_specs, check_vma=False
    )
```

time: 68.2 us -> 64.1 us (0.940)
  blocking collectives: 11.7 us -> 0 us
  waiting for transfers between devices: 9.55 us -> 13.9 us
  starting transfers between devices: 18.7 us -> 22.4 us
  Pallas kernels: 26.1 us -> 25.4 us
    all_to_all x1 -> x0, blocking collectives: 11.7 us -> none  [per_device(): windows = lax.all_to_all(windows, 'pts', 0, 0, tiled=True)]
    all_to_all x0 -> x1, waiting for transfers between devices: none -> 10.7 us  [per_device(): windows = lax.all_to_all(windows, ('band', 'pts'), 0, 0, tiled=True)]
    all_to_all x0 -> x1, starting transfers between devices: none -> 6.87 us  [per_device(): windows = lax.all_to_all(windows, ('band', 'pts'), 0, 0, tiled=True)]
    ppermute x9 -> x6, waiting for transfers between devices: 9.55 us -> 3.14 us  [band_parts(): lax.ppermute(x, 'band', [(i, i ^ k) for i in range(BANDS)])]
    ppermute x9 -> x6, starting transfers between devices: 12.5 us -> 9.55 us  [band_parts(): lax.ppermute(x, 'band', [(i, i ^ k) for i in range(BANDS)])]
    pallas_call x6 -> x9, Pallas kernels: 26.1 us -> 25.4 us  [the longest x1 5.72 us: pack(): pl.pallas_call(pack_kernel, in_specs=[VM], out_specs=[VM, VM], out_shape=...]
  transfers between devices with their start and end apart: 11 -> 9, of which waited for: 6 -> 4; matrix products, arithmetic and copies ran while one was open for 0% -> 0% of each run, Pallas kernels for 6% -> 18%
where the time goes in v2:
time: 64.1 us; the launch traced here: 63.6 us
  Pallas kernels  25.4 us (40%)
  starting transfers between devices  22.4 us (35%)
  waiting for transfers between devices  13.9 us (22%)
  local copies, waits for them, and re-layouts  1.76 us (3%)
    all_to_all x1, waiting for transfers between devices, per_device(): windows = lax.all_to_all(windows, ('band', 'pts'), 0, 0, tiled=True)  10.7 us
    ppermute x6, starting transfers between devices, band_parts(): lax.ppermute(x, 'band', [(i, i ^ k) for i in range(BANDS)])  9.55 us
    all_to_all x1, starting transfers between devices, per_device(): windows = lax.all_to_all(windows, ('band', 'pts'), 0, 0, tiled=True)  6.87 us
    ppermute x1, starting transfers between devices, per_device(): rh = lax.ppermute(ml, 'pts', LEFT)  6.01 us
    pallas_call x1, Pallas kernels, pack(): pl.pallas_call(pack_kernel, in_specs=[VM], out_specs=[VM, VM], out_shape=...  5.72 us
    pallas_call x1, Pallas kernels, inner_step(): pl.pallas_call(inner_kernel, in_specs=[SM] + [VM] * 7, out_specs=[VM] * 4...  3.93 us
    pallas_call x1, Pallas kernels, second_step(): pl.pallas_call(second_kernel, in_specs=[SM] + [VM] * 11, out_specs=[VM] *...  3.35 us
    ppermute x6, waiting for transfers between devices, band_parts(): lax.ppermute(x, 'band', [(i, i ^ k) for i in range(BANDS)])  3.14 us
  transfers between devices with their start and end apart: 9, of which 4 were waited for; matrix products, arithmetic and copies ran while one was open for 0% of the time, Pallas kernels for 18%

profile of v2, /device:TPU:0, one launch (start us, length us, event | category | flops | bytes accessed | tf_op | source)
XLA Modules:
  0.0 63.6 jit_solution(18320153763348806744)
XLA Ops:
  0.0 0.0 copy-start
  0.0 1.7 %copy-done = f32[16,9,36,128]{3,0,2,1:T(8,128)S(1)} copy-done((f32[16,9,36,128]{3,0,2,1:T(8,128)S(1)}, f32[16,9,36,128]{3,0,2,1:T(8,128)}, u32[]{:S(2)}) %copy-start) | copy-done | bytes 2654232
  1.8 0.0 copy-start.3
  1.8 0.0 copy-start.1
  1.8 0.0 copy-start.2
  1.8 5.7 %pack.1 = (f32[2,9,9,16,128]{4,3,2,1,0:T(8,128)}, f32[2,9,9,16,128]{4,3,2,1,0:T(8,128)}) custom-call(f32[9,36,16,128]{3,2,1,0:T(8,128)S(1)} %bitcast.9), custom_call_target="tpu_custom_call" | custom-call | bytes 6000000 | tf_op jit(solution)/shard_map/pack/pallas_call | solution.py:118
  7.5 0.0 collective-permute-start
  7.5 6.0 %collective-permute-start.1 = (f32[2,9,9,16,128]{4,3,2,1,0:T(8,128)}, f32[2,9,9,16,128]{4,3,2,1,0:T(8,128)S(1)}, u32[]{:S(2)}, u32[]{:S(2)}) collective-permute-start(f32[2,9,9,16,128]{4,3,2,1,0:T(8,128)} %get-tuple-element.21.ml), channel_id=1, source_target_pairs={{1,0},{2,1},{3,2},{4,3},{5,4},{6,5},{7,6},{8,7},{9,8},{10,9},{11,1... | collective-permute-start | bytes 3981320 | tf_op jit(solution)/shard_map/ppermute | solution.py:591
  13.5 0.0 copy-done.3
  13.5 0.0 copy-done.1
  13.5 0.0 copy-done.2
  13.5 1.0 %forcing.1 = f32[128,2,128]{2,1,0:T(2,128)} custom-call(f32[32,128]{1,0:T(8,128)S(1)} %bitcast.10), custom_call_target="tpu_custom_call" | custom-call | bytes 2400000 | tf_op jit(solution)/shard_map/forcing/pallas_call | solution.py:150
  14.5 6.9 %all-to-all-start = ((f32[128,2,128]{2,1,0:T(2,128)}), f32[128,2,128]{2,1,0:T(2,128)S(1)}, u32[]{:S(2)}, u32[]{:S(2)}) async-start(f32[128,2,128]{2,1,0:T(2,128)} %forcing.1), calls=%async_computation | async-start | bytes 262144 | tf_op jit(solution)/shard_map/all_to_all | solution.py:588
  21.4 0.1 pad_add_fusion.at
  21.5 10.7 %all-to-all-done.win = f32[128,2,128]{2,1,0:T(2,128)S(1)} async-done(((f32[128,2,128]{2,1,0:T(2,128)}), f32[128,2,128]{2,1,0:T(2,128)S(1)}, u32[]{:S(2)}, u32[]{:S(2)}) %all-to-all-start) | async-done | bytes 131104 | tf_op jit(solution)/shard_map/all_to_all | solution.py:588
  32.2 2.7 %speeds.1 = (f32[9,8,16,128]{3,2,1,0:T(8,128)S(1)}, f32[2,8,16,128]{3,2,1,0:T(8,128)S(1)}, f32[2,8,16,128]{3,2,1,0:T(8,128)S(1)}, f32[8,16,128]{2,1,0:T(8,128)S(...) custom-call(s32[2]{0:T(128)S(1)} %pad_add_fusion.at, f32[128,2,128]{2,1,0:T(2,128)S(1)} %all-to-all-done.win), custom_call_target="tpu_custom_call" | custom-call | bytes 6000000 | tf_op jit(solution)/shard_map/speeds/pallas_call | solution.py:218
  35.0 3.9 %inner_step.1 = (f32[4,9,9,16,128]{4,3,2,1,0:T(8,128)S(1)}, f32[9,9,16,128]{3,2,1,0:T(8,128)S(1)}, f32[9,9,16,128]{3,2,1,0:T(8,128)S(1)}, f32[2,2,16,128]{3,2,1,0:T(8,128)S(1)}) custom-call(s32[2]{0:T(128)S(1)} %pad_add_fusion.at, f32[2,9,9,16,128]{4,3,2,1,0:T(8,128)} %get-tuple-element.21.ml, f32[2,9,9,16,128]{4,3,2,1,0:T(8,128)} %get-tuple-element.22.mr, ...), custom_call_target="tpu_custom_call" | custom-call | bytes 12000000 | tf_op jit(solution)/shard_map/inner_step/pallas_call | solution.py:346
  38.9 0.0 collective-permute-done.lh
  38.9 0.0 collective-permute-done.1.rh
  38.9 2.8 %outer_step.1 = (f32[4,9,9,16,128]{4,3,2,1,0:T(8,128)S(1)}, f32[2,2,16,128]{3,2,1,0:T(8,128)S(1)}) custom-call(s32[2]{0:T(128)S(1)} %pad_add_fusion.at, f32[2,9,9,16,128]{4,3,2,1,0:T(8,128)S(1)} %collective-permute-done.lh, f32[2,9,9,16,128]{4,3,2,1,0:T(8,128)S(1)} %collective-permute-done.1.rh, f32[4,9,9,16,128]{4,3,2,1,0:T(8,128)S(1)} %get-tuple-element.28.e_ref.in_ref, ...), custom_call_target="tpu_custom_call" | custom-call | bytes 9000000 | tf_op jit(solution)/shard_map/outer_step/pallas_call | solution.py:414
  41.7 1.6 %collective-permute-start.2 = (f32[2,2,16,128]{3,2,1,0:T(8,128)S(1)}, f32[2,2,16,128]{3,2,1,0:T(8,128)S(1)}, u32[]{:S(2)}, u32[]{:S(2)}) collective-permute-start(f32[2,2,16,128]{3,2,1,0:T(8,128)S(1)} %get-tuple-element.33.m0), channel_id=1, source_target_pairs={{0,32},{32,0},{64,96},{96,64},{1,33},{33,1},{65,97},{97,65},{2,34}... | collective-permute-start | bytes 98312 | tf_op jit(solution)/shard_map/ppermute | solution.py:573
  43.3 2.7 %collective-permute-start.3 = (f32[2,2,16,128]{3,2,1,0:T(8,128)S(1)}, f32[2,2,16,128]{3,2,1,0:T(8,128)S(1)}, u32[]{:S(2)}, u32[]{:S(2)}) collective-permute-start(f32[2,2,16,128]{3,2,1,0:T(8,128)S(1)} %get-tuple-element.33.m0), channel_id=1, source_target_pairs={{0,64},{32,96},{64,0},{96,32},{1,65},{33,97},{65,1},{97,33},{2,66}... | collective-permute-start | bytes 98312 | tf_op jit(solution)/shard_map/ppermute | solution.py:573
  46.0 0.5 collective-permute-start.4
  46.5 1.9 %second_speeds.1.c_ref = f32[9,8,16,128]{3,2,1,0:T(8,128)S(1)} custom-call(s32[2]{0:T(128)S(1)} %pad_add_fusion.at, f32[2,16,128]{2,1,0:T(8,128)S(1)} %get-tuple-element.34.h_ref), custom_call_target="tpu_custom_call" | custom-call | bytes 4500000 | tf_op jit(solution)/shard_map/second_speeds/pallas_call | solution.py:245
  48.5 0.0 collective-permute-done.2.m1
  48.5 0.2 collective-permute-done.3.m2
  48.7 2.4 %collective-permute-done.4.m3 = f32[2,2,16,128]{3,2,1,0:T(8,128)S(1)} collective-permute-done((f32[2,2,16,128]{3,2,1,0:T(8,128)S(1)}, f32[2,2,16,128]{3,2,1,0:T(8,128)S(1)}, u32[]{:S(2)}, u32[]{:S(2)}) %collective-permute-start.4) | collective-permute-done | bytes 32800 | tf_op jit(solution)/shard_map/ppermute | solution.py:573
  51.2 3.4 %second_step.1 = (f32[4,9,9,16,128]{4,3,2,1,0:T(8,128)S(1)}, f32[2,16,128]{2,1,0:T(8,128)S(1)}) custom-call(s32[2]{0:T(128)S(1)} %pad_add_fusion.at, f32[4,9,9,16,128]{4,3,2,1,0:T(8,128)S(1)} %get-tuple-element.28.e_ref.in_ref, f32[4,9,9,16,128]{4,3,2,1,0:T(8,128)S(1)} %get-tuple-element.32.edge_ref, f32[2,2,16,128]{3,2,1,0:T(8,128)S(1)} %get-tuple-element.33.m0, ...), custom_call_target="tpu_custom_call" | custom-call | bytes 10500000 | tf_op jit(solution)/shard_map/second_step/pallas_call | solution.py:489
  54.5 0.1 collective-permute-start.5
  54.6 1.9 %collective-permute-start.6 = (f32[2,16,128]{2,1,0:T(8,128)S(1)}, f32[2,16,128]{2,1,0:T(8,128)S(1)}, u32[]{:S(2)}, u32[]{:S(2)}) collective-permute-start(f32[2,16,128]{2,1,0:T(8,128)S(1)} %get-tuple-element.36.m0), channel_id=1, source_target_pairs={{0,64},{32,96},{64,0},{96,32},{1,65},{33,97},{65,1},{97,33},{2,66}... | collective-permute-start | bytes 49160 | tf_op jit(solution)/shard_map/ppermute | solution.py:573
  56.5 2.8 %collective-permute-start.7 = (f32[2,16,128]{2,1,0:T(8,128)S(1)}, f32[2,16,128]{2,1,0:T(8,128)S(1)}, u32[]{:S(2)}, u32[]{:S(2)}) collective-permute-start(f32[2,16,128]{2,1,0:T(8,128)S(1)} %get-tuple-element.36.m0), channel_id=1, source_target_pairs={{0,96},{32,64},{64,32},{96,0},{1,97},{33,65},{65,33},{97,1},{2,98}... | collective-permute-start | bytes 49160 | tf_op jit(solution)/shard_map/ppermute | solution.py:573
  59.3 1.7 %unpack.1.e_ref = f32[9,36,16,128]{3,2,1,0:T(8,128)S(1)} custom-call(f32[4,9,9,16,128]{4,3,2,1,0:T(8,128)S(1)} %get-tuple-element.35.e_ref), custom_call_target="tpu_custom_call" | custom-call | bytes 6000000 | tf_op jit(solution)/shard_map/unpack/pallas_call | solution.py:520
  61.0 0.0 collective-permute-done.5.m1
  61.0 0.0 collective-permute-done.6.m2
  61.0 0.5 collective-permute-done.7.m3
  61.5 2.2 %last_step.1 = f32[9,36,16,128]{3,2,1,0:T(8,128)} custom-call(s32[2]{0:T(128)S(1)} %pad_add_fusion.at, f32[9,36,16,128]{3,2,1,0:T(8,128)S(1)} %unpack.1.e_ref, f32[2,16,128]{2,1,0:T(8,128)S(1)} %get-tuple-element.36.m0, f32[2,16,128]{2,1,0:T(8,128)S(1)} %collective-permute-done.5.m1, f32[2,16,128]{2,1,0:T(8,128)S(1)} %collective-permute-done.6.m2, ...), custom_call_target="tpu_custom_call" | custom-call | bytes 4500000 | tf_op jit(solution)/shard_map/last_step/pallas_call | solution.py:552
  (2 shorter events, 0.0 us)
Async XLA Ops:
  0.0 1.7 %copy-start = (f32[16,9,36,128]{3,0,2,1:T(8,128)S(1)}, f32[16,9,36,128]{3,0,2,1:T(8,128)}, u32[]{:S(2)}) copy-start(f32[16,9,36,128]{3,0,2,1:T(8,128)} %param.4) | copy-start | bytes 7962628
  1.8 11.7 %copy-start.3 = (s32[4,128]{1,0:T(4,128)S(1)}, s32[4,128]{1,0:T(4,128)}, u32[]{:S(2)}) copy-start(s32[4,128]{1,0:T(4,128)} %param.7) | copy-start | bytes 6148
  1.8 11.7 %copy-start.1 = (f32[2,3,4,128]{3,2,1,0:T(4,128)S(1)}, f32[2,3,4,128]{3,2,1,0:T(4,128)}, u32[]{:S(2)}) copy-start(f32[2,3,4,128]{3,2,1,0:T(4,128)} %param.5) | copy-start | bytes 36868
  1.8 11.7 %copy-start.2 = (f32[4,128]{1,0:T(4,128)S(1)}, f32[4,128]{1,0:T(4,128)}, u32[]{:S(2)}) copy-start(f32[4,128]{1,0:T(4,128)} %param.6) | copy-start | bytes 6148
  7.5 31.4 %collective-permute-start = (f32[2,9,9,16,128]{4,3,2,1,0:T(8,128)}, f32[2,9,9,16,128]{4,3,2,1,0:T(8,128)S(1)}, u32[]{:S(2)}, u32[]{:S(2)}) collective-permute-start(f32[2,9,9,16,128]{4,3,2,1,0:T(8,128)} %get-tuple-element.22.mr), channel_id=1, source_target_pairs={{0,1},{1,2},{2,3},{3,4},{4,5},{5,6},{6,7},{7,8},{8,9},{9,10},{10,1... | collective-permute-start | bytes 3981320 | tf_op jit(solution)/shard_map/ppermute | solution.py:590
  7.5 31.4 %collective-permute-start.1 = (f32[2,9,9,16,128]{4,3,2,1,0:T(8,128)}, f32[2,9,9,16,128]{4,3,2,1,0:T(8,128)S(1)}, u32[]{:S(2)}, u32[]{:S(2)}) collective-permute-start(f32[2,9,9,16,128]{4,3,2,1,0:T(8,128)} %get-tuple-element.21.ml), channel_id=1, source_target_pairs={{1,0},{2,1},{3,2},{4,3},{5,4},{6,5},{7,6},{8,7},{9,8},{10,9},{11,1... | collective-permute-start | bytes 3981320 | tf_op jit(solution)/shard_map/ppermute | solution.py:591
  14.5 17.7 %all-to-all-start = ((f32[128,2,128]{2,1,0:T(2,128)}), f32[128,2,128]{2,1,0:T(2,128)S(1)}, u32[]{:S(2)}, u32[]{:S(2)}) async-start(f32[128,2,128]{2,1,0:T(2,128)} %forcing.1), calls=%async_computation | async-start | bytes 262144 | tf_op jit(solution)/shard_map/all_to_all | solution.py:588
  41.7 6.7 %collective-permute-start.2 = (f32[2,2,16,128]{3,2,1,0:T(8,128)S(1)}, f32[2,2,16,128]{3,2,1,0:T(8,128)S(1)}, u32[]{:S(2)}, u32[]{:S(2)}) collective-permute-start(f32[2,2,16,128]{3,2,1,0:T(8,128)S(1)} %get-tuple-element.33.m0), channel_id=1, source_target_pairs={{0,32},{32,0},{64,96},{96,64},{1,33},{33,1},{65,97},{97,65},{2,34}... | collective-permute-start | bytes 98312 | tf_op jit(solution)/shard_map/ppermute | solution.py:573
  43.3 5.4 %collective-permute-start.3 = (f32[2,2,16,128]{3,2,1,0:T(8,128)S(1)}, f32[2,2,16,128]{3,2,1,0:T(8,128)S(1)}, u32[]{:S(2)}, u32[]{:S(2)}) collective-permute-start(f32[2,2,16,128]{3,2,1,0:T(8,128)S(1)} %get-tuple-element.33.m0), channel_id=1, source_target_pairs={{0,64},{32,96},{64,0},{96,32},{1,65},{33,97},{65,1},{97,33},{2,66}... | collective-permute-start | bytes 98312 | tf_op jit(solution)/shard_map/ppermute | solution.py:573
  46.0 5.1 %collective-permute-start.4 = (f32[2,2,16,128]{3,2,1,0:T(8,128)S(1)}, f32[2,2,16,128]{3,2,1,0:T(8,128)S(1)}, u32[]{:S(2)}, u32[]{:S(2)}) collective-permute-start(f32[2,2,16,128]{3,2,1,0:T(8,128)S(1)} %get-tuple-element.33.m0), channel_id=1, source_target_pairs={{0,96},{32,64},{64,32},{96,0},{1,97},{33,65},{65,33},{97,1},{2,98}... | collective-permute-start | bytes 98312 | tf_op jit(solution)/shard_map/ppermute | solution.py:573
  54.5 6.5 %collective-permute-start.5 = (f32[2,16,128]{2,1,0:T(8,128)S(1)}, f32[2,16,128]{2,1,0:T(8,128)S(1)}, u32[]{:S(2)}, u32[]{:S(2)}) collective-permute-start(f32[2,16,128]{2,1,0:T(8,128)S(1)} %get-tuple-element.36.m0), channel_id=1, source_target_pairs={{0,32},{32,0},{64,96},{96,64},{1,33},{33,1},{65,97},{97,65},{2,34}... | collective-permute-start | bytes 49160 | tf_op jit(solution)/shard_map/ppermute | solution.py:573
  54.6 6.4 %collective-permute-start.6 = (f32[2,16,128]{2,1,0:T(8,128)S(1)}, f32[2,16,128]{2,1,0:T(8,128)S(1)}, u32[]{:S(2)}, u32[]{:S(2)}) collective-permute-start(f32[2,16,128]{2,1,0:T(8,128)S(1)} %get-tuple-element.36.m0), channel_id=1, source_target_pairs={{0,64},{32,96},{64,0},{96,32},{1,65},{33,97},{65,1},{97,33},{2,66}... | collective-permute-start | bytes 49160 | tf_op jit(solution)/shard_map/ppermute | solution.py:573
  56.5 4.9 %collective-permute-start.7 = (f32[2,16,128]{2,1,0:T(8,128)S(1)}, f32[2,16,128]{2,1,0:T(8,128)S(1)}, u32[]{:S(2)}, u32[]{:S(2)}) collective-permute-start(f32[2,16,128]{2,1,0:T(8,128)S(1)} %get-tuple-element.36.m0), channel_id=1, source_target_pairs={{0,96},{32,64},{64,32},{96,0},{1,97},{33,65},{65,33},{97,1},{2,98}... | collective-permute-start | bytes 49160 | tf_op jit(solution)/shard_map/ppermute | solution.py:573

commit v3 on v2

v3 whole, which is shorter than its diff:
```python
import math

import jax
import jax.numpy as jnp
from jax import lax
from jax.experimental import pallas as pl
from jax.experimental.pallas import tpu as pltpu
from jax.sharding import PartitionSpec as P

GRAVITY = 9.81
COURANT = 0.02
DISSIPATION = 1.0
MOMENT_FLOOR = 0.01
FREQ_FIRST = 0.035
FREQ_STEP = 1.1
BAND_WIDTH = 0.0955
ND = 36
NQ = 9
NFB = 9
ROWS = 16
BANDS = 4
PTS = 32
SUBSTEPS = 2
FIELDS = 8
LANES = 128
F32 = jnp.float32
VMEM_LIMIT = 40 * 1024 * 1024
VM = pl.BlockSpec(memory_space=pltpu.VMEM)
SM = pl.BlockSpec(memory_space=pltpu.SMEM)
HB = pl.BlockSpec(memory_space=pltpu.HBM)
PARAMS = pltpu.CompilerParams(vmem_limit_bytes=VMEM_LIMIT)


def lane_group():
    return lax.broadcasted_iota(jnp.int32, (ROWS, LANES), 1) & 3


def lroll(x, shift):
    return pltpu.roll(x, shift % LANES, 1)


def lane_swap(x, distance):
    index = lax.broadcasted_iota(jnp.int32, x.shape, 1) ^ distance
    return jnp.take_along_axis(x, index, axis=1)


def quad_transpose(a):
    lane = lane_group()

    def exchange(x, y, distance):
        low = (lane & distance) == 0
        t = lane_swap(jnp.where(low, y, x), distance)
        return jnp.where(low, x, t), jnp.where(low, t, y)

    b0, b2 = exchange(a[0], a[2], 2)
    b1, b3 = exchange(a[1], a[3], 2)
    o0, o1 = exchange(b0, b1, 1)
    o2, o3 = exchange(b2, b3, 1)
    return o0, o1, o2, o3


def quad_spread(x):
    lane = lax.broadcasted_iota(jnp.int32, x.shape, 1)
    return tuple(jnp.take_along_axis(x, (lane & ~3) + k, axis=1) for k in range(4))


def quad_sum(x):
    x = x + lane_swap(x, 1)
    return x + lane_swap(x, 2)


def select4(x):
    lane = lane_group()
    return jnp.where(
        lane < 2, jnp.where(lane == 0, x[0], x[1]), jnp.where(lane == 2, x[2], x[3])
    )


def frequency_of(index):
    return FREQ_FIRST * jnp.exp(
        jnp.full((ROWS, LANES), index, jnp.int32).astype(F32) * math.log(FREQ_STEP)
    )


def edge_shifts(pts):
    left = jnp.where(pts == 0, 4, 0)
    right = jnp.where(pts == PTS - 1, LANES - 4, 0)
    return left, right


def cost(microseconds):
    return pl.CostEstimate(
        flops=0, transcendentals=0, bytes_accessed=int(microseconds * 3.0e6)
    )


def loop(count, body):
    lax.fori_loop(0, count, lambda i, carry: (body(i), carry)[1], 0)


def load_rows(ref, lead):
    return jnp.concatenate(
        [ref[lead + (pl.ds(parity, 8, stride=2), slice(None))] for parity in range(2)], axis=0
    )


def store_rows(ref, lead, value):
    for parity in range(2):
        ref[lead + (pl.ds(parity, 8, stride=2), slice(None))] = value[8 * parity : 8 * parity + 8]


def pack_kernel(e_ref, ml_ref, mr_ref):
    def body(f):
        for d in range(NQ):
            out = quad_transpose([load_rows(e_ref, (f, d + NQ * q)) for q in range(4)])
            ml_ref[0, f, d] = out[0]
            ml_ref[1, f, d] = out[1]
            mr_ref[0, f, d] = out[2]
            mr_ref[1, f, d] = out[3]

    loop(NFB, body)


def pack(spectra):
    shape = jax.ShapeDtypeStruct((2, NFB, NQ, ROWS, LANES), F32)
    return pl.pallas_call(
        pack_kernel,
        in_specs=[VM],
        out_specs=[VM, VM],
        out_shape=[shape, shape],
        compiler_params=PARAMS,
        cost_estimate=cost(2.0),
        name="pack",
    )(spectra)


def exact_dot(a, b, dims):
    return lax.dot_general(
        a, b, (dims, ((), ())), precision=lax.Precision.HIGHEST, preferred_element_type=F32
    )


def forcing_kernel(own, out_ref):
    shape = (8 * PTS, LANES)
    place = lax.broadcasted_iota(jnp.int32, shape, 0)
    wanted = (4 * (place & (PTS - 1)) + (place >> 5) + (LANES - 2)) & (LANES - 1)
    pick = (lax.broadcasted_iota(jnp.int32, shape, 1) == wanted).astype(F32)
    x = exact_dot(pick, own[...], ((1,), (1,)))
    for h in range(2):
        row = jnp.concatenate(
            [x[PTS * (4 * h + k) : PTS * (4 * h + k) + PTS] for k in range(4)], axis=1
        )
        for band in range(BANDS):
            out_ref[PTS * band : PTS * band + PTS, h, :] = row


def forcing_windows(forcing):
    return pl.pallas_call(
        forcing_kernel,
        in_specs=[VM],
        out_specs=VM,
        out_shape=jax.ShapeDtypeStruct((BANDS * PTS, 2, LANES), F32),
        compiler_params=PARAMS,
        cost_estimate=cost(0.8),
        name="forcing",
    )(forcing)


def spread_columns(x, y):
    a, b = quad_spread(x), quad_spread(y)
    return (b[2], b[3]) + a + (b[0], b[1])


def celerities(first, h_ref, c_ref):
    def body(f):
        angular = (2.0 * math.pi) * frequency_of(first + f)
        deep = angular * angular / GRAVITY
        speed = []
        for part in range(2):
            height = h_ref[part]
            wavenumber = deep / jnp.sqrt(jnp.tanh(deep * height))
            q = 2.0 * wavenumber * height
            ratio = 2.0 * q * jnp.exp(-q) / (1.0 - jnp.exp(-2.0 * q))
            speed.append((0.5 * COURANT) * (1.0 + ratio) * angular / wavenumber)
        for i, x in enumerate(spread_columns(*speed)):
            c_ref[f, i] = x

    loop(NFB, body)


def speed_kernel(at, win, c_ref, u_ref, v_ref, w_ref, h_ref, f_scr, h_scr):
    left, right = edge_shifts(at[1])
    shape = (PTS, LANES)
    place = lax.broadcasted_iota(jnp.int32, shape, 0)
    spread = ((lax.broadcasted_iota(jnp.int32, shape, 1) >> 2) == place).astype(F32)
    for band in range(BANDS):
        for h in range(2):
            block = win[PTS * band : PTS * band + PTS, h, :]
            fields = exact_dot(block, spread, ((0,), (0,)))
            for k in range(4):
                i = 4 * h + k
                part = fields[32 * k : 32 * k + 32]
                if i < 2:
                    part = pltpu.roll(part, left, 1)
                if i >= 6:
                    part = pltpu.roll(part, right, 1)
                for n in range(FIELDS):
                    f_scr[i, n, 4 * band : 4 * band + 4, :] = part[4 * n : 4 * n + 4]
    for i in range(8):
        w_ref[i] = load_rows(f_scr, (i, 7))
        for s in range(SUBSTEPS):
            u_ref[s, i] = COURANT * load_rows(f_scr, (i, 3 * s))
            v_ref[s, i] = COURANT * load_rows(f_scr, (i, 3 * s + 1))
    for s, ref in ((0, h_scr), (1, h_ref)):
        depth = [load_rows(f_scr, (i, 6)) + load_rows(f_scr, (i, 3 * s + 2)) for i in range(8)]
        ref[0] = select4(depth[2:6])
        ref[1] = select4([depth[6], depth[7], depth[0], depth[1]])
    celerities(at[0] * NFB, h_scr, c_ref)


def speeds(at, windows):
    return pl.pallas_call(
        speed_kernel,
        in_specs=[SM, VM],
        out_specs=[VM] * 5,
        out_shape=[
            jax.ShapeDtypeStruct((NFB, 8, ROWS, LANES), F32),
            jax.ShapeDtypeStruct((SUBSTEPS, 8, ROWS, LANES), F32),
            jax.ShapeDtypeStruct((SUBSTEPS, 8, ROWS, LANES), F32),
            jax.ShapeDtypeStruct((8, ROWS, LANES), F32),
            jax.ShapeDtypeStruct((2, ROWS, LANES), F32),
        ],
        scratch_shapes=[
            pltpu.VMEM((8, FIELDS, ROWS, LANES), F32),
            pltpu.VMEM((2, ROWS, LANES), F32),
        ],
        compiler_params=PARAMS,
        cost_estimate=cost(2.0),
        name="speeds",
    )(at, windows)


def turn_kernel(t_ref):
    for d in range(NQ):
        angle = (d + NQ * lane_group()[0:8]).astype(F32) * (2.0 * math.pi / ND)
        t_ref[0, d] = jnp.cos(angle)
        t_ref[1, d] = jnp.sin(angle)


def turns():
    return pl.pallas_call(
        turn_kernel,
        out_specs=VM,
        out_shape=jax.ShapeDtypeStruct((2, NQ, 8, LANES), F32),
        compiler_params=PARAMS,
        cost_estimate=cost(0.5),
        name="turns",
    )()


def second_speed_kernel(at, h_ref, c_ref):
    celerities(at[0] * NFB, h_ref, c_ref)


def second_speeds(at, h):
    return pl.pallas_call(
        second_speed_kernel,
        in_specs=[SM, VM],
        out_specs=VM,
        out_shape=jax.ShapeDtypeStruct((NFB, 8, ROWS, LANES), F32),
        compiler_params=PARAMS,
        cost_estimate=cost(1.5),
        name="second_speeds",
    )(at, h)


def row_flux(b):
    sub = lax.broadcasted_iota(jnp.int32, (8, LANES), 0)
    plus, minus = jnp.maximum(b, 0.0), jnp.minimum(b, 0.0)
    even = plus[0:8] + minus[8:16]
    odd = plus[8:16] + jnp.where(sub == 7, 0.0, pltpu.roll(minus[0:8], 7, 0))
    before = jnp.where(sub == 0, minus[0:8], pltpu.roll(odd, 1, 0))
    return jnp.concatenate([even - before, odd - even], axis=0)


def advance(count, energy, speed, current_x, current_y, cos, sin, store):
    plus = None
    entered = None
    part = None
    for i in range(count):
        e = energy(i)
        c = speed(i)
        a = (c * cos + current_x(i)) * e
        if plus is not None:
            crossed = plus + jnp.minimum(a, 0.0)
            if part is not None:
                store(i - 1, part - crossed)
            entered = crossed
        if 0 < i < count - 1:
            b = (c * sin + current_y(i)) * e
            part = e + entered - row_flux(b)
        plus = jnp.maximum(a, 0.0)


UNROLL = 9


def zeros(count):
    return tuple(jnp.zeros((ROWS, LANES), F32) for _ in range(count))


def twice(x):
    return jnp.concatenate([x, x], axis=0)


def add_moments(acc, levels, wet, freq):
    weight = (BAND_WIDTH * (2.0 * math.pi / ND)) * freq
    for i, level in enumerate(levels):
        t = level * wet(i) * weight
        acc[0, i] = acc[0, i] + t
        acc[1, i] = acc[1, i] + t * freq


def first_kernel(at, lh, ml, mr, rh, c_ref, u_ref, v_ref, w_ref, t_ref, out_ref, mom_ref, acc):
    left, right = edge_shifts(at[1])
    first = at[0] * NFB
    acc[...] = jnp.zeros_like(acc)

    def body(f):
        def over(d, levels):
            levels = list(levels)

            def store(i, value):
                out_ref[i - 1, f, d] = value
                levels[i - 1] = levels[i - 1] + value

            def energy(i):
                e = (lh, ml, mr, rh)[i // 2][i % 2, f, d]
                if i < 2:
                    e = pltpu.roll(e, left, 1)
                if i >= 6:
                    e = pltpu.roll(e, right, 1)
                return e * w_ref[i]

            advance(
                8,
                energy,
                lambda i: c_ref[f, i],
                lambda i: u_ref[0, i],
                lambda i: v_ref[0, i],
                twice(t_ref[0, d]),
                twice(t_ref[1, d]),
                store,
            )
            return tuple(levels)

        levels = lax.fori_loop(0, NQ, over, zeros(6), unroll=UNROLL)
        add_moments(acc, levels, lambda i: w_ref[i + 1], frequency_of(first + f))

    loop(NFB, body)
    for m in range(2):
        sums = [quad_sum(acc[m, i]) for i in range(6)]
        mom_ref[m, 0] = select4(sums[1:5])
        mom_ref[m, 1] = jnp.where(lane_group() < 2, sums[0], sums[5])


def first_step(at, lh, ml, mr, rh, tables):
    return pl.pallas_call(
        first_kernel,
        in_specs=[SM] + [VM] * 9,
        out_specs=[VM] * 2,
        out_shape=[
            jax.ShapeDtypeStruct((6, NFB, NQ, ROWS, LANES), F32),
            jax.ShapeDtypeStruct((2, 2, ROWS, LANES), F32),
        ],
        scratch_shapes=[pltpu.VMEM((2, 6, ROWS, LANES), F32)],
        compiler_params=PARAMS,
        cost_estimate=cost(5.0),
        name="first_step",
    )(at, lh, ml, mr, rh, *tables)


def strength_of(parts, k):
    def total(m):
        a = [p[(m,) + k] for p in parts]
        return (a[0] + a[1]) + (a[2] + a[3])

    zeroth, first_moment = total(0), total(1)
    return DISSIPATION * zeroth * (first_moment / jnp.maximum(zeroth, MOMENT_FLOOR))


def second_kernel(
    at, e_ref, m0, m1, m2, m3, c_ref, u_ref, v_ref, w_ref, t_ref,
    out_ref, mom_ref, acc, s_scr, d_scr,
):
    first = at[0] * NFB
    acc[...] = jnp.zeros_like(acc)
    own = quad_spread(strength_of((m0, m1, m2, m3), (0,)))
    edge = quad_spread(strength_of((m0, m1, m2, m3), (1,)))
    for i, x in enumerate((edge[0],) + own + (edge[2],)):
        s_scr[i] = x

    def body(f, carry):
        freq = frequency_of(first + f)
        square = freq * freq
        for i in range(6):
            d_scr[i] = w_ref[i + 1] / (1.0 + s_scr[i] * square)
        def over(d, levels):
            levels = list(levels)

            def store(i, value):
                out_ref[i - 1, f, d] = value
                levels[i - 1] = levels[i - 1] + value

            advance(
                6,
                lambda i: e_ref[i, f, d] * d_scr[i],
                lambda i: c_ref[f, i + 1],
                lambda i: u_ref[1, i + 1],
                lambda i: v_ref[1, i + 1],
                twice(t_ref[0, d]),
                twice(t_ref[1, d]),
                store,
            )
            return tuple(levels)

        levels = lax.fori_loop(0, NQ, over, zeros(4), unroll=UNROLL)
        add_moments(acc, levels, lambda i: w_ref[i + 2], freq)
        return carry

    lax.fori_loop(0, NFB, body, 0)
    for m in range(2):
        mom_ref[m] = select4([quad_sum(acc[m, i]) for i in range(4)])


def second_step(at, e, moments, c, u, v, w, t):
    return pl.pallas_call(
        second_kernel,
        in_specs=[SM] + [VM] * 10,
        out_specs=[VM] * 2,
        out_shape=[
            jax.ShapeDtypeStruct((4, NFB, NQ, ROWS, LANES), F32),
            jax.ShapeDtypeStruct((2, ROWS, LANES), F32),
        ],
        scratch_shapes=[
            pltpu.VMEM((2, 4, ROWS, LANES), F32),
            pltpu.VMEM((6, ROWS, LANES), F32),
            pltpu.VMEM((6, ROWS, LANES), F32),
        ],
        compiler_params=PARAMS,
        cost_estimate=cost(3.5),
        name="second_step",
    )(at, e, *moments, c, u, v, w, t)


def unpack_kernel(e_ref, out_ref):
    def body(f, carry):
        for d in range(NQ):
            out = quad_transpose([e_ref[c, f, d] for c in range(4)])
            for q in range(4):
                store_rows(out_ref, (f, d + NQ * q), out[q])
        return carry

    lax.fori_loop(0, NFB, body, 0)


def unpack(e):
    return pl.pallas_call(
        unpack_kernel,
        in_specs=[VM],
        out_specs=VM,
        out_shape=jax.ShapeDtypeStruct((NFB, ND, ROWS, LANES), F32),
        compiler_params=PARAMS,
        cost_estimate=cost(2.0),
        name="unpack",
    )(e)


def last_kernel(at, e_ref, w_ref, m0, m1, m2, m3, out_hbm, buf, s_scr, sem):
    first = at[0] * NFB
    store_rows(s_scr, (0,), strength_of((m0, m1, m2, m3), ()))
    store_rows(s_scr, (1,), select4([w_ref[i] for i in range(2, 6)]))

    def save(f):
        return pltpu.make_async_copy(buf.at[f], out_hbm.at[f], sem.at[f])

    def body(f, carry):
        freq = frequency_of(first + f)
        damp = s_scr[1] / (1.0 + s_scr[0] * (freq * freq))
        for d in range(ND):
            buf[f, d] = e_ref[f, d] * damp
        save(f).start()
        return carry

    lax.fori_loop(0, NFB, body, 0)
    for f in range(NFB):
        save(f).wait()


def last_step(at, e, w, moments):
    return pl.pallas_call(
        last_kernel,
        in_specs=[SM] + [VM] * 6,
        out_specs=HB,
        out_shape=jax.ShapeDtypeStruct((NFB, ND, ROWS, LANES), F32),
        scratch_shapes=[
            pltpu.VMEM((NFB, ND, ROWS, LANES), F32),
            pltpu.VMEM((2, ROWS, LANES), F32),
            pltpu.SemaphoreType.DMA((NFB,)),
        ],
        compiler_params=PARAMS,
        cost_estimate=cost(1.5),
        name="last_step",
    )(at, e, w, *moments)


RIGHT = [(i, (i + 1) % PTS) for i in range(PTS)]
LEFT = [(b, a) for a, b in RIGHT]


def band_parts(x):
    return [x] + [
        lax.ppermute(x, "band", [(i, i ^ k) for i in range(BANDS)]) for k in range(1, BANDS)
    ]


def per_device(spectra, currents, bathymetry, sea_mask):
    forcing = jnp.concatenate(
        [
            currents.reshape(3 * SUBSTEPS, 4, LANES),
            bathymetry[None],
            sea_mask.astype(F32)[None],
        ],
        0,
    ).reshape(4 * FIELDS, LANES)
    at = jnp.stack([lax.axis_index("band"), lax.axis_index("pts")]).astype(jnp.int32)
    windows = forcing_windows(forcing)
    ml, mr = pack(jnp.transpose(spectra, (1, 2, 0, 3)))
    windows = lax.all_to_all(windows, ("band", "pts"), 0, 0, tiled=True)
    lh = lax.ppermute(mr, "pts", RIGHT)
    rh = lax.ppermute(ml, "pts", LEFT)
    turn = turns()
    c, u, v, w, depth = speeds(at, windows)
    e, moments = first_step(at, lh, ml, mr, rh, (c, u, v, w, turn))
    c = second_speeds(at, depth)
    e, moments = second_step(at, e, band_parts(moments), c, u, v, w, turn)
    return jnp.transpose(last_step(at, unpack(e), w, band_parts(moments)), (2, 0, 1, 3))


def solution(mesh):
    in_specs = (
        P(None, "band", None, "pts"),
        P(None, None, "band", "pts"),
        P("band", "pts"),
        P("band", "pts"),
    )
    out_specs = P(None, "band", None, "pts")
    return jax.shard_map(
        per_device, mesh=mesh, in_specs=in_specs, out_specs=out_specs, check_vma=False
    )
```

time: 64.1 us -> 58.2 us (0.908)
  Pallas kernels: 25.4 us -> 19.7 us
    pallas_call x1, Pallas kernels: 5.72 us -> 1.71 us  [pack(): pl.pallas_call(pack_kernel, in_specs=[VM], out_specs=[VM, VM], out_shape=...]
    pallas_call x5, Pallas kernels: 15 us -> 13.4 us  [the longest x1 5.34 us: first_step(): pl.pallas_call(first_kernel, in_specs=[SM] + [VM] * 9, out_specs=[VM] * 2...]
  transfers between devices with their start and end apart: 9 -> 9, of which waited for: 4 -> 4; matrix products, arithmetic and copies ran while one was open for 0% -> 0% of each run, Pallas kernels for 18% -> 13%
where the time goes in v3:
time: 58.2 us; the launch traced here: 57.7 us
  starting transfers between devices  22.5 us (39%)
  Pallas kernels  19.7 us (34%)
  waiting for transfers between devices  13.5 us (23%)
  local copies, waits for them, and re-layouts  1.76 us (3%)
    all_to_all x1, waiting for transfers between devices, per_device(): windows = lax.all_to_all(windows, ('band', 'pts'), 0, 0, tiled=True)  10.3 us
    ppermute x6, starting transfers between devices, band_parts(): lax.ppermute(x, 'band', [(i, i ^ k) for i in range(BANDS)])  9.55 us
    all_to_all x1, starting transfers between devices, per_device(): windows = lax.all_to_all(windows, ('band', 'pts'), 0, 0, tiled=True)  6.79 us
    ppermute x1, starting transfers between devices, per_device(): rh = lax.ppermute(ml, 'pts', LEFT)  6.08 us
    pallas_call x1, Pallas kernels, first_step(): pl.pallas_call(first_kernel, in_specs=[SM] + [VM] * 9, out_specs=[VM] * 2...  5.34 us
    ppermute x6, waiting for transfers between devices, band_parts(): lax.ppermute(x, 'band', [(i, i ^ k) for i in range(BANDS)])  3.14 us
    pallas_call x1, Pallas kernels, second_step(): pl.pallas_call(second_kernel, in_specs=[SM] + [VM] * 10, out_specs=[VM] *...  3.02 us
    pallas_call x1, Pallas kernels, speeds(): pl.pallas_call(speed_kernel, in_specs=[SM, VM], out_specs=[VM] * 5, out_s...  2.67 us
  transfers between devices with their start and end apart: 9, of which 4 were waited for; matrix products, arithmetic and copies ran while one was open for 0% of the time, Pallas kernels for 13%

profile of v3, /device:TPU:0, one launch (start us, length us, event | category | flops | bytes accessed | tf_op | source)
XLA Modules:
  0.0 57.7 jit_solution(2068329194449745724)
XLA Ops:
  0.0 0.0 copy-start
  0.0 1.7 %copy-done = f32[16,9,36,128]{3,0,2,1:T(8,128)S(1)} copy-done((f32[16,9,36,128]{3,0,2,1:T(8,128)S(1)}, f32[16,9,36,128]{3,0,2,1:T(8,128)}, u32[]{:S(2)}) %copy-start) | copy-done | bytes 2654232
  1.8 0.0 copy-start.3
  1.8 0.0 copy-start.1
  1.8 0.0 copy-start.2
  1.8 1.7 %pack.1 = (f32[2,9,9,16,128]{4,3,2,1,0:T(8,128)S(1)}, f32[2,9,9,16,128]{4,3,2,1,0:T(8,128)S(1)}) custom-call(f32[9,36,16,128]{3,2,1,0:T(8,128)S(1)} %bitcast.9), custom_call_target="tpu_custom_call" | custom-call | bytes 6000000 | tf_op jit(solution)/shard_map/pack/pallas_call | solution.py:126
  3.5 0.1 collective-permute-start
  3.6 6.1 %collective-permute-start.1 = (f32[2,9,9,16,128]{4,3,2,1,0:T(8,128)S(1)}, f32[2,9,9,16,128]{4,3,2,1,0:T(8,128)}, u32[]{:S(2)}, u32[]{:S(2)}) collective-permute-start(f32[2,9,9,16,128]{4,3,2,1,0:T(8,128)S(1)} %get-tuple-element.17.ml), channel_id=1, source_target_pairs={{1,0},{2,1},{3,2},{4,3},{5,4},{6,5},{7,6},{8,7},{9,8},{10,9},{11,1... | collective-permute-start | bytes 3981320 | tf_op jit(solution)/shard_map/ppermute | solution.py:541
  9.6 0.0 copy-done.3
  9.6 0.0 copy-done.1
  9.6 0.0 copy-done.2
  9.7 1.0 %forcing.1 = f32[128,2,128]{2,1,0:T(2,128)} custom-call(f32[32,128]{1,0:T(8,128)S(1)} %bitcast.10), custom_call_target="tpu_custom_call" | custom-call | bytes 2400000 | tf_op jit(solution)/shard_map/forcing/pallas_call | solution.py:158
  10.7 6.8 %all-to-all-start = ((f32[128,2,128]{2,1,0:T(2,128)}), f32[128,2,128]{2,1,0:T(2,128)S(1)}, u32[]{:S(2)}, u32[]{:S(2)}) async-start(f32[128,2,128]{2,1,0:T(2,128)} %forcing.1), calls=%async_computation | async-start | bytes 262144 | tf_op jit(solution)/shard_map/all_to_all | solution.py:539
  17.5 0.1 turns.1.t_ref
  17.7 0.1 pad_add_fusion.at
  17.7 10.3 %all-to-all-done.win = f32[128,2,128]{2,1,0:T(2,128)S(1)} async-done(((f32[128,2,128]{2,1,0:T(2,128)}), f32[128,2,128]{2,1,0:T(2,128)S(1)}, u32[]{:S(2)}, u32[]{:S(2)}) %all-to-all-start) | async-done | bytes 131104 | tf_op jit(solution)/shard_map/all_to_all | solution.py:539
  28.1 2.7 %speeds.1 = (f32[9,8,16,128]{3,2,1,0:T(8,128)S(1)}, f32[2,8,16,128]{3,2,1,0:T(8,128)S(1)}, f32[2,8,16,128]{3,2,1,0:T(8,128)S(1)}, f32[8,16,128]{2,1,0:T(8,128)S(1)}, f32[2,16,128]{2,1,0:T(8,128)S(1)}) custom-call(s32[2]{0:T(128)S(1)} %pad_add_fusion.at, f32[128,2,128]{2,1,0:T(2,128)S(1)} %all-to-all-done.win), custom_call_target="tpu_custom_call" | custom-call | bytes 6000000 | tf_op jit(solution)/shard_map/speeds/pallas_call | solution.py:222
  30.7 0.0 collective-permute-done.lh
  30.8 0.0 collective-permute-done.1.rh
  30.8 5.3 %first_step.1 = (f32[6,9,9,16,128]{4,3,2,1,0:T(8,128)S(1)}, f32[2,2,16,128]{3,2,1,0:T(8,128)S(1)}) custom-call(s32[2]{0:T(128)S(1)} %pad_add_fusion.at, f32[2,9,9,16,128]{4,3,2,1,0:T(8,128)} %collective-permute-done.lh, f32[2,9,9,16,128]{4,3,2,1,0:T(8,128)S(1)} %get-tuple-element.17.ml, f32[2,9,9,16,128]{4,3,2,1,0:T(8,128)S(1)} %get-tuple-element.16.mr, ...), custom_call_target="tpu_custom_call" | custom-call | bytes 15000000 | tf_op jit(solution)/shard_map/first_step/pallas_call | solution.py:368
  36.1 1.6 %collective-permute-start.2 = (f32[2,2,16,128]{3,2,1,0:T(8,128)S(1)}, f32[2,2,16,128]{3,2,1,0:T(8,128)S(1)}, u32[]{:S(2)}, u32[]{:S(2)}) collective-permute-start(f32[2,2,16,128]{3,2,1,0:T(8,128)S(1)} %get-tuple-element.23.m0), channel_id=1, source_target_pairs={{0,32},{32,0},{64,96},{96,64},{1,33},{33,1},{65,97},{97,65},{2,34}... | collective-permute-start | bytes 98312 | tf_op jit(solution)/shard_map/ppermute | solution.py:523
  37.7 2.7 %collective-permute-start.3 = (f32[2,2,16,128]{3,2,1,0:T(8,128)S(1)}, f32[2,2,16,128]{3,2,1,0:T(8,128)S(1)}, u32[]{:S(2)}, u32[]{:S(2)}) collective-permute-start(f32[2,2,16,128]{3,2,1,0:T(8,128)S(1)} %get-tuple-element.23.m0), channel_id=1, source_target_pairs={{0,64},{32,96},{64,0},{96,32},{1,65},{33,97},{65,1},{97,33},{2,66}... | collective-permute-start | bytes 98312 | tf_op jit(solution)/shard_map/ppermute | solution.py:523
  40.4 0.5 collective-permute-start.4
  40.9 1.9 %second_speeds.1.c_ref = f32[9,8,16,128]{3,2,1,0:T(8,128)S(1)} custom-call(s32[2]{0:T(128)S(1)} %pad_add_fusion.at, f32[2,16,128]{2,1,0:T(8,128)S(1)} %get-tuple-element.24.h_ref), custom_call_target="tpu_custom_call" | custom-call | bytes 4500000 | tf_op jit(solution)/shard_map/second_speeds/pallas_call | solution.py:266
  42.9 0.0 collective-permute-done.2.m1
  42.9 0.2 collective-permute-done.3.m2
  43.1 2.4 %collective-permute-done.4.m3 = f32[2,2,16,128]{3,2,1,0:T(8,128)S(1)} collective-permute-done((f32[2,2,16,128]{3,2,1,0:T(8,128)S(1)}, f32[2,2,16,128]{3,2,1,0:T(8,128)S(1)}, u32[]{:S(2)}, u32[]{:S(2)}) %collective-permute-start.4) | collective-permute-done | bytes 32800 | tf_op jit(solution)/shard_map/ppermute | solution.py:523
  45.5 3.0 %second_step.1 = (f32[4,9,9,16,128]{4,3,2,1,0:T(8,128)S(1)}, f32[2,16,128]{2,1,0:T(8,128)S(1)}) custom-call(s32[2]{0:T(128)S(1)} %pad_add_fusion.at, f32[6,9,9,16,128]{4,3,2,1,0:T(8,128)S(1)} %get-tuple-element.22.e_ref, f32[2,2,16,128]{3,2,1,0:T(8,128)S(1)} %get-tuple-element.23.m0, f32[2,2,16,128]{3,2,1,0:T(8,128)S(1)} %collective-permute-done.2.m1, ...), custom_call_target="tpu_custom_call" | custom-call | bytes 10500000 | tf_op jit(solution)/shard_map/second_step/pallas_call | solution.py:437
  48.6 0.1 collective-permute-start.5
  48.7 1.9 %collective-permute-start.6 = (f32[2,16,128]{2,1,0:T(8,128)S(1)}, f32[2,16,128]{2,1,0:T(8,128)S(1)}, u32[]{:S(2)}, u32[]{:S(2)}) collective-permute-start(f32[2,16,128]{2,1,0:T(8,128)S(1)} %get-tuple-element.26.m0), channel_id=1, source_target_pairs={{0,64},{32,96},{64,0},{96,32},{1,65},{33,97},{65,1},{97,33},{2,66}... | collective-permute-start | bytes 49160 | tf_op jit(solution)/shard_map/ppermute | solution.py:523
  50.6 2.8 %collective-permute-start.7 = (f32[2,16,128]{2,1,0:T(8,128)S(1)}, f32[2,16,128]{2,1,0:T(8,128)S(1)}, u32[]{:S(2)}, u32[]{:S(2)}) collective-permute-start(f32[2,16,128]{2,1,0:T(8,128)S(1)} %get-tuple-element.26.m0), channel_id=1, source_target_pairs={{0,96},{32,64},{64,32},{96,0},{1,97},{33,65},{65,33},{97,1},{2,98}... | collective-permute-start | bytes 49160 | tf_op jit(solution)/shard_map/ppermute | solution.py:523
  53.4 1.7 %unpack.1.e_ref = f32[9,36,16,128]{3,2,1,0:T(8,128)S(1)} custom-call(f32[4,9,9,16,128]{4,3,2,1,0:T(8,128)S(1)} %get-tuple-element.25.e_ref), custom_call_target="tpu_custom_call" | custom-call | bytes 6000000 | tf_op jit(solution)/shard_map/unpack/pallas_call | solution.py:468
  55.1 0.0 collective-permute-done.5.m1
  55.1 0.0 collective-permute-done.6.m2
  55.1 0.5 collective-permute-done.7.m3
  55.6 2.2 %last_step.1 = f32[9,36,16,128]{3,2,1,0:T(8,128)} custom-call(s32[2]{0:T(128)S(1)} %pad_add_fusion.at, f32[9,36,16,128]{3,2,1,0:T(8,128)S(1)} %unpack.1.e_ref, f32[8,16,128]{2,1,0:T(8,128)S(1)} %get-tuple-element.21.w_ref, f32[2,16,128]{2,1,0:T(8,128)S(1)} %get-tuple-element.26.m0, f32[2,16,128]{2,1,0:T(8,128)S(1)} %collective-permute-done.5.m1, ...), custom_call_target="tpu_custom_call" | custom-call | bytes 4500000 | tf_op jit(solution)/shard_map/last_step/pallas_call | solution.py:501
  (2 shorter events, 0.0 us)
Async XLA Ops:
  0.0 1.7 %copy-start = (f32[16,9,36,128]{3,0,2,1:T(8,128)S(1)}, f32[16,9,36,128]{3,0,2,1:T(8,128)}, u32[]{:S(2)}) copy-start(f32[16,9,36,128]{3,0,2,1:T(8,128)} %param.4) | copy-start | bytes 7962628
  1.8 7.9 %copy-start.3 = (s32[4,128]{1,0:T(4,128)S(1)}, s32[4,128]{1,0:T(4,128)}, u32[]{:S(2)}) copy-start(s32[4,128]{1,0:T(4,128)} %param.7) | copy-start | bytes 6148
  1.8 7.9 %copy-start.1 = (f32[2,3,4,128]{3,2,1,0:T(4,128)S(1)}, f32[2,3,4,128]{3,2,1,0:T(4,128)}, u32[]{:S(2)}) copy-start(f32[2,3,4,128]{3,2,1,0:T(4,128)} %param.5) | copy-start | bytes 36868
  1.8 7.9 %copy-start.2 = (f32[4,128]{1,0:T(4,128)S(1)}, f32[4,128]{1,0:T(4,128)}, u32[]{:S(2)}) copy-start(f32[4,128]{1,0:T(4,128)} %param.6) | copy-start | bytes 6148
  3.5 27.3 %collective-permute-start = (f32[2,9,9,16,128]{4,3,2,1,0:T(8,128)S(1)}, f32[2,9,9,16,128]{4,3,2,1,0:T(8,128)}, u32[]{:S(2)}, u32[]{:S(2)}) collective-permute-start(f32[2,9,9,16,128]{4,3,2,1,0:T(8,128)S(1)} %get-tuple-element.16.mr), channel_id=1, source_target_pairs={{0,1},{1,2},{2,3},{3,4},{4,5},{5,6},{6,7},{7,8},{8,9},{9,10},{10,1... | collective-permute-start | bytes 3981320 | tf_op jit(solution)/shard_map/ppermute | solution.py:540
  3.6 27.2 %collective-permute-start.1 = (f32[2,9,9,16,128]{4,3,2,1,0:T(8,128)S(1)}, f32[2,9,9,16,128]{4,3,2,1,0:T(8,128)}, u32[]{:S(2)}, u32[]{:S(2)}) collective-permute-start(f32[2,9,9,16,128]{4,3,2,1,0:T(8,128)S(1)} %get-tuple-element.17.ml), channel_id=1, source_target_pairs={{1,0},{2,1},{3,2},{4,3},{5,4},{6,5},{7,6},{8,7},{9,8},{10,9},{11,1... | collective-permute-start | bytes 3981320 | tf_op jit(solution)/shard_map/ppermute | solution.py:541
  10.7 17.4 %all-to-all-start = ((f32[128,2,128]{2,1,0:T(2,128)}), f32[128,2,128]{2,1,0:T(2,128)S(1)}, u32[]{:S(2)}, u32[]{:S(2)}) async-start(f32[128,2,128]{2,1,0:T(2,128)} %forcing.1), calls=%async_computation | async-start | bytes 262144 | tf_op jit(solution)/shard_map/all_to_all | solution.py:539
  36.1 6.7 %collective-permute-start.2 = (f32[2,2,16,128]{3,2,1,0:T(8,128)S(1)}, f32[2,2,16,128]{3,2,1,0:T(8,128)S(1)}, u32[]{:S(2)}, u32[]{:S(2)}) collective-permute-start(f32[2,2,16,128]{3,2,1,0:T(8,128)S(1)} %get-tuple-element.23.m0), channel_id=1, source_target_pairs={{0,32},{32,0},{64,96},{96,64},{1,33},{33,1},{65,97},{97,65},{2,34}... | collective-permute-start | bytes 98312 | tf_op jit(solution)/shard_map/ppermute | solution.py:523
  37.7 5.4 %collective-permute-start.3 = (f32[2,2,16,128]{3,2,1,0:T(8,128)S(1)}, f32[2,2,16,128]{3,2,1,0:T(8,128)S(1)}, u32[]{:S(2)}, u32[]{:S(2)}) collective-permute-start(f32[2,2,16,128]{3,2,1,0:T(8,128)S(1)} %get-tuple-element.23.m0), channel_id=1, source_target_pairs={{0,64},{32,96},{64,0},{96,32},{1,65},{33,97},{65,1},{97,33},{2,66}... | collective-permute-start | bytes 98312 | tf_op jit(solution)/shard_map/ppermute | solution.py:523
  40.4 5.1 %collective-permute-start.4 = (f32[2,2,16,128]{3,2,1,0:T(8,128)S(1)}, f32[2,2,16,128]{3,2,1,0:T(8,128)S(1)}, u32[]{:S(2)}, u32[]{:S(2)}) collective-permute-start(f32[2,2,16,128]{3,2,1,0:T(8,128)S(1)} %get-tuple-element.23.m0), channel_id=1, source_target_pairs={{0,96},{32,64},{64,32},{96,0},{1,97},{33,65},{65,33},{97,1},{2,98}... | collective-permute-start | bytes 98312 | tf_op jit(solution)/shard_map/ppermute | solution.py:523
  48.6 6.5 %collective-permute-start.5 = (f32[2,16,128]{2,1,0:T(8,128)S(1)}, f32[2,16,128]{2,1,0:T(8,128)S(1)}, u32[]{:S(2)}, u32[]{:S(2)}) collective-permute-start(f32[2,16,128]{2,1,0:T(8,128)S(1)} %get-tuple-element.26.m0), channel_id=1, source_target_pairs={{0,32},{32,0},{64,96},{96,64},{1,33},{33,1},{65,97},{97,65},{2,34}... | collective-permute-start | bytes 49160 | tf_op jit(solution)/shard_map/ppermute | solution.py:523
  48.7 6.4 %collective-permute-start.6 = (f32[2,16,128]{2,1,0:T(8,128)S(1)}, f32[2,16,128]{2,1,0:T(8,128)S(1)}, u32[]{:S(2)}, u32[]{:S(2)}) collective-permute-start(f32[2,16,128]{2,1,0:T(8,128)S(1)} %get-tuple-element.26.m0), channel_id=1, source_target_pairs={{0,64},{32,96},{64,0},{96,32},{1,65},{33,97},{65,1},{97,33},{2,66}... | collective-permute-start | bytes 49160 | tf_op jit(solution)/shard_map/ppermute | solution.py:523
  50.6 4.9 %collective-permute-start.7 = (f32[2,16,128]{2,1,0:T(8,128)S(1)}, f32[2,16,128]{2,1,0:T(8,128)S(1)}, u32[]{:S(2)}, u32[]{:S(2)}) collective-permute-start(f32[2,16,128]{2,1,0:T(8,128)S(1)} %get-tuple-element.26.m0), channel_id=1, source_target_pairs={{0,96},{32,64},{64,32},{96,0},{1,97},{33,65},{65,33},{97,1},{2,98}... | collective-permute-start | bytes 49160 | tf_op jit(solution)/shard_map/ppermute | solution.py:523

commit v4 on v3

--- a/solution.py
+++ b/solution.py
@@ -109,10 +109,17 @@
         ref[lead + (pl.ds(parity, 8, stride=2), slice(None))] = value[8 * parity : 8 * parity + 8]
 
 
-def pack_kernel(e_ref, ml_ref, mr_ref):
+def pack_kernel(e_hbm, ml_ref, mr_ref, buf, sem):
+    def load(f):
+        return pltpu.make_async_copy(e_hbm.at[f], buf.at[f], sem.at[f])
+
+    for f in range(NFB):
+        load(f).start()
+
     def body(f):
+        load(f).wait()
         for d in range(NQ):
-            out = quad_transpose([load_rows(e_ref, (f, d + NQ * q)) for q in range(4)])
+            out = quad_transpose([load_rows(buf, (f, d + NQ * q)) for q in range(4)])
             ml_ref[0, f, d] = out[0]
             ml_ref[1, f, d] = out[1]
             mr_ref[0, f, d] = out[2]
@@ -125,11 +132,15 @@
     shape = jax.ShapeDtypeStruct((2, NFB, NQ, ROWS, LANES), F32)
     return pl.pallas_call(
         pack_kernel,
-        in_specs=[VM],
+        in_specs=[HB],
         out_specs=[VM, VM],
         out_shape=[shape, shape],
-        compiler_params=PARAMS,
-        cost_estimate=cost(2.0),
+        scratch_shapes=[
+            pltpu.VMEM((NFB, ND, ROWS, LANES), F32),
+            pltpu.SemaphoreType.DMA((NFB,)),
+        ],
+        compiler_params=pltpu.CompilerParams(vmem_limit_bytes=50 * 1024 * 1024),
+        cost_estimate=cost(2.5),
         name="pack",
     )(spectra)
 
@@ -172,23 +183,24 @@
 
 
 def celerities(first, h_ref, c_ref):
-    def body(f):
-        angular = (2.0 * math.pi) * frequency_of(first + f)
-        deep = angular * angular / GRAVITY
-        speed = []
-        for part in range(2):
-            height = h_ref[part]
-            wavenumber = deep / jnp.sqrt(jnp.tanh(deep * height))
-            q = 2.0 * wavenumber * height
-            ratio = 2.0 * q * jnp.exp(-q) / (1.0 - jnp.exp(-2.0 * q))
-            speed.append((0.5 * COURANT) * (1.0 + ratio) * angular / wavenumber)
-        for i, x in enumerate(spread_columns(*speed)):
-            c_ref[f, i] = x
-
-    loop(NFB, body)
-
-
-def speed_kernel(at, win, c_ref, u_ref, v_ref, w_ref, h_ref, f_scr, h_scr):
+    def body(third):
+        for f in [3 * third + k for k in range(3)]:
+            angular = (2.0 * math.pi) * frequency_of(first + f)
+            deep = angular * angular / GRAVITY
+            speed = []
+            for part in range(2):
+                height = h_ref[part]
+                wavenumber = deep / jnp.sqrt(jnp.tanh(deep * height))
+                q = 2.0 * wavenumber * height
+                ratio = 2.0 * q * jnp.exp(-q) / (1.0 - jnp.exp(-2.0 * q))
+                speed.append((0.5 * COURANT) * (1.0 + ratio) * angular / wavenumber)
+            for i, x in enumerate(spread_columns(*speed)):
+                c_ref[f, i] = x
+
+    loop(NFB // 3, body)
+
+
+def speed_kernel(at, win, after, c_ref, u_ref, v_ref, w_ref, h_ref, f_scr, h_scr):
     left, right = edge_shifts(at[1])
     shape = (PTS, LANES)
     place = lax.broadcasted_iota(jnp.int32, shape, 0)
@@ -218,10 +230,10 @@
     celerities(at[0] * NFB, h_scr, c_ref)
 
 
-def speeds(at, windows):
+def speeds(at, windows, after):
     return pl.pallas_call(
         speed_kernel,
-        in_specs=[SM, VM],
+        in_specs=[SM, VM, pl.BlockSpec(memory_space=pl.ANY)],
         out_specs=[VM] * 5,
         out_shape=[
             jax.ShapeDtypeStruct((NFB, 8, ROWS, LANES), F32),
@@ -237,7 +249,7 @@
         compiler_params=PARAMS,
         cost_estimate=cost(2.0),
         name="speeds",
-    )(at, windows)
+    )(at, windows, after)
 
 
 def turn_kernel(t_ref):
@@ -256,6 +268,38 @@
         cost_estimate=cost(0.5),
         name="turns",
     )()
+
+
+def align_kernel(at, lh, rh, lo_ref, ro_ref):
+    def shift(ref, amount):
+        def body(f):
+            for k in range(2):
+                for d in range(NQ):
+                    ref[k, f, d] = lroll(ref[k, f, d], amount)
+
+        loop(NFB, body)
+
+    @pl.when(at[1] == 0)
+    def _():
+        shift(lo_ref, 4)
+
+    @pl.when(at[1] == PTS - 1)
+    def _():
+        shift(ro_ref, -4)
+
+
+def align(at, lh, rh):
+    shape = jax.ShapeDtypeStruct((2, NFB, NQ, ROWS, LANES), F32)
+    return pl.pallas_call(
+        align_kernel,
+        in_specs=[SM, VM, VM],
+        out_specs=[VM, VM],
+        out_shape=[shape, shape],
+        input_output_aliases={1: 0, 2: 1},
+        compiler_params=PARAMS,
+        cost_estimate=cost(1.0),
+        name="align",
+    )(at, lh, rh)
 
 
 def second_speed_kernel(at, h_ref, c_ref):
@@ -322,7 +366,6 @@
 
 
 def first_kernel(at, lh, ml, mr, rh, c_ref, u_ref, v_ref, w_ref, t_ref, out_ref, mom_ref, acc):
-    left, right = edge_shifts(at[1])
     first = at[0] * NFB
     acc[...] = jnp.zeros_like(acc)
 
@@ -335,12 +378,7 @@
                 levels[i - 1] = levels[i - 1] + value
 
             def energy(i):
-                e = (lh, ml, mr, rh)[i // 2][i % 2, f, d]
-                if i < 2:
-                    e = pltpu.roll(e, left, 1)
-                if i >= 6:
-                    e = pltpu.roll(e, right, 1)
-                return e * w_ref[i]
+                return (lh, ml, mr, rh)[i // 2][i % 2, f, d] * w_ref[i]
 
             advance(
                 8,
@@ -519,9 +557,10 @@
 
 
 def band_parts(x):
-    return [x] + [
-        lax.ppermute(x, "band", [(i, i ^ k) for i in range(BANDS)]) for k in range(1, BANDS)
+    far, middle, near = [
+        lax.ppermute(x, "band", [(i, i ^ k) for i in range(BANDS)]) for k in (3, 2, 1)
     ]
+    return [x, near, middle, far]
 
 
 def per_device(spectra, currents, bathymetry, sea_mask):
@@ -540,7 +579,8 @@
     lh = lax.ppermute(mr, "pts", RIGHT)
     rh = lax.ppermute(ml, "pts", LEFT)
     turn = turns()
-    c, u, v, w, depth = speeds(at, windows)
+    lh, rh = align(at, lh, rh)
+    c, u, v, w, depth = speeds(at, windows, lh)
     e, moments = first_step(at, lh, ml, mr, rh, (c, u, v, w, turn))
     c = second_speeds(at, depth)
     e, moments = second_step(at, e, band_parts(moments), c, u, v, w, turn)

time: 58.2 us -> 56.8 us (0.976)
  Pallas kernels: 19.7 us -> 22.1 us
  local copies, waits for them, and re-layouts: 1.76 us -> 0.01 us
  starting transfers between devices: 22.5 us -> 21.3 us
  waiting for transfers between devices: 13.5 us -> 12.8 us
    all_to_all x1, waiting for transfers between devices: 10.3 us -> 0.05 us  [per_device(): windows = lax.all_to_all(windows, ('band', 'pts'), 0, 0, tiled=True)]
    ppermute x1, waiting for transfers between devices: 0.01 us -> 8.56 us  [per_device(): lh = lax.ppermute(mr, 'pts', RIGHT)]
    pallas_call x2 -> x3, Pallas kernels: 4.38 us -> 7.78 us  [the longest x1 4.34 us: pack(): pl.pallas_call(pack_kernel, in_specs=[HB], out_specs=[VM, VM], out_shape=...]
    unnamed x8 -> x6, local copies, waits for them, and re-layouts: 1.76 us -> 0.01 us
    ppermute x6, starting transfers between devices: 9.55 us -> 8.35 us  [band_parts(): lax.ppermute(x, 'band', [(i, i ^ k) for i in range(BANDS)])]
    pallas_call x1, Pallas kernels: 1.94 us -> 1.24 us  [second_speeds(): pl.pallas_call(second_speed_kernel, in_specs=[SM, VM], out_specs=VM, out_...]
  transfers between devices with their start and end apart: 9 -> 9, of which waited for: 4 -> 4; matrix products, arithmetic and copies ran while one was open for 0% -> 0% of each run, Pallas kernels for 13% -> 10%
where the time goes in v4:
time: 56.8 us; the launch traced here: 56.4 us
  Pallas kernels  22.1 us (39%)
  starting transfers between devices  21.3 us (38%)
  waiting for transfers between devices  12.8 us (23%)
    ppermute x1, waiting for transfers between devices, per_device(): lh = lax.ppermute(mr, 'pts', RIGHT)  8.56 us
    ppermute x6, starting transfers between devices, band_parts(): lax.ppermute(x, 'band', [(i, i ^ k) for i in range(BANDS)])  8.35 us
    all_to_all x1, starting transfers between devices, per_device(): windows = lax.all_to_all(windows, ('band', 'pts'), 0, 0, tiled=True)  6.8 us
    ppermute x1, starting transfers between devices, per_device(): rh = lax.ppermute(ml, 'pts', LEFT)  6.08 us
    pallas_call x1, Pallas kernels, first_step(): pl.pallas_call(first_kernel, in_specs=[SM] + [VM] * 9, out_specs=[VM] * 2...  5.01 us
    pallas_call x1, Pallas kernels, pack(): pl.pallas_call(pack_kernel, in_specs=[HB], out_specs=[VM, VM], out_shape=...  4.34 us
    ppermute x6, waiting for transfers between devices, band_parts(): lax.ppermute(x, 'band', [(i, i ^ k) for i in range(BANDS)])  3.71 us
    pallas_call x1, Pallas kernels, second_step(): pl.pallas_call(second_kernel, in_specs=[SM] + [VM] * 10, out_specs=[VM] *...  3.01 us
  transfers between devices with their start and end apart: 9, of which 4 were waited for; matrix products, arithmetic and copies ran while one was open for 0% of the time, Pallas kernels for 10%

profile of v4, /device:TPU:0, one launch (start us, length us, event | category | flops | bytes accessed | tf_op | source)
XLA Modules:
  0.0 56.4 jit_solution(5279417494543723161)
XLA Ops:
  0.0 0.0 copy-start.2
  0.0 0.0 copy-start
  0.0 0.0 copy-start.1
  0.0 4.3 %pack.1 = (f32[2,9,9,16,128]{4,3,2,1,0:T(8,128)}, f32[2,9,9,16,128]{4,3,2,1,0:T(8,128)}) custom-call(f32[9,36,16,128]{3,2,1,0:T(8,128)} %bitcast.10), custom_call_target="tpu_custom_call" | custom-call | bytes 7500000 | tf_op jit(solution)/shard_map/pack/pallas_call | solution.py:133
  4.4 0.1 collective-permute-start
  4.4 6.1 %collective-permute-start.1 = (f32[2,9,9,16,128]{4,3,2,1,0:T(8,128)}, f32[2,9,9,16,128]{4,3,2,1,0:T(8,128)S(1)}, u32[]{:S(2)}, u32[]{:S(2)}) collective-permute-start(f32[2,9,9,16,128]{4,3,2,1,0:T(8,128)} %get-tuple-element.19.ml), channel_id=1, source_target_pairs={{1,0},{2,1},{3,2},{4,3},{5,4},{6,5},{7,6},{8,7},{9,8},{10,9},{11,1... | collective-permute-start | bytes 3981320 | tf_op jit(solution)/shard_map/ppermute | solution.py:580
  10.5 0.0 copy-done.2
  10.5 0.0 copy-done
  10.5 0.0 copy-done.1
  10.5 1.0 %forcing.1 = f32[128,2,128]{2,1,0:T(2,128)} custom-call(f32[32,128]{1,0:T(8,128)S(1)} %bitcast.9), custom_call_target="tpu_custom_call" | custom-call | bytes 2400000 | tf_op jit(solution)/shard_map/forcing/pallas_call | solution.py:169
  11.6 6.8 %all-to-all-start = ((f32[128,2,128]{2,1,0:T(2,128)}), f32[128,2,128]{2,1,0:T(2,128)S(1)}, u32[]{:S(2)}, u32[]{:S(2)}) async-start(f32[128,2,128]{2,1,0:T(2,128)} %forcing.1), calls=%async_computation | async-start | bytes 262144 | tf_op jit(solution)/shard_map/all_to_all | solution.py:578
  18.4 0.1 turns.1.t_ref
  18.5 0.1 pad_add_fusion.at
  18.6 8.6 %collective-permute-done.lh = f32[2,9,9,16,128]{4,3,2,1,0:T(8,128)S(1)} collective-permute-done((f32[2,9,9,16,128]{4,3,2,1,0:T(8,128)}, f32[2,9,9,16,128]{4,3,2,1,0:T(8,128)S(1)}, u32[]{:S(2)}, u32[]{:S(2)}) %collective-permute-start) | collective-permute-done | bytes 1327136 | tf_op jit(solution)/shard_map/ppermute | solution.py:579
  27.2 0.4 collective-permute-done.1.rh
  27.6 1.5 %align.1 = (f32[2,9,9,16,128]{4,3,2,1,0:T(8,128)S(1)}, f32[2,9,9,16,128]{4,3,2,1,0:T(8,128)S(1)}) custom-call(s32[2]{0:T(128)S(1)} %pad_add_fusion.at, f32[2,9,9,16,128]{4,3,2,1,0:T(8,128)S(1)} %collective-permute-done.lh, f32[2,9,9,16,128]{4,3,2,1,0:T(8,128)S(1)} %collective-permute-done.1.rh), custom_call_target="tpu_custom_call", output_to_operand_aliasing={{0}: (1, {}), {1}: (2, {})} | custom-call | bytes 3000000 | tf_op jit(solution)/shard_map/align/pallas_call | solution.py:293
  29.1 0.1 all-to-all-done.win
  29.2 2.0 %speeds.1 = (f32[9,8,16,128]{3,2,1,0:T(8,128)S(1)}, f32[2,8,16,128]{3,2,1,0:T(8,128)S(1)}, f32[2,8,16,128]{3,2,1,0:T(8,128)S(1)}, f32[8,16,128]{2,1,0:T(8,128)S(1)}, f32[2,16,128]{2,1,0:T(8,128)S(1)}) custom-call(s32[2]{0:T(128)S(1)} %pad_add_fusion.at, f32[128,2,128]{2,1,0:T(2,128)S(1)} %all-to-all-done.win, ...), custom_call_target="tpu_custom_call" | custom-call | bytes 6000000 | tf_op jit(solution)/shard_map/speeds/pallas_call | solution.py:234
  31.1 5.0 %first_step.1 = (f32[6,9,9,16,128]{4,3,2,1,0:T(8,128)S(1)}, f32[2,2,16,128]{3,2,1,0:T(8,128)S(1)}) custom-call(s32[2]{0:T(128)S(1)} %pad_add_fusion.at, f32[2,9,9,16,128]{4,3,2,1,0:T(8,128)S(1)} %get-tuple-element.20.after.lh, f32[2,9,9,16,128]{4,3,2,1,0:T(8,128)} %get-tuple-element.19.ml, f32[2,9,9,16,128]{4,3,2,1,0:T(8,128)} %get-tuple-element.18.mr, ...), custom_call_target="tpu_custom_call" | custom-call | bytes 15000000 | tf_op jit(solution)/shard_map/first_step/pallas_call | solution.py:406
  36.1 2.9 %collective-permute-start.4 = (f32[2,2,16,128]{3,2,1,0:T(8,128)S(1)}, f32[2,2,16,128]{3,2,1,0:T(8,128)S(1)}, u32[]{:S(2)}, u32[]{:S(2)}) collective-permute-start(f32[2,2,16,128]{3,2,1,0:T(8,128)S(1)} %get-tuple-element.27.m0), channel_id=1, source_target_pairs={{0,96},{32,64},{64,32},{96,0},{1,97},{33,65},{65,33},{97,1},{2,98}... | collective-permute-start | bytes 98312 | tf_op jit(solution)/shard_map/ppermute | solution.py:561
  39.0 0.7 %collective-permute-start.3 = (f32[2,2,16,128]{3,2,1,0:T(8,128)S(1)}, f32[2,2,16,128]{3,2,1,0:T(8,128)S(1)}, u32[]{:S(2)}, u32[]{:S(2)}) collective-permute-start(f32[2,2,16,128]{3,2,1,0:T(8,128)S(1)} %get-tuple-element.27.m0), channel_id=1, source_target_pairs={{0,64},{32,96},{64,0},{96,32},{1,65},{33,97},{65,1},{97,33},{2,66}... | collective-permute-start | bytes 98312 | tf_op jit(solution)/shard_map/ppermute | solution.py:561
  39.8 0.5 collective-permute-start.2
  40.3 1.2 %second_speeds.1.c_ref = f32[9,8,16,128]{3,2,1,0:T(8,128)S(1)} custom-call(s32[2]{0:T(128)S(1)} %pad_add_fusion.at, f32[2,16,128]{2,1,0:T(8,128)S(1)} %get-tuple-element.28.h_ref), custom_call_target="tpu_custom_call" | custom-call | bytes 4500000 | tf_op jit(solution)/shard_map/second_speeds/pallas_call | solution.py:310
  41.6 0.0 collective-permute-done.4.m3
  41.6 2.9 %collective-permute-done.3.m2 = f32[2,2,16,128]{3,2,1,0:T(8,128)S(1)} collective-permute-done((f32[2,2,16,128]{3,2,1,0:T(8,128)S(1)}, f32[2,2,16,128]{3,2,1,0:T(8,128)S(1)}, u32[]{:S(2)}, u32[]{:S(2)}) %collective-permute-start.3) | collective-permute-done | bytes 32800 | tf_op jit(solution)/shard_map/ppermute | solution.py:561
  44.5 0.0 collective-permute-done.2.m1
  44.5 3.0 %second_step.1 = (f32[4,9,9,16,128]{4,3,2,1,0:T(8,128)S(1)}, f32[2,16,128]{2,1,0:T(8,128)S(1)}) custom-call(s32[2]{0:T(128)S(1)} %pad_add_fusion.at, f32[6,9,9,16,128]{4,3,2,1,0:T(8,128)S(1)} %get-tuple-element.26.e_ref, f32[2,2,16,128]{3,2,1,0:T(8,128)S(1)} %get-tuple-element.27.m0, f32[2,2,16,128]{3,2,1,0:T(8,128)S(1)} %collective-permute-done.2.m1, ...), custom_call_target="tpu_custom_call" | custom-call | bytes 10500000 | tf_op jit(solution)/shard_map/second_step/pallas_call | solution.py:475
  47.5 1.5 %collective-permute-start.7 = (f32[2,16,128]{2,1,0:T(8,128)S(1)}, f32[2,16,128]{2,1,0:T(8,128)S(1)}, u32[]{:S(2)}, u32[]{:S(2)}) collective-permute-start(f32[2,16,128]{2,1,0:T(8,128)S(1)} %get-tuple-element.30.m0), channel_id=1, source_target_pairs={{0,96},{32,64},{64,32},{96,0},{1,97},{33,65},{65,33},{97,1},{2,98}... | collective-permute-start | bytes 49160 | tf_op jit(solution)/shard_map/ppermute | solution.py:561
  48.9 1.0 %collective-permute-start.6 = (f32[2,16,128]{2,1,0:T(8,128)S(1)}, f32[2,16,128]{2,1,0:T(8,128)S(1)}, u32[]{:S(2)}, u32[]{:S(2)}) collective-permute-start(f32[2,16,128]{2,1,0:T(8,128)S(1)} %get-tuple-element.30.m0), channel_id=1, source_target_pairs={{0,64},{32,96},{64,0},{96,32},{1,65},{33,97},{65,1},{97,33},{2,66}... | collective-permute-start | bytes 49160 | tf_op jit(solution)/shard_map/ppermute | solution.py:561
  49.9 1.7 %collective-permute-start.5 = (f32[2,16,128]{2,1,0:T(8,128)S(1)}, f32[2,16,128]{2,1,0:T(8,128)S(1)}, u32[]{:S(2)}, u32[]{:S(2)}) collective-permute-start(f32[2,16,128]{2,1,0:T(8,128)S(1)} %get-tuple-element.30.m0), channel_id=1, source_target_pairs={{0,32},{32,0},{64,96},{96,64},{1,33},{33,1},{65,97},{97,65},{2,34}... | collective-permute-start | bytes 49160 | tf_op jit(solution)/shard_map/ppermute | solution.py:561
  51.7 1.7 %unpack.1.e_ref = f32[9,36,16,128]{3,2,1,0:T(8,128)S(1)} custom-call(f32[4,9,9,16,128]{4,3,2,1,0:T(8,128)S(1)} %get-tuple-element.29.e_ref), custom_call_target="tpu_custom_call" | custom-call | bytes 6000000 | tf_op jit(solution)/shard_map/unpack/pallas_call | solution.py:506
  53.4 0.0 collective-permute-done.7.m3
  53.4 0.8 %collective-permute-done.6.m2 = f32[2,16,128]{2,1,0:T(8,128)S(1)} collective-permute-done((f32[2,16,128]{2,1,0:T(8,128)S(1)}, f32[2,16,128]{2,1,0:T(8,128)S(1)}, u32[]{:S(2)}, u32[]{:S(2)}) %collective-permute-start.6) | collective-permute-done | bytes 16416 | tf_op jit(solution)/shard_map/ppermute | solution.py:561
  54.2 0.0 collective-permute-done.5.m1
  54.2 2.2 %last_step.1 = f32[9,36,16,128]{3,2,1,0:T(8,128)} custom-call(s32[2]{0:T(128)S(1)} %pad_add_fusion.at, f32[9,36,16,128]{3,2,1,0:T(8,128)S(1)} %unpack.1.e_ref, f32[8,16,128]{2,1,0:T(8,128)S(1)} %get-tuple-element.25.w_ref, f32[2,16,128]{2,1,0:T(8,128)S(1)} %get-tuple-element.30.m0, f32[2,16,128]{2,1,0:T(8,128)S(1)} %collective-permute-done.5.m1, ...), custom_call_target="tpu_custom_call" | custom-call | bytes 4500000 | tf_op jit(solution)/shard_map/last_step/pallas_call | solution.py:539
  (2 shorter events, 0.0 us)
Async XLA Ops:
  0.0 10.5 %copy-start.2 = (s32[4,128]{1,0:T(4,128)S(1)}, s32[4,128]{1,0:T(4,128)}, u32[]{:S(2)}) copy-start(s32[4,128]{1,0:T(4,128)} %param.7) | copy-start | bytes 6148
  0.0 10.5 %copy-start = (f32[2,3,4,128]{3,2,1,0:T(4,128)S(1)}, f32[2,3,4,128]{3,2,1,0:T(4,128)}, u32[]{:S(2)}) copy-start(f32[2,3,4,128]{3,2,1,0:T(4,128)} %param.5) | copy-start | bytes 36868
  0.0 10.5 %copy-start.1 = (f32[4,128]{1,0:T(4,128)S(1)}, f32[4,128]{1,0:T(4,128)}, u32[]{:S(2)}) copy-start(f32[4,128]{1,0:T(4,128)} %param.6) | copy-start | bytes 6148
  4.4 22.8 %collective-permute-start = (f32[2,9,9,16,128]{4,3,2,1,0:T(8,128)}, f32[2,9,9,16,128]{4,3,2,1,0:T(8,128)S(1)}, u32[]{:S(2)}, u32[]{:S(2)}) collective-permute-start(f32[2,9,9,16,128]{4,3,2,1,0:T(8,128)} %get-tuple-element.18.mr), channel_id=1, source_target_pairs={{0,1},{1,2},{2,3},{3,4},{4,5},{5,6},{6,7},{7,8},{8,9},{9,10},{10,1... | collective-permute-start | bytes 3981320 | tf_op jit(solution)/shard_map/ppermute | solution.py:579
  4.4 23.2 %collective-permute-start.1 = (f32[2,9,9,16,128]{4,3,2,1,0:T(8,128)}, f32[2,9,9,16,128]{4,3,2,1,0:T(8,128)S(1)}, u32[]{:S(2)}, u32[]{:S(2)}) collective-permute-start(f32[2,9,9,16,128]{4,3,2,1,0:T(8,128)} %get-tuple-element.19.ml), channel_id=1, source_target_pairs={{1,0},{2,1},{3,2},{4,3},{5,4},{6,5},{7,6},{8,7},{9,8},{10,9},{11,1... | collective-permute-start | bytes 3981320 | tf_op jit(solution)/shard_map/ppermute | solution.py:580
  11.6 17.6 %all-to-all-start = ((f32[128,2,128]{2,1,0:T(2,128)}), f32[128,2,128]{2,1,0:T(2,128)S(1)}, u32[]{:S(2)}, u32[]{:S(2)}) async-start(f32[128,2,128]{2,1,0:T(2,128)} %forcing.1), calls=%async_computation | async-start | bytes 262144 | tf_op jit(solution)/shard_map/all_to_all | solution.py:578
  36.1 5.4 %collective-permute-start.4 = (f32[2,2,16,128]{3,2,1,0:T(8,128)S(1)}, f32[2,2,16,128]{3,2,1,0:T(8,128)S(1)}, u32[]{:S(2)}, u32[]{:S(2)}) collective-permute-start(f32[2,2,16,128]{3,2,1,0:T(8,128)S(1)} %get-tuple-element.27.m0), channel_id=1, source_target_pairs={{0,96},{32,64},{64,32},{96,0},{1,97},{33,65},{65,33},{97,1},{2,98}... | collective-permute-start | bytes 98312 | tf_op jit(solution)/shard_map/ppermute | solution.py:561
  39.0 5.4 %collective-permute-start.3 = (f32[2,2,16,128]{3,2,1,0:T(8,128)S(1)}, f32[2,2,16,128]{3,2,1,0:T(8,128)S(1)}, u32[]{:S(2)}, u32[]{:S(2)}) collective-permute-start(f32[2,2,16,128]{3,2,1,0:T(8,128)S(1)} %get-tuple-element.27.m0), channel_id=1, source_target_pairs={{0,64},{32,96},{64,0},{96,32},{1,65},{33,97},{65,1},{97,33},{2,66}... | collective-permute-start | bytes 98312 | tf_op jit(solution)/shard_map/ppermute | solution.py:561
  39.8 4.7 %collective-permute-start.2 = (f32[2,2,16,128]{3,2,1,0:T(8,128)S(1)}, f32[2,2,16,128]{3,2,1,0:T(8,128)S(1)}, u32[]{:S(2)}, u32[]{:S(2)}) collective-permute-start(f32[2,2,16,128]{3,2,1,0:T(8,128)S(1)} %get-tuple-element.27.m0), channel_id=1, source_target_pairs={{0,32},{32,0},{64,96},{96,64},{1,33},{33,1},{65,97},{97,65},{2,34}... | collective-permute-start | bytes 98312 | tf_op jit(solution)/shard_map/ppermute | solution.py:561
  47.5 5.9 %collective-permute-start.7 = (f32[2,16,128]{2,1,0:T(8,128)S(1)}, f32[2,16,128]{2,1,0:T(8,128)S(1)}, u32[]{:S(2)}, u32[]{:S(2)}) collective-permute-start(f32[2,16,128]{2,1,0:T(8,128)S(1)} %get-tuple-element.30.m0), channel_id=1, source_target_pairs={{0,96},{32,64},{64,32},{96,0},{1,97},{33,65},{65,33},{97,1},{2,98}... | collective-permute-start | bytes 49160 | tf_op jit(solution)/shard_map/ppermute | solution.py:561
  48.9 5.2 %collective-permute-start.6 = (f32[2,16,128]{2,1,0:T(8,128)S(1)}, f32[2,16,128]{2,1,0:T(8,128)S(1)}, u32[]{:S(2)}, u32[]{:S(2)}) collective-permute-start(f32[2,16,128]{2,1,0:T(8,128)S(1)} %get-tuple-element.30.m0), channel_id=1, source_target_pairs={{0,64},{32,96},{64,0},{96,32},{1,65},{33,97},{65,1},{97,33},{2,66}... | collective-permute-start | bytes 49160 | tf_op jit(solution)/shard_map/ppermute | solution.py:561
  49.9 4.3 %collective-permute-start.5 = (f32[2,16,128]{2,1,0:T(8,128)S(1)}, f32[2,16,128]{2,1,0:T(8,128)S(1)}, u32[]{:S(2)}, u32[]{:S(2)}) collective-permute-start(f32[2,16,128]{2,1,0:T(8,128)S(1)} %get-tuple-element.30.m0), channel_id=1, source_target_pairs={{0,32},{32,0},{64,96},{96,64},{1,33},{33,1},{65,97},{97,65},{2,34}... | collective-permute-start | bytes 49160 | tf_op jit(solution)/shard_map/ppermute | solution.py:561

commit v5 on v4

--- a/solution.py
+++ b/solution.py
@@ -557,10 +557,10 @@
 
 
 def band_parts(x):
-    far, middle, near = [
-        lax.ppermute(x, "band", [(i, i ^ k) for i in range(BANDS)]) for k in (3, 2, 1)
+    near, middle, far = [
+        lax.ppermute(x, "band", [(i, i ^ k) for i in range(BANDS)]) for k in (1, 2, 3)
     ]
-    return [x, near, middle, far]
+    return [x, near, far, middle]
 
 
 def per_device(spectra, currents, bathymetry, sea_mask):

time: 56.8 us -> 56.5 us (level)
  transfers between devices with their start and end apart: 9 -> 9, of which waited for: 4 -> 5; matrix products, arithmetic and copies ran while one was open for 0% -> 0% of each run, Pallas kernels for 10% -> 10%
where the time goes in v5:
time: 56.5 us; the launch traced here: 56.1 us
  Pallas kernels  22.1 us (39%)
  starting transfers between devices  20.8 us (37%)
  waiting for transfers between devices  13.1 us (23%)
    ppermute x1, waiting for transfers between devices, per_device(): lh = lax.ppermute(mr, 'pts', RIGHT)  8.56 us
    ppermute x6, starting transfers between devices, band_parts(): lax.ppermute(x, 'band', [(i, i ^ k) for i in range(BANDS)])  7.81 us
    all_to_all x1, starting transfers between devices, per_device(): windows = lax.all_to_all(windows, ('band', 'pts'), 0, 0, tiled=True)  6.8 us
    ppermute x1, starting transfers between devices, per_device(): rh = lax.ppermute(ml, 'pts', LEFT)  6.08 us
    pallas_call x1, Pallas kernels, first_step(): pl.pallas_call(first_kernel, in_specs=[SM] + [VM] * 9, out_specs=[VM] * 2...  5.01 us
    pallas_call x1, Pallas kernels, pack(): pl.pallas_call(pack_kernel, in_specs=[HB], out_specs=[VM, VM], out_shape=...  4.34 us
    ppermute x6, waiting for transfers between devices, band_parts(): lax.ppermute(x, 'band', [(i, i ^ k) for i in range(BANDS)])  4 us
    pallas_call x1, Pallas kernels, second_step(): pl.pallas_call(second_kernel, in_specs=[SM] + [VM] * 10, out_specs=[VM] *...  3.01 us
  transfers between devices with their start and end apart: 9, of which 5 were waited for; matrix products, arithmetic and copies ran while one was open for 0% of the time, Pallas kernels for 10%

profile of v5, /device:TPU:0, one launch (start us, length us, event | category | flops | bytes accessed | tf_op | source)
XLA Modules:
  0.0 56.1 jit_solution(11968073885814819258)
XLA Ops:
  0.0 0.0 copy-start.2
  0.0 0.0 copy-start
  0.0 0.0 copy-start.1
  0.0 4.3 %pack.1 = (f32[2,9,9,16,128]{4,3,2,1,0:T(8,128)}, f32[2,9,9,16,128]{4,3,2,1,0:T(8,128)}) custom-call(f32[9,36,16,128]{3,2,1,0:T(8,128)} %bitcast.10), custom_call_target="tpu_custom_call" | custom-call | bytes 7500000 | tf_op jit(solution)/shard_map/pack/pallas_call | solution.py:133
  4.4 0.1 collective-permute-start
  4.4 6.1 %collective-permute-start.1 = (f32[2,9,9,16,128]{4,3,2,1,0:T(8,128)}, f32[2,9,9,16,128]{4,3,2,1,0:T(8,128)S(1)}, u32[]{:S(2)}, u32[]{:S(2)}) collective-permute-start(f32[2,9,9,16,128]{4,3,2,1,0:T(8,128)} %get-tuple-element.19.ml), channel_id=1, source_target_pairs={{1,0},{2,1},{3,2},{4,3},{5,4},{6,5},{7,6},{8,7},{9,8},{10,9},{11,1... | collective-permute-start | bytes 3981320 | tf_op jit(solution)/shard_map/ppermute | solution.py:580
  10.5 0.0 copy-done.2
  10.5 0.0 copy-done
  10.5 0.0 copy-done.1
  10.5 1.0 %forcing.1 = f32[128,2,128]{2,1,0:T(2,128)} custom-call(f32[32,128]{1,0:T(8,128)S(1)} %bitcast.9), custom_call_target="tpu_custom_call" | custom-call | bytes 2400000 | tf_op jit(solution)/shard_map/forcing/pallas_call | solution.py:169
  11.6 6.8 %all-to-all-start = ((f32[128,2,128]{2,1,0:T(2,128)}), f32[128,2,128]{2,1,0:T(2,128)S(1)}, u32[]{:S(2)}, u32[]{:S(2)}) async-start(f32[128,2,128]{2,1,0:T(2,128)} %forcing.1), calls=%async_computation | async-start | bytes 262144 | tf_op jit(solution)/shard_map/all_to_all | solution.py:578
  18.4 0.1 turns.1.t_ref
  18.5 0.1 pad_add_fusion.at
  18.6 8.6 %collective-permute-done.lh = f32[2,9,9,16,128]{4,3,2,1,0:T(8,128)S(1)} collective-permute-done((f32[2,9,9,16,128]{4,3,2,1,0:T(8,128)}, f32[2,9,9,16,128]{4,3,2,1,0:T(8,128)S(1)}, u32[]{:S(2)}, u32[]{:S(2)}) %collective-permute-start) | collective-permute-done | bytes 1327136 | tf_op jit(solution)/shard_map/ppermute | solution.py:579
  27.2 0.4 collective-permute-done.1.rh
  27.6 1.5 %align.1 = (f32[2,9,9,16,128]{4,3,2,1,0:T(8,128)S(1)}, f32[2,9,9,16,128]{4,3,2,1,0:T(8,128)S(1)}) custom-call(s32[2]{0:T(128)S(1)} %pad_add_fusion.at, f32[2,9,9,16,128]{4,3,2,1,0:T(8,128)S(1)} %collective-permute-done.lh, f32[2,9,9,16,128]{4,3,2,1,0:T(8,128)S(1)} %collective-permute-done.1.rh), custom_call_target="tpu_custom_call", output_to_operand_aliasing={{0}: (1, {}), {1}: (2, {})} | custom-call | bytes 3000000 | tf_op jit(solution)/shard_map/align/pallas_call | solution.py:293
  29.1 0.1 all-to-all-done.win
  29.2 2.0 %speeds.1 = (f32[9,8,16,128]{3,2,1,0:T(8,128)S(1)}, f32[2,8,16,128]{3,2,1,0:T(8,128)S(1)}, f32[2,8,16,128]{3,2,1,0:T(8,128)S(1)}, f32[8,16,128]{2,1,0:T(8,128)S(1)}, f32[2,16,128]{2,1,0:T(8,128)S(1)}) custom-call(s32[2]{0:T(128)S(1)} %pad_add_fusion.at, f32[128,2,128]{2,1,0:T(2,128)S(1)} %all-to-all-done.win, ...), custom_call_target="tpu_custom_call" | custom-call | bytes 6000000 | tf_op jit(solution)/shard_map/speeds/pallas_call | solution.py:234
  31.1 5.0 %first_step.1 = (f32[6,9,9,16,128]{4,3,2,1,0:T(8,128)S(1)}, f32[2,2,16,128]{3,2,1,0:T(8,128)S(1)}) custom-call(s32[2]{0:T(128)S(1)} %pad_add_fusion.at, f32[2,9,9,16,128]{4,3,2,1,0:T(8,128)S(1)} %get-tuple-element.20.after.lh, f32[2,9,9,16,128]{4,3,2,1,0:T(8,128)} %get-tuple-element.19.ml, f32[2,9,9,16,128]{4,3,2,1,0:T(8,128)} %get-tuple-element.18.mr, ...), custom_call_target="tpu_custom_call" | custom-call | bytes 15000000 | tf_op jit(solution)/shard_map/first_step/pallas_call | solution.py:406
  36.1 3.2 %collective-permute-start.4 = (f32[2,2,16,128]{3,2,1,0:T(8,128)S(1)}, f32[2,2,16,128]{3,2,1,0:T(8,128)S(1)}, u32[]{:S(2)}, u32[]{:S(2)}) collective-permute-start(f32[2,2,16,128]{3,2,1,0:T(8,128)S(1)} %get-tuple-element.27.m0), channel_id=1, source_target_pairs={{0,64},{32,96},{64,0},{96,32},{1,65},{33,97},{65,1},{97,33},{2,66}... | collective-permute-start | bytes 98312 | tf_op jit(solution)/shard_map/ppermute | solution.py:561
  39.3 1.1 %collective-permute-start.3 = (f32[2,2,16,128]{3,2,1,0:T(8,128)S(1)}, f32[2,2,16,128]{3,2,1,0:T(8,128)S(1)}, u32[]{:S(2)}, u32[]{:S(2)}) collective-permute-start(f32[2,2,16,128]{3,2,1,0:T(8,128)S(1)} %get-tuple-element.27.m0), channel_id=1, source_target_pairs={{0,96},{32,64},{64,32},{96,0},{1,97},{33,65},{65,33},{97,1},{2,98}... | collective-permute-start | bytes 98312 | tf_op jit(solution)/shard_map/ppermute | solution.py:561
  40.4 0.0 collective-permute-start.2
  40.4 1.2 %second_speeds.1.c_ref = f32[9,8,16,128]{3,2,1,0:T(8,128)S(1)} custom-call(s32[2]{0:T(128)S(1)} %pad_add_fusion.at, f32[2,16,128]{2,1,0:T(8,128)S(1)} %get-tuple-element.28.h_ref), custom_call_target="tpu_custom_call" | custom-call | bytes 4500000 | tf_op jit(solution)/shard_map/second_speeds/pallas_call | solution.py:310
  41.6 0.0 collective-permute-done.4.m3
  41.6 2.8 %collective-permute-done.3.m2 = f32[2,2,16,128]{3,2,1,0:T(8,128)S(1)} collective-permute-done((f32[2,2,16,128]{3,2,1,0:T(8,128)S(1)}, f32[2,2,16,128]{3,2,1,0:T(8,128)S(1)}, u32[]{:S(2)}, u32[]{:S(2)}) %collective-permute-start.3) | collective-permute-done | bytes 32800 | tf_op jit(solution)/shard_map/ppermute | solution.py:561
  44.4 0.0 collective-permute-done.2.m1
  44.4 3.0 %second_step.1 = (f32[4,9,9,16,128]{4,3,2,1,0:T(8,128)S(1)}, f32[2,16,128]{2,1,0:T(8,128)S(1)}) custom-call(s32[2]{0:T(128)S(1)} %pad_add_fusion.at, f32[6,9,9,16,128]{4,3,2,1,0:T(8,128)S(1)} %get-tuple-element.26.e_ref, f32[2,2,16,128]{3,2,1,0:T(8,128)S(1)} %get-tuple-element.27.m0, f32[2,2,16,128]{3,2,1,0:T(8,128)S(1)} %collective-permute-done.2.m1, ...), custom_call_target="tpu_custom_call" | custom-call | bytes 10500000 | tf_op jit(solution)/shard_map/second_step/pallas_call | solution.py:475
  47.5 1.5 %collective-permute-start.7 = (f32[2,16,128]{2,1,0:T(8,128)S(1)}, f32[2,16,128]{2,1,0:T(8,128)S(1)}, u32[]{:S(2)}, u32[]{:S(2)}) collective-permute-start(f32[2,16,128]{2,1,0:T(8,128)S(1)} %get-tuple-element.30.m0), channel_id=1, source_target_pairs={{0,64},{32,96},{64,0},{96,32},{1,65},{33,97},{65,1},{97,33},{2,66}... | collective-permute-start | bytes 49160 | tf_op jit(solution)/shard_map/ppermute | solution.py:561
  49.0 1.1 %collective-permute-start.6 = (f32[2,16,128]{2,1,0:T(8,128)S(1)}, f32[2,16,128]{2,1,0:T(8,128)S(1)}, u32[]{:S(2)}, u32[]{:S(2)}) collective-permute-start(f32[2,16,128]{2,1,0:T(8,128)S(1)} %get-tuple-element.30.m0), channel_id=1, source_target_pairs={{0,96},{32,64},{64,32},{96,0},{1,97},{33,65},{65,33},{97,1},{2,98}... | collective-permute-start | bytes 49160 | tf_op jit(solution)/shard_map/ppermute | solution.py:561
  50.1 0.9 %collective-permute-start.5 = (f32[2,16,128]{2,1,0:T(8,128)S(1)}, f32[2,16,128]{2,1,0:T(8,128)S(1)}, u32[]{:S(2)}, u32[]{:S(2)}) collective-permute-start(f32[2,16,128]{2,1,0:T(8,128)S(1)} %get-tuple-element.30.m0), channel_id=1, source_target_pairs={{0,32},{32,0},{64,96},{96,64},{1,33},{33,1},{65,97},{97,65},{2,34}... | collective-permute-start | bytes 49160 | tf_op jit(solution)/shard_map/ppermute | solution.py:561
  51.0 1.7 %unpack.1.e_ref = f32[9,36,16,128]{3,2,1,0:T(8,128)S(1)} custom-call(f32[4,9,9,16,128]{4,3,2,1,0:T(8,128)S(1)} %get-tuple-element.29.e_ref), custom_call_target="tpu_custom_call" | custom-call | bytes 6000000 | tf_op jit(solution)/shard_map/unpack/pallas_call | solution.py:506
  52.7 0.2 collective-permute-done.7.m3
  52.9 1.0 %collective-permute-done.6.m2 = f32[2,16,128]{2,1,0:T(8,128)S(1)} collective-permute-done((f32[2,16,128]{2,1,0:T(8,128)S(1)}, f32[2,16,128]{2,1,0:T(8,128)S(1)}, u32[]{:S(2)}, u32[]{:S(2)}) %collective-permute-start.6) | collective-permute-done | bytes 16416 | tf_op jit(solution)/shard_map/ppermute | solution.py:561
  53.9 0.0 collective-permute-done.5.m1
  53.9 2.2 %last_step.1 = f32[9,36,16,128]{3,2,1,0:T(8,128)} custom-call(s32[2]{0:T(128)S(1)} %pad_add_fusion.at, f32[9,36,16,128]{3,2,1,0:T(8,128)S(1)} %unpack.1.e_ref, f32[8,16,128]{2,1,0:T(8,128)S(1)} %get-tuple-element.25.w_ref, f32[2,16,128]{2,1,0:T(8,128)S(1)} %get-tuple-element.30.m0, f32[2,16,128]{2,1,0:T(8,128)S(1)} %collective-permute-done.5.m1, ...), custom_call_target="tpu_custom_call" | custom-call | bytes 4500000 | tf_op jit(solution)/shard_map/last_step/pallas_call | solution.py:539
  (2 shorter events, 0.0 us)
Async XLA Ops:
  0.0 10.5 %copy-start.2 = (s32[4,128]{1,0:T(4,128)S(1)}, s32[4,128]{1,0:T(4,128)}, u32[]{:S(2)}) copy-start(s32[4,128]{1,0:T(4,128)} %param.7) | copy-start | bytes 6148
  0.0 10.5 %copy-start = (f32[2,3,4,128]{3,2,1,0:T(4,128)S(1)}, f32[2,3,4,128]{3,2,1,0:T(4,128)}, u32[]{:S(2)}) copy-start(f32[2,3,4,128]{3,2,1,0:T(4,128)} %param.5) | copy-start | bytes 36868
  0.0 10.5 %copy-start.1 = (f32[4,128]{1,0:T(4,128)S(1)}, f32[4,128]{1,0:T(4,128)}, u32[]{:S(2)}) copy-start(f32[4,128]{1,0:T(4,128)} %param.6) | copy-start | bytes 6148
  4.4 22.8 %collective-permute-start = (f32[2,9,9,16,128]{4,3,2,1,0:T(8,128)}, f32[2,9,9,16,128]{4,3,2,1,0:T(8,128)S(1)}, u32[]{:S(2)}, u32[]{:S(2)}) collective-permute-start(f32[2,9,9,16,128]{4,3,2,1,0:T(8,128)} %get-tuple-element.18.mr), channel_id=1, source_target_pairs={{0,1},{1,2},{2,3},{3,4},{4,5},{5,6},{6,7},{7,8},{8,9},{9,10},{10,1... | collective-permute-start | bytes 3981320 | tf_op jit(solution)/shard_map/ppermute | solution.py:579
  4.4 23.2 %collective-permute-start.1 = (f32[2,9,9,16,128]{4,3,2,1,0:T(8,128)}, f32[2,9,9,16,128]{4,3,2,1,0:T(8,128)S(1)}, u32[]{:S(2)}, u32[]{:S(2)}) collective-permute-start(f32[2,9,9,16,128]{4,3,2,1,0:T(8,128)} %get-tuple-element.19.ml), channel_id=1, source_target_pairs={{1,0},{2,1},{3,2},{4,3},{5,4},{6,5},{7,6},{8,7},{9,8},{10,9},{11,1... | collective-permute-start | bytes 3981320 | tf_op jit(solution)/shard_map/ppermute | solution.py:580
  11.6 17.6 %all-to-all-start = ((f32[128,2,128]{2,1,0:T(2,128)}), f32[128,2,128]{2,1,0:T(2,128)S(1)}, u32[]{:S(2)}, u32[]{:S(2)}) async-start(f32[128,2,128]{2,1,0:T(2,128)} %forcing.1), calls=%async_computation | async-start | bytes 262144 | tf_op jit(solution)/shard_map/all_to_all | solution.py:578
  36.1 5.5 %collective-permute-start.4 = (f32[2,2,16,128]{3,2,1,0:T(8,128)S(1)}, f32[2,2,16,128]{3,2,1,0:T(8,128)S(1)}, u32[]{:S(2)}, u32[]{:S(2)}) collective-permute-start(f32[2,2,16,128]{3,2,1,0:T(8,128)S(1)} %get-tuple-element.27.m0), channel_id=1, source_target_pairs={{0,64},{32,96},{64,0},{96,32},{1,65},{33,97},{65,1},{97,33},{2,66}... | collective-permute-start | bytes 98312 | tf_op jit(solution)/shard_map/ppermute | solution.py:561
  39.3 5.1 %collective-permute-start.3 = (f32[2,2,16,128]{3,2,1,0:T(8,128)S(1)}, f32[2,2,16,128]{3,2,1,0:T(8,128)S(1)}, u32[]{:S(2)}, u32[]{:S(2)}) collective-permute-start(f32[2,2,16,128]{3,2,1,0:T(8,128)S(1)} %get-tuple-element.27.m0), channel_id=1, source_target_pairs={{0,96},{32,64},{64,32},{96,0},{1,97},{33,65},{65,33},{97,1},{2,98}... | collective-permute-start | bytes 98312 | tf_op jit(solution)/shard_map/ppermute | solution.py:561
  40.4 4.0 %collective-permute-start.2 = (f32[2,2,16,128]{3,2,1,0:T(8,128)S(1)}, f32[2,2,16,128]{3,2,1,0:T(8,128)S(1)}, u32[]{:S(2)}, u32[]{:S(2)}) collective-permute-start(f32[2,2,16,128]{3,2,1,0:T(8,128)S(1)} %get-tuple-element.27.m0), channel_id=1, source_target_pairs={{0,32},{32,0},{64,96},{96,64},{1,33},{33,1},{65,97},{97,65},{2,34}... | collective-permute-start | bytes 98312 | tf_op jit(solution)/shard_map/ppermute | solution.py:561
  47.5 5.5 %collective-permute-start.7 = (f32[2,16,128]{2,1,0:T(8,128)S(1)}, f32[2,16,128]{2,1,0:T(8,128)S(1)}, u32[]{:S(2)}, u32[]{:S(2)}) collective-permute-start(f32[2,16,128]{2,1,0:T(8,128)S(1)} %get-tuple-element.30.m0), channel_id=1, source_target_pairs={{0,64},{32,96},{64,0},{96,32},{1,65},{33,97},{65,1},{97,33},{2,66}... | collective-permute-start | bytes 49160 | tf_op jit(solution)/shard_map/ppermute | solution.py:561
  49.0 4.9 %collective-permute-start.6 = (f32[2,16,128]{2,1,0:T(8,128)S(1)}, f32[2,16,128]{2,1,0:T(8,128)S(1)}, u32[]{:S(2)}, u32[]{:S(2)}) collective-permute-start(f32[2,16,128]{2,1,0:T(8,128)S(1)} %get-tuple-element.30.m0), channel_id=1, source_target_pairs={{0,96},{32,64},{64,32},{96,0},{1,97},{33,65},{65,33},{97,1},{2,98}... | collective-permute-start | bytes 49160 | tf_op jit(solution)/shard_map/ppermute | solution.py:561
  50.1 3.9 %collective-permute-start.5 = (f32[2,16,128]{2,1,0:T(8,128)S(1)}, f32[2,16,128]{2,1,0:T(8,128)S(1)}, u32[]{:S(2)}, u32[]{:S(2)}) collective-permute-start(f32[2,16,128]{2,1,0:T(8,128)S(1)} %get-tuple-element.30.m0), channel_id=1, source_target_pairs={{0,32},{32,0},{64,96},{96,64},{1,33},{33,1},{65,97},{97,65},{2,34}... | collective-permute-start | bytes 49160 | tf_op jit(solution)/shard_map/ppermute | solution.py:561

commit v6 on v5

--- a/solution.py
+++ b/solution.py
@@ -139,7 +139,7 @@
             pltpu.VMEM((NFB, ND, ROWS, LANES), F32),
             pltpu.SemaphoreType.DMA((NFB,)),
         ],
-        compiler_params=pltpu.CompilerParams(vmem_limit_bytes=50 * 1024 * 1024),
+        compiler_params=pltpu.CompilerParams(vmem_limit_bytes=52 * 1024 * 1024),
         cost_estimate=cost(2.5),
         name="pack",
     )(spectra)
@@ -183,21 +183,18 @@
 
 
 def celerities(first, h_ref, c_ref):
-    def body(third):
-        for f in [3 * third + k for k in range(3)]:
-            angular = (2.0 * math.pi) * frequency_of(first + f)
-            deep = angular * angular / GRAVITY
-            speed = []
-            for part in range(2):
-                height = h_ref[part]
-                wavenumber = deep / jnp.sqrt(jnp.tanh(deep * height))
-                q = 2.0 * wavenumber * height
-                ratio = 2.0 * q * jnp.exp(-q) / (1.0 - jnp.exp(-2.0 * q))
-                speed.append((0.5 * COURANT) * (1.0 + ratio) * angular / wavenumber)
-            for i, x in enumerate(spread_columns(*speed)):
-                c_ref[f, i] = x
-
-    loop(NFB // 3, body)
+    for f in range(NFB):
+        angular = (2.0 * math.pi) * frequency_of(first + f)
+        deep = angular * angular / GRAVITY
+        speed = []
+        for part in range(2):
+            height = h_ref[part]
+            wavenumber = deep / jnp.sqrt(jnp.tanh(deep * height))
+            q = 2.0 * wavenumber * height
+            ratio = 2.0 * q * jnp.exp(-q) / (1.0 - jnp.exp(-2.0 * q))
+            speed.append((0.5 * COURANT) * (1.0 + ratio) * angular / wavenumber)
+        for i, x in enumerate(spread_columns(*speed)):
+            c_ref[f, i] = x
 
 
 def speed_kernel(at, win, after, c_ref, u_ref, v_ref, w_ref, h_ref, f_scr, h_scr):

time: 56.5 us -> 55.8 us (0.988)
  Pallas kernels: 22.1 us -> 21.1 us
  transfers between devices with their start and end apart: 9 -> 9, of which waited for: 5 -> 6; matrix products, arithmetic and copies ran while one was open for 0% -> 0% of each run, Pallas kernels for 10% -> 10%
where the time goes in v6:
time: 55.8 us; the launch traced here: 55.4 us
  Pallas kernels  21.1 us (38%)
  starting transfers between devices  20.8 us (37%)
  waiting for transfers between devices  13.3 us (24%)
    ppermute x1, waiting for transfers between devices, per_device(): lh = lax.ppermute(mr, 'pts', RIGHT)  8.57 us
    ppermute x6, starting transfers between devices, band_parts(): lax.ppermute(x, 'band', [(i, i ^ k) for i in range(BANDS)])  7.82 us
    all_to_all x1, starting transfers between devices, per_device(): windows = lax.all_to_all(windows, ('band', 'pts'), 0, 0, tiled=True)  6.8 us
    ppermute x1, starting transfers between devices, per_device(): rh = lax.ppermute(ml, 'pts', LEFT)  6.08 us
    pallas_call x1, Pallas kernels, first_step(): pl.pallas_call(first_kernel, in_specs=[SM] + [VM] * 9, out_specs=[VM] * 2...  4.57 us
    pallas_call x1, Pallas kernels, pack(): pl.pallas_call(pack_kernel, in_specs=[HB], out_specs=[VM, VM], out_shape=...  4.33 us
    ppermute x6, waiting for transfers between devices, band_parts(): lax.ppermute(x, 'band', [(i, i ^ k) for i in range(BANDS)])  4.24 us
    pallas_call x1, Pallas kernels, second_step(): pl.pallas_call(second_kernel, in_specs=[SM] + [VM] * 10, out_specs=[VM] *...  3.03 us
  transfers between devices with their start and end apart: 9, of which 6 were waited for; matrix products, arithmetic and copies ran while one was open for 0% of the time, Pallas kernels for 10%

profile of v6, /device:TPU:0, one launch (start us, length us, event | category | flops | bytes accessed | tf_op | source)
XLA Modules:
  0.0 55.4 jit_solution(8407816990433136974)
XLA Ops:
  0.0 0.0 copy-start.3
  0.0 0.0 copy-start.1
  0.0 0.0 copy-start.2
  0.0 4.3 %pack.1 = (f32[2,9,9,16,128]{4,3,2,1,0:T(8,128)}, f32[2,9,9,16,128]{4,3,2,1,0:T(8,128)}) custom-call(f32[9,36,16,128]{3,2,1,0:T(8,128)} %bitcast.10), custom_call_target="tpu_custom_call" | custom-call | bytes 7500000 | tf_op jit(solution)/shard_map/pack/pallas_call | solution.py:133
  4.3 0.1 collective-permute-start
  4.4 6.1 %collective-permute-start.1 = (f32[2,9,9,16,128]{4,3,2,1,0:T(8,128)}, f32[2,9,9,16,128]{4,3,2,1,0:T(8,128)S(1)}, u32[]{:S(2)}, u32[]{:S(2)}) collective-permute-start(f32[2,9,9,16,128]{4,3,2,1,0:T(8,128)} %get-tuple-element.19.ml), channel_id=1, source_target_pairs={{1,0},{2,1},{3,2},{4,3},{5,4},{6,5},{7,6},{8,7},{9,8},{10,9},{11,1... | collective-permute-start | bytes 3981320 | tf_op jit(solution)/shard_map/ppermute | solution.py:577
  10.5 0.0 copy-done.3
  10.5 0.0 copy-done.1
  10.5 0.0 copy-done.2
  10.5 1.0 %forcing.1 = f32[128,2,128]{2,1,0:T(2,128)} custom-call(f32[32,128]{1,0:T(8,128)S(1)} %bitcast.9), custom_call_target="tpu_custom_call" | custom-call | bytes 2400000 | tf_op jit(solution)/shard_map/forcing/pallas_call | solution.py:169
  11.6 6.8 %all-to-all-start = ((f32[128,2,128]{2,1,0:T(2,128)}), f32[128,2,128]{2,1,0:T(2,128)S(1)}, u32[]{:S(2)}, u32[]{:S(2)}) async-start(f32[128,2,128]{2,1,0:T(2,128)} %forcing.1), calls=%async_computation | async-start | bytes 262144 | tf_op jit(solution)/shard_map/all_to_all | solution.py:575
  18.4 0.1 turns.1.t_ref
  18.5 0.1 pad_add_fusion.at
  18.6 8.6 %collective-permute-done.lh = f32[2,9,9,16,128]{4,3,2,1,0:T(8,128)S(1)} collective-permute-done((f32[2,9,9,16,128]{4,3,2,1,0:T(8,128)}, f32[2,9,9,16,128]{4,3,2,1,0:T(8,128)S(1)}, u32[]{:S(2)}, u32[]{:S(2)}) %collective-permute-start) | collective-permute-done | bytes 1327136 | tf_op jit(solution)/shard_map/ppermute | solution.py:576
  27.2 0.4 collective-permute-done.1.rh
  27.6 1.5 %align.1 = (f32[2,9,9,16,128]{4,3,2,1,0:T(8,128)S(1)}, f32[2,9,9,16,128]{4,3,2,1,0:T(8,128)S(1)}) custom-call(s32[2]{0:T(128)S(1)} %pad_add_fusion.at, f32[2,9,9,16,128]{4,3,2,1,0:T(8,128)S(1)} %collective-permute-done.lh, f32[2,9,9,16,128]{4,3,2,1,0:T(8,128)S(1)} %collective-permute-done.1.rh), custom_call_target="tpu_custom_call", output_to_operand_aliasing={{0}: (1, {}), {1}: (2, {})} | custom-call | bytes 3000000 | tf_op jit(solution)/shard_map/align/pallas_call | solution.py:290
  29.1 0.1 all-to-all-done.win
  29.2 0.0 copy-start
  29.2 1.7 %speeds.1 = (f32[9,8,16,128]{3,2,1,0:T(8,128)S(1)}, f32[2,8,16,128]{3,2,1,0:T(8,128)S(1)}, f32[2,8,16,128]{3,2,1,0:T(8,128)S(1)}, f32[8,16,128]{2,1,0:T(8,128)S(1)}, f32[2,16,128]{2,1,0:T(8,128)S(1)}) custom-call(s32[2]{0:T(128)S(1)} %pad_add_fusion.at, f32[128,2,128]{2,1,0:T(2,128)S(1)} %all-to-all-done.win, ...), custom_call_target="tpu_custom_call" | custom-call | bytes 6000000 | tf_op jit(solution)/shard_map/speeds/pallas_call | solution.py:231
  30.8 0.0 copy-done
  30.8 4.6 %first_step.1 = (f32[6,9,9,16,128]{4,3,2,1,0:T(8,128)S(1)}, f32[2,2,16,128]{3,2,1,0:T(8,128)S(1)}) custom-call(s32[2]{0:T(128)S(1)} %pad_add_fusion.at, f32[2,9,9,16,128]{4,3,2,1,0:T(8,128)S(1)} %get-tuple-element.20.after.lh, f32[2,9,9,16,128]{4,3,2,1,0:T(8,128)} %get-tuple-element.19.ml, f32[2,9,9,16,128]{4,3,2,1,0:T(8,128)S(1)} %copy-done, ...), custom_call_target="tpu_custom_call" | custom-call | bytes 15000000 | tf_op jit(solution)/shard_map/first_step/pallas_call | solution.py:403
  35.4 3.2 %collective-permute-start.4 = (f32[2,2,16,128]{3,2,1,0:T(8,128)S(1)}, f32[2,2,16,128]{3,2,1,0:T(8,128)S(1)}, u32[]{:S(2)}, u32[]{:S(2)}) collective-permute-start(f32[2,2,16,128]{3,2,1,0:T(8,128)S(1)} %get-tuple-element.27.m0), channel_id=1, source_target_pairs={{0,64},{32,96},{64,0},{96,32},{1,65},{33,97},{65,1},{97,33},{2,66}... | collective-permute-start | bytes 98312 | tf_op jit(solution)/shard_map/ppermute | solution.py:558
  38.6 1.1 %collective-permute-start.3 = (f32[2,2,16,128]{3,2,1,0:T(8,128)S(1)}, f32[2,2,16,128]{3,2,1,0:T(8,128)S(1)}, u32[]{:S(2)}, u32[]{:S(2)}) collective-permute-start(f32[2,2,16,128]{3,2,1,0:T(8,128)S(1)} %get-tuple-element.27.m0), channel_id=1, source_target_pairs={{0,96},{32,64},{64,32},{96,0},{1,97},{33,65},{65,33},{97,1},{2,98}... | collective-permute-start | bytes 98312 | tf_op jit(solution)/shard_map/ppermute | solution.py:558
  39.6 0.0 collective-permute-start.2
  39.7 1.0 %second_speeds.1.c_ref = f32[9,8,16,128]{3,2,1,0:T(8,128)S(1)} custom-call(s32[2]{0:T(128)S(1)} %pad_add_fusion.at, f32[2,16,128]{2,1,0:T(8,128)S(1)} %get-tuple-element.28.h_ref), custom_call_target="tpu_custom_call" | custom-call | bytes 4500000 | tf_op jit(solution)/shard_map/second_speeds/pallas_call | solution.py:307
  40.7 0.2 collective-permute-done.4.m3
  40.9 2.8 %collective-permute-done.3.m2 = f32[2,2,16,128]{3,2,1,0:T(8,128)S(1)} collective-permute-done((f32[2,2,16,128]{3,2,1,0:T(8,128)S(1)}, f32[2,2,16,128]{3,2,1,0:T(8,128)S(1)}, u32[]{:S(2)}, u32[]{:S(2)}) %collective-permute-start.3) | collective-permute-done | bytes 32800 | tf_op jit(solution)/shard_map/ppermute | solution.py:558
  43.7 0.0 collective-permute-done.2.m1
  43.7 3.0 %second_step.1 = (f32[4,9,9,16,128]{4,3,2,1,0:T(8,128)S(1)}, f32[2,16,128]{2,1,0:T(8,128)S(1)}) custom-call(s32[2]{0:T(128)S(1)} %pad_add_fusion.at, f32[6,9,9,16,128]{4,3,2,1,0:T(8,128)S(1)} %get-tuple-element.26.e_ref, f32[2,2,16,128]{3,2,1,0:T(8,128)S(1)} %get-tuple-element.27.m0, f32[2,2,16,128]{3,2,1,0:T(8,128)S(1)} %collective-permute-done.2.m1, ...), custom_call_target="tpu_custom_call" | custom-call | bytes 10500000 | tf_op jit(solution)/shard_map/second_step/pallas_call | solution.py:472
  46.7 1.5 %collective-permute-start.7 = (f32[2,16,128]{2,1,0:T(8,128)S(1)}, f32[2,16,128]{2,1,0:T(8,128)S(1)}, u32[]{:S(2)}, u32[]{:S(2)}) collective-permute-start(f32[2,16,128]{2,1,0:T(8,128)S(1)} %get-tuple-element.30.m0), channel_id=1, source_target_pairs={{0,64},{32,96},{64,0},{96,32},{1,65},{33,97},{65,1},{97,33},{2,66}... | collective-permute-start | bytes 49160 | tf_op jit(solution)/shard_map/ppermute | solution.py:558
  48.3 1.1 %collective-permute-start.6 = (f32[2,16,128]{2,1,0:T(8,128)S(1)}, f32[2,16,128]{2,1,0:T(8,128)S(1)}, u32[]{:S(2)}, u32[]{:S(2)}) collective-permute-start(f32[2,16,128]{2,1,0:T(8,128)S(1)} %get-tuple-element.30.m0), channel_id=1, source_target_pairs={{0,96},{32,64},{64,32},{96,0},{1,97},{33,65},{65,33},{97,1},{2,98}... | collective-permute-start | bytes 49160 | tf_op jit(solution)/shard_map/ppermute | solution.py:558
  49.4 0.9 %collective-permute-start.5 = (f32[2,16,128]{2,1,0:T(8,128)S(1)}, f32[2,16,128]{2,1,0:T(8,128)S(1)}, u32[]{:S(2)}, u32[]{:S(2)}) collective-permute-start(f32[2,16,128]{2,1,0:T(8,128)S(1)} %get-tuple-element.30.m0), channel_id=1, source_target_pairs={{0,32},{32,0},{64,96},{96,64},{1,33},{33,1},{65,97},{97,65},{2,34}... | collective-permute-start | bytes 49160 | tf_op jit(solution)/shard_map/ppermute | solution.py:558
  50.3 1.7 %unpack.1.e_ref = f32[9,36,16,128]{3,2,1,0:T(8,128)S(1)} custom-call(f32[4,9,9,16,128]{4,3,2,1,0:T(8,128)S(1)} %get-tuple-element.29.e_ref), custom_call_target="tpu_custom_call" | custom-call | bytes 6000000 | tf_op jit(solution)/shard_map/unpack/pallas_call | solution.py:503
  52.0 0.2 collective-permute-done.7.m3
  52.2 1.0 %collective-permute-done.6.m2 = f32[2,16,128]{2,1,0:T(8,128)S(1)} collective-permute-done((f32[2,16,128]{2,1,0:T(8,128)S(1)}, f32[2,16,128]{2,1,0:T(8,128)S(1)}, u32[]{:S(2)}, u32[]{:S(2)}) %collective-permute-start.6) | collective-permute-done | bytes 16416 | tf_op jit(solution)/shard_map/ppermute | solution.py:558
  53.2 0.0 collective-permute-done.5.m1
  53.2 2.2 %last_step.1 = f32[9,36,16,128]{3,2,1,0:T(8,128)} custom-call(s32[2]{0:T(128)S(1)} %pad_add_fusion.at, f32[9,36,16,128]{3,2,1,0:T(8,128)S(1)} %unpack.1.e_ref, f32[8,16,128]{2,1,0:T(8,128)S(1)} %get-tuple-element.25.w_ref, f32[2,16,128]{2,1,0:T(8,128)S(1)} %get-tuple-element.30.m0, f32[2,16,128]{2,1,0:T(8,128)S(1)} %collective-permute-done.5.m1, ...), custom_call_target="tpu_custom_call" | custom-call | bytes 4500000 | tf_op jit(solution)/shard_map/last_step/pallas_call | solution.py:536
  (2 shorter events, 0.0 us)
Async XLA Ops:
  0.0 10.5 %copy-start.3 = (s32[4,128]{1,0:T(4,128)S(1)}, s32[4,128]{1,0:T(4,128)}, u32[]{:S(2)}) copy-start(s32[4,128]{1,0:T(4,128)} %param.7) | copy-start | bytes 6148
  0.0 10.5 %copy-start.1 = (f32[2,3,4,128]{3,2,1,0:T(4,128)S(1)}, f32[2,3,4,128]{3,2,1,0:T(4,128)}, u32[]{:S(2)}) copy-start(f32[2,3,4,128]{3,2,1,0:T(4,128)} %param.5) | copy-start | bytes 36868
  0.0 10.5 %copy-start.2 = (f32[4,128]{1,0:T(4,128)S(1)}, f32[4,128]{1,0:T(4,128)}, u32[]{:S(2)}) copy-start(f32[4,128]{1,0:T(4,128)} %param.6) | copy-start | bytes 6148
  4.3 22.8 %collective-permute-start = (f32[2,9,9,16,128]{4,3,2,1,0:T(8,128)}, f32[2,9,9,16,128]{4,3,2,1,0:T(8,128)S(1)}, u32[]{:S(2)}, u32[]{:S(2)}) collective-permute-start(f32[2,9,9,16,128]{4,3,2,1,0:T(8,128)} %get-tuple-element.18.mr), channel_id=1, source_target_pairs={{0,1},{1,2},{2,3},{3,4},{4,5},{5,6},{6,7},{7,8},{8,9},{9,10},{10,1... | collective-permute-start | bytes 3981320 | tf_op jit(solution)/shard_map/ppermute | solution.py:576
  4.4 23.2 %collective-permute-start.1 = (f32[2,9,9,16,128]{4,3,2,1,0:T(8,128)}, f32[2,9,9,16,128]{4,3,2,1,0:T(8,128)S(1)}, u32[]{:S(2)}, u32[]{:S(2)}) collective-permute-start(f32[2,9,9,16,128]{4,3,2,1,0:T(8,128)} %get-tuple-element.19.ml), channel_id=1, source_target_pairs={{1,0},{2,1},{3,2},{4,3},{5,4},{6,5},{7,6},{8,7},{9,8},{10,9},{11,1... | collective-permute-start | bytes 3981320 | tf_op jit(solution)/shard_map/ppermute | solution.py:577
  11.6 17.6 %all-to-all-start = ((f32[128,2,128]{2,1,0:T(2,128)}), f32[128,2,128]{2,1,0:T(2,128)S(1)}, u32[]{:S(2)}, u32[]{:S(2)}) async-start(f32[128,2,128]{2,1,0:T(2,128)} %forcing.1), calls=%async_computation | async-start | bytes 262144 | tf_op jit(solution)/shard_map/all_to_all | solution.py:575
  29.2 1.7 %copy-start = (f32[2,9,9,16,128]{4,3,2,1,0:T(8,128)S(1)}, f32[2,9,9,16,128]{4,3,2,1,0:T(8,128)}, u32[]{:S(2)}) copy-start(f32[2,9,9,16,128]{4,3,2,1,0:T(8,128)} %get-tuple-element.18.mr) | copy-start | bytes 3981316
  35.4 5.5 %collective-permute-start.4 = (f32[2,2,16,128]{3,2,1,0:T(8,128)S(1)}, f32[2,2,16,128]{3,2,1,0:T(8,128)S(1)}, u32[]{:S(2)}, u32[]{:S(2)}) collective-permute-start(f32[2,2,16,128]{3,2,1,0:T(8,128)S(1)} %get-tuple-element.27.m0), channel_id=1, source_target_pairs={{0,64},{32,96},{64,0},{96,32},{1,65},{33,97},{65,1},{97,33},{2,66}... | collective-permute-start | bytes 98312 | tf_op jit(solution)/shard_map/ppermute | solution.py:558
  38.6 5.1 %collective-permute-start.3 = (f32[2,2,16,128]{3,2,1,0:T(8,128)S(1)}, f32[2,2,16,128]{3,2,1,0:T(8,128)S(1)}, u32[]{:S(2)}, u32[]{:S(2)}) collective-permute-start(f32[2,2,16,128]{3,2,1,0:T(8,128)S(1)} %get-tuple-element.27.m0), channel_id=1, source_target_pairs={{0,96},{32,64},{64,32},{96,0},{1,97},{33,65},{65,33},{97,1},{2,98}... | collective-permute-start | bytes 98312 | tf_op jit(solution)/shard_map/ppermute | solution.py:558
  39.6 4.0 %collective-permute-start.2 = (f32[2,2,16,128]{3,2,1,0:T(8,128)S(1)}, f32[2,2,16,128]{3,2,1,0:T(8,128)S(1)}, u32[]{:S(2)}, u32[]{:S(2)}) collective-permute-start(f32[2,2,16,128]{3,2,1,0:T(8,128)S(1)} %get-tuple-element.27.m0), channel_id=1, source_target_pairs={{0,32},{32,0},{64,96},{96,64},{1,33},{33,1},{65,97},{97,65},{2,34}... | collective-permute-start | bytes 98312 | tf_op jit(solution)/shard_map/ppermute | solution.py:558
  46.7 5.5 %collective-permute-start.7 = (f32[2,16,128]{2,1,0:T(8,128)S(1)}, f32[2,16,128]{2,1,0:T(8,128)S(1)}, u32[]{:S(2)}, u32[]{:S(2)}) collective-permute-start(f32[2,16,128]{2,1,0:T(8,128)S(1)} %get-tuple-element.30.m0), channel_id=1, source_target_pairs={{0,64},{32,96},{64,0},{96,32},{1,65},{33,97},{65,1},{97,33},{2,66}... | collective-permute-start | bytes 49160 | tf_op jit(solution)/shard_map/ppermute | solution.py:558
  48.3 4.9 %collective-permute-start.6 = (f32[2,16,128]{2,1,0:T(8,128)S(1)}, f32[2,16,128]{2,1,0:T(8,128)S(1)}, u32[]{:S(2)}, u32[]{:S(2)}) collective-permute-start(f32[2,16,128]{2,1,0:T(8,128)S(1)} %get-tuple-element.30.m0), channel_id=1, source_target_pairs={{0,96},{32,64},{64,32},{96,0},{1,97},{33,65},{65,33},{97,1},{2,98}... | collective-permute-start | bytes 49160 | tf_op jit(solution)/shard_map/ppermute | solution.py:558
  49.4 3.9 %collective-permute-start.5 = (f32[2,16,128]{2,1,0:T(8,128)S(1)}, f32[2,16,128]{2,1,0:T(8,128)S(1)}, u32[]{:S(2)}, u32[]{:S(2)}) collective-permute-start(f32[2,16,128]{2,1,0:T(8,128)S(1)} %get-tuple-element.30.m0), channel_id=1, source_target_pairs={{0,32},{32,0},{64,96},{96,64},{1,33},{33,1},{65,97},{97,65},{2,34}... | collective-permute-start | bytes 49160 | tf_op jit(solution)/shard_map/ppermute | solution.py:558

commit v7 on v6

--- a/solution.py
+++ b/solution.py
@@ -110,14 +110,17 @@
 
 
 def pack_kernel(e_hbm, ml_ref, mr_ref, buf, sem):
-    def load(f):
-        return pltpu.make_async_copy(e_hbm.at[f], buf.at[f], sem.at[f])
+    def load(f, h):
+        part = pl.ds(18 * h, 18)
+        return pltpu.make_async_copy(e_hbm.at[f, part], buf.at[f, part], sem.at[f, h])
 
     for f in range(NFB):
-        load(f).start()
+        load(f, 0).start()
+        load(f, 1).start()
 
     def body(f):
-        load(f).wait()
+        load(f, 0).wait()
+        load(f, 1).wait()
         for d in range(NQ):
             out = quad_transpose([load_rows(buf, (f, d + NQ * q)) for q in range(4)])
             ml_ref[0, f, d] = out[0]
@@ -137,7 +140,7 @@
         out_shape=[shape, shape],
         scratch_shapes=[
             pltpu.VMEM((NFB, ND, ROWS, LANES), F32),
-            pltpu.SemaphoreType.DMA((NFB,)),
+            pltpu.SemaphoreType.DMA((NFB, 2)),
         ],
         compiler_params=pltpu.CompilerParams(vmem_limit_bytes=52 * 1024 * 1024),
         cost_estimate=cost(2.5),

time: 55.8 us -> 55.9 us (level)
  no operation moved by 1% of the time
where the time goes in v7:
time: 55.9 us; the launch traced here: 55.5 us
  Pallas kernels  21.2 us (38%)
  starting transfers between devices  20.8 us (37%)
  waiting for transfers between devices  13.3 us (24%)
    ppermute x1, waiting for transfers between devices, per_device(): lh = lax.ppermute(mr, 'pts', RIGHT)  8.57 us
    ppermute x6, starting transfers between devices, band_parts(): lax.ppermute(x, 'band', [(i, i ^ k) for i in range(BANDS)])  7.82 us
    all_to_all x1, starting transfers between devices, per_device(): windows = lax.all_to_all(windows, ('band', 'pts'), 0, 0, tiled=True)  6.8 us
    ppermute x1, starting transfers between devices, per_device(): rh = lax.ppermute(ml, 'pts', LEFT)  6.08 us
    pallas_call x1, Pallas kernels, first_step(): pl.pallas_call(first_kernel, in_specs=[SM] + [VM] * 9, out_specs=[VM] * 2...  4.57 us
    pallas_call x1, Pallas kernels, pack(): pl.pallas_call(pack_kernel, in_specs=[HB], out_specs=[VM, VM], out_shape=...  4.44 us
    ppermute x6, waiting for transfers between devices, band_parts(): lax.ppermute(x, 'band', [(i, i ^ k) for i in range(BANDS)])  4.24 us
    pallas_call x1, Pallas kernels, second_step(): pl.pallas_call(second_kernel, in_specs=[SM] + [VM] * 10, out_specs=[VM] *...  3.03 us
  transfers between devices with their start and end apart: 9, of which 6 were waited for; matrix products, arithmetic and copies ran while one was open for 0% of the time, Pallas kernels for 10%

profile of v7, /device:TPU:0, one launch (start us, length us, event | category | flops | bytes accessed | tf_op | source)
XLA Modules:
  0.0 55.5 jit_solution(18057584041953378077)
XLA Ops:
  0.0 0.0 copy-start.3
  0.0 0.0 copy-start.1
  0.0 0.0 copy-start.2
  0.0 4.4 %pack.1 = (f32[2,9,9,16,128]{4,3,2,1,0:T(8,128)}, f32[2,9,9,16,128]{4,3,2,1,0:T(8,128)}) custom-call(f32[9,36,16,128]{3,2,1,0:T(8,128)} %bitcast.10), custom_call_target="tpu_custom_call" | custom-call | bytes 7500000 | tf_op jit(solution)/shard_map/pack/pallas_call | solution.py:136
  4.5 0.1 collective-permute-start
  4.5 6.1 %collective-permute-start.1 = (f32[2,9,9,16,128]{4,3,2,1,0:T(8,128)}, f32[2,9,9,16,128]{4,3,2,1,0:T(8,128)S(1)}, u32[]{:S(2)}, u32[]{:S(2)}) collective-permute-start(f32[2,9,9,16,128]{4,3,2,1,0:T(8,128)} %get-tuple-element.19.ml), channel_id=1, source_target_pairs={{1,0},{2,1},{3,2},{4,3},{5,4},{6,5},{7,6},{8,7},{9,8},{10,9},{11,1... | collective-permute-start | bytes 3981320 | tf_op jit(solution)/shard_map/ppermute | solution.py:580
  10.6 0.0 copy-done.3
  10.6 0.0 copy-done.1
  10.6 0.0 copy-done.2
  10.6 1.0 %forcing.1 = f32[128,2,128]{2,1,0:T(2,128)} custom-call(f32[32,128]{1,0:T(8,128)S(1)} %bitcast.9), custom_call_target="tpu_custom_call" | custom-call | bytes 2400000 | tf_op jit(solution)/shard_map/forcing/pallas_call | solution.py:172
  11.7 6.8 %all-to-all-start = ((f32[128,2,128]{2,1,0:T(2,128)}), f32[128,2,128]{2,1,0:T(2,128)S(1)}, u32[]{:S(2)}, u32[]{:S(2)}) async-start(f32[128,2,128]{2,1,0:T(2,128)} %forcing.1), calls=%async_computation | async-start | bytes 262144 | tf_op jit(solution)/shard_map/all_to_all | solution.py:578
  18.5 0.1 turns.1.t_ref
  18.6 0.1 pad_add_fusion.at
  18.7 8.6 %collective-permute-done.lh = f32[2,9,9,16,128]{4,3,2,1,0:T(8,128)S(1)} collective-permute-done((f32[2,9,9,16,128]{4,3,2,1,0:T(8,128)}, f32[2,9,9,16,128]{4,3,2,1,0:T(8,128)S(1)}, u32[]{:S(2)}, u32[]{:S(2)}) %collective-permute-start) | collective-permute-done | bytes 1327136 | tf_op jit(solution)/shard_map/ppermute | solution.py:579
  27.3 0.4 collective-permute-done.1.rh
  27.7 1.5 %align.1 = (f32[2,9,9,16,128]{4,3,2,1,0:T(8,128)S(1)}, f32[2,9,9,16,128]{4,3,2,1,0:T(8,128)S(1)}) custom-call(s32[2]{0:T(128)S(1)} %pad_add_fusion.at, f32[2,9,9,16,128]{4,3,2,1,0:T(8,128)S(1)} %collective-permute-done.lh, f32[2,9,9,16,128]{4,3,2,1,0:T(8,128)S(1)} %collective-permute-done.1.rh), custom_call_target="tpu_custom_call", output_to_operand_aliasing={{0}: (1, {}), {1}: (2, {})} | custom-call | bytes 3000000 | tf_op jit(solution)/shard_map/align/pallas_call | solution.py:293
  29.2 0.1 all-to-all-done.win
  29.3 0.0 copy-start
  29.3 1.7 %speeds.1 = (f32[9,8,16,128]{3,2,1,0:T(8,128)S(1)}, f32[2,8,16,128]{3,2,1,0:T(8,128)S(1)}, f32[2,8,16,128]{3,2,1,0:T(8,128)S(1)}, f32[8,16,128]{2,1,0:T(8,128)S(1)}, f32[2,16,128]{2,1,0:T(8,128)S(1)}) custom-call(s32[2]{0:T(128)S(1)} %pad_add_fusion.at, f32[128,2,128]{2,1,0:T(2,128)S(1)} %all-to-all-done.win, ...), custom_call_target="tpu_custom_call" | custom-call | bytes 6000000 | tf_op jit(solution)/shard_map/speeds/pallas_call | solution.py:234
  30.9 0.0 copy-done
  30.9 4.6 %first_step.1 = (f32[6,9,9,16,128]{4,3,2,1,0:T(8,128)S(1)}, f32[2,2,16,128]{3,2,1,0:T(8,128)S(1)}) custom-call(s32[2]{0:T(128)S(1)} %pad_add_fusion.at, f32[2,9,9,16,128]{4,3,2,1,0:T(8,128)S(1)} %get-tuple-element.20.after.lh, f32[2,9,9,16,128]{4,3,2,1,0:T(8,128)} %get-tuple-element.19.ml, f32[2,9,9,16,128]{4,3,2,1,0:T(8,128)S(1)} %copy-done, ...), custom_call_target="tpu_custom_call" | custom-call | bytes 15000000 | tf_op jit(solution)/shard_map/first_step/pallas_call | solution.py:406
  35.5 3.2 %collective-permute-start.4 = (f32[2,2,16,128]{3,2,1,0:T(8,128)S(1)}, f32[2,2,16,128]{3,2,1,0:T(8,128)S(1)}, u32[]{:S(2)}, u32[]{:S(2)}) collective-permute-start(f32[2,2,16,128]{3,2,1,0:T(8,128)S(1)} %get-tuple-element.27.m0), channel_id=1, source_target_pairs={{0,64},{32,96},{64,0},{96,32},{1,65},{33,97},{65,1},{97,33},{2,66}... | collective-permute-start | bytes 98312 | tf_op jit(solution)/shard_map/ppermute | solution.py:561
  38.7 1.1 %collective-permute-start.3 = (f32[2,2,16,128]{3,2,1,0:T(8,128)S(1)}, f32[2,2,16,128]{3,2,1,0:T(8,128)S(1)}, u32[]{:S(2)}, u32[]{:S(2)}) collective-permute-start(f32[2,2,16,128]{3,2,1,0:T(8,128)S(1)} %get-tuple-element.27.m0), channel_id=1, source_target_pairs={{0,96},{32,64},{64,32},{96,0},{1,97},{33,65},{65,33},{97,1},{2,98}... | collective-permute-start | bytes 98312 | tf_op jit(solution)/shard_map/ppermute | solution.py:561
  39.8 0.0 collective-permute-start.2
  39.8 1.0 %second_speeds.1.c_ref = f32[9,8,16,128]{3,2,1,0:T(8,128)S(1)} custom-call(s32[2]{0:T(128)S(1)} %pad_add_fusion.at, f32[2,16,128]{2,1,0:T(8,128)S(1)} %get-tuple-element.28.h_ref), custom_call_target="tpu_custom_call" | custom-call | bytes 4500000 | tf_op jit(solution)/shard_map/second_speeds/pallas_call | solution.py:310
  40.8 0.2 collective-permute-done.4.m3
  41.0 2.8 %collective-permute-done.3.m2 = f32[2,2,16,128]{3,2,1,0:T(8,128)S(1)} collective-permute-done((f32[2,2,16,128]{3,2,1,0:T(8,128)S(1)}, f32[2,2,16,128]{3,2,1,0:T(8,128)S(1)}, u32[]{:S(2)}, u32[]{:S(2)}) %collective-permute-start.3) | collective-permute-done | bytes 32800 | tf_op jit(solution)/shard_map/ppermute | solution.py:561
  43.8 0.0 collective-permute-done.2.m1
  43.8 3.0 %second_step.1 = (f32[4,9,9,16,128]{4,3,2,1,0:T(8,128)S(1)}, f32[2,16,128]{2,1,0:T(8,128)S(1)}) custom-call(s32[2]{0:T(128)S(1)} %pad_add_fusion.at, f32[6,9,9,16,128]{4,3,2,1,0:T(8,128)S(1)} %get-tuple-element.26.e_ref, f32[2,2,16,128]{3,2,1,0:T(8,128)S(1)} %get-tuple-element.27.m0, f32[2,2,16,128]{3,2,1,0:T(8,128)S(1)} %collective-permute-done.2.m1, ...), custom_call_target="tpu_custom_call" | custom-call | bytes 10500000 | tf_op jit(solution)/shard_map/second_step/pallas_call | solution.py:475
  46.8 1.5 %collective-permute-start.7 = (f32[2,16,128]{2,1,0:T(8,128)S(1)}, f32[2,16,128]{2,1,0:T(8,128)S(1)}, u32[]{:S(2)}, u32[]{:S(2)}) collective-permute-start(f32[2,16,128]{2,1,0:T(8,128)S(1)} %get-tuple-element.30.m0), channel_id=1, source_target_pairs={{0,64},{32,96},{64,0},{96,32},{1,65},{33,97},{65,1},{97,33},{2,66}... | collective-permute-start | bytes 49160 | tf_op jit(solution)/shard_map/ppermute | solution.py:561
  48.4 1.1 %collective-permute-start.6 = (f32[2,16,128]{2,1,0:T(8,128)S(1)}, f32[2,16,128]{2,1,0:T(8,128)S(1)}, u32[]{:S(2)}, u32[]{:S(2)}) collective-permute-start(f32[2,16,128]{2,1,0:T(8,128)S(1)} %get-tuple-element.30.m0), channel_id=1, source_target_pairs={{0,96},{32,64},{64,32},{96,0},{1,97},{33,65},{65,33},{97,1},{2,98}... | collective-permute-start | bytes 49160 | tf_op jit(solution)/shard_map/ppermute | solution.py:561
  49.5 0.9 %collective-permute-start.5 = (f32[2,16,128]{2,1,0:T(8,128)S(1)}, f32[2,16,128]{2,1,0:T(8,128)S(1)}, u32[]{:S(2)}, u32[]{:S(2)}) collective-permute-start(f32[2,16,128]{2,1,0:T(8,128)S(1)} %get-tuple-element.30.m0), channel_id=1, source_target_pairs={{0,32},{32,0},{64,96},{96,64},{1,33},{33,1},{65,97},{97,65},{2,34}... | collective-permute-start | bytes 49160 | tf_op jit(solution)/shard_map/ppermute | solution.py:561
  50.4 1.7 %unpack.1.e_ref = f32[9,36,16,128]{3,2,1,0:T(8,128)S(1)} custom-call(f32[4,9,9,16,128]{4,3,2,1,0:T(8,128)S(1)} %get-tuple-element.29.e_ref), custom_call_target="tpu_custom_call" | custom-call | bytes 6000000 | tf_op jit(solution)/shard_map/unpack/pallas_call | solution.py:506
  52.1 0.2 collective-permute-done.7.m3
  52.3 1.0 %collective-permute-done.6.m2 = f32[2,16,128]{2,1,0:T(8,128)S(1)} collective-permute-done((f32[2,16,128]{2,1,0:T(8,128)S(1)}, f32[2,16,128]{2,1,0:T(8,128)S(1)}, u32[]{:S(2)}, u32[]{:S(2)}) %collective-permute-start.6) | collective-permute-done | bytes 16416 | tf_op jit(solution)/shard_map/ppermute | solution.py:561
  53.3 0.0 collective-permute-done.5.m1
  53.3 2.2 %last_step.1 = f32[9,36,16,128]{3,2,1,0:T(8,128)} custom-call(s32[2]{0:T(128)S(1)} %pad_add_fusion.at, f32[9,36,16,128]{3,2,1,0:T(8,128)S(1)} %unpack.1.e_ref, f32[8,16,128]{2,1,0:T(8,128)S(1)} %get-tuple-element.25.w_ref, f32[2,16,128]{2,1,0:T(8,128)S(1)} %get-tuple-element.30.m0, f32[2,16,128]{2,1,0:T(8,128)S(1)} %collective-permute-done.5.m1, ...), custom_call_target="tpu_custom_call" | custom-call | bytes 4500000 | tf_op jit(solution)/shard_map/last_step/pallas_call | solution.py:539
  (2 shorter events, 0.0 us)
Async XLA Ops:
  0.0 10.6 %copy-start.3 = (s32[4,128]{1,0:T(4,128)S(1)}, s32[4,128]{1,0:T(4,128)}, u32[]{:S(2)}) copy-start(s32[4,128]{1,0:T(4,128)} %param.7) | copy-start | bytes 6148
  0.0 10.6 %copy-start.1 = (f32[2,3,4,128]{3,2,1,0:T(4,128)S(1)}, f32[2,3,4,128]{3,2,1,0:T(4,128)}, u32[]{:S(2)}) copy-start(f32[2,3,4,128]{3,2,1,0:T(4,128)} %param.5) | copy-start | bytes 36868
  0.0 10.6 %copy-start.2 = (f32[4,128]{1,0:T(4,128)S(1)}, f32[4,128]{1,0:T(4,128)}, u32[]{:S(2)}) copy-start(f32[4,128]{1,0:T(4,128)} %param.6) | copy-start | bytes 6148
  4.5 22.8 %collective-permute-start = (f32[2,9,9,16,128]{4,3,2,1,0:T(8,128)}, f32[2,9,9,16,128]{4,3,2,1,0:T(8,128)S(1)}, u32[]{:S(2)}, u32[]{:S(2)}) collective-permute-start(f32[2,9,9,16,128]{4,3,2,1,0:T(8,128)} %get-tuple-element.18.mr), channel_id=1, source_target_pairs={{0,1},{1,2},{2,3},{3,4},{4,5},{5,6},{6,7},{7,8},{8,9},{9,10},{10,1... | collective-permute-start | bytes 3981320 | tf_op jit(solution)/shard_map/ppermute | solution.py:579
  4.5 23.2 %collective-permute-start.1 = (f32[2,9,9,16,128]{4,3,2,1,0:T(8,128)}, f32[2,9,9,16,128]{4,3,2,1,0:T(8,128)S(1)}, u32[]{:S(2)}, u32[]{:S(2)}) collective-permute-start(f32[2,9,9,16,128]{4,3,2,1,0:T(8,128)} %get-tuple-element.19.ml), channel_id=1, source_target_pairs={{1,0},{2,1},{3,2},{4,3},{5,4},{6,5},{7,6},{8,7},{9,8},{10,9},{11,1... | collective-permute-start | bytes 3981320 | tf_op jit(solution)/shard_map/ppermute | solution.py:580
  11.7 17.6 %all-to-all-start = ((f32[128,2,128]{2,1,0:T(2,128)}), f32[128,2,128]{2,1,0:T(2,128)S(1)}, u32[]{:S(2)}, u32[]{:S(2)}) async-start(f32[128,2,128]{2,1,0:T(2,128)} %forcing.1), calls=%async_computation | async-start | bytes 262144 | tf_op jit(solution)/shard_map/all_to_all | solution.py:578
  29.3 1.7 %copy-start = (f32[2,9,9,16,128]{4,3,2,1,0:T(8,128)S(1)}, f32[2,9,9,16,128]{4,3,2,1,0:T(8,128)}, u32[]{:S(2)}) copy-start(f32[2,9,9,16,128]{4,3,2,1,0:T(8,128)} %get-tuple-element.18.mr) | copy-start | bytes 3981316
  35.5 5.5 %collective-permute-start.4 = (f32[2,2,16,128]{3,2,1,0:T(8,128)S(1)}, f32[2,2,16,128]{3,2,1,0:T(8,128)S(1)}, u32[]{:S(2)}, u32[]{:S(2)}) collective-permute-start(f32[2,2,16,128]{3,2,1,0:T(8,128)S(1)} %get-tuple-element.27.m0), channel_id=1, source_target_pairs={{0,64},{32,96},{64,0},{96,32},{1,65},{33,97},{65,1},{97,33},{2,66}... | collective-permute-start | bytes 98312 | tf_op jit(solution)/shard_map/ppermute | solution.py:561
  38.7 5.1 %collective-permute-start.3 = (f32[2,2,16,128]{3,2,1,0:T(8,128)S(1)}, f32[2,2,16,128]{3,2,1,0:T(8,128)S(1)}, u32[]{:S(2)}, u32[]{:S(2)}) collective-permute-start(f32[2,2,16,128]{3,2,1,0:T(8,128)S(1)} %get-tuple-element.27.m0), channel_id=1, source_target_pairs={{0,96},{32,64},{64,32},{96,0},{1,97},{33,65},{65,33},{97,1},{2,98}... | collective-permute-start | bytes 98312 | tf_op jit(solution)/shard_map/ppermute | solution.py:561
  39.8 4.0 %collective-permute-start.2 = (f32[2,2,16,128]{3,2,1,0:T(8,128)S(1)}, f32[2,2,16,128]{3,2,1,0:T(8,128)S(1)}, u32[]{:S(2)}, u32[]{:S(2)}) collective-permute-start(f32[2,2,16,128]{3,2,1,0:T(8,128)S(1)} %get-tuple-element.27.m0), channel_id=1, source_target_pairs={{0,32},{32,0},{64,96},{96,64},{1,33},{33,1},{65,97},{97,65},{2,34}... | collective-permute-start | bytes 98312 | tf_op jit(solution)/shard_map/ppermute | solution.py:561
  46.8 5.5 %collective-permute-start.7 = (f32[2,16,128]{2,1,0:T(8,128)S(1)}, f32[2,16,128]{2,1,0:T(8,128)S(1)}, u32[]{:S(2)}, u32[]{:S(2)}) collective-permute-start(f32[2,16,128]{2,1,0:T(8,128)S(1)} %get-tuple-element.30.m0), channel_id=1, source_target_pairs={{0,64},{32,96},{64,0},{96,32},{1,65},{33,97},{65,1},{97,33},{2,66}... | collective-permute-start | bytes 49160 | tf_op jit(solution)/shard_map/ppermute | solution.py:561
  48.4 4.9 %collective-permute-start.6 = (f32[2,16,128]{2,1,0:T(8,128)S(1)}, f32[2,16,128]{2,1,0:T(8,128)S(1)}, u32[]{:S(2)}, u32[]{:S(2)}) collective-permute-start(f32[2,16,128]{2,1,0:T(8,128)S(1)} %get-tuple-element.30.m0), channel_id=1, source_target_pairs={{0,96},{32,64},{64,32},{96,0},{1,97},{33,65},{65,33},{97,1},{2,98}... | collective-permute-start | bytes 49160 | tf_op jit(solution)/shard_map/ppermute | solution.py:561
  49.5 3.9 %collective-permute-start.5 = (f32[2,16,128]{2,1,0:T(8,128)S(1)}, f32[2,16,128]{2,1,0:T(8,128)S(1)}, u32[]{:S(2)}, u32[]{:S(2)}) collective-permute-start(f32[2,16,128]{2,1,0:T(8,128)S(1)} %get-tuple-element.30.m0), channel_id=1, source_target_pairs={{0,32},{32,0},{64,96},{96,64},{1,33},{33,1},{65,97},{97,65},{2,34}... | collective-permute-start | bytes 49160 | tf_op jit(solution)/shard_map/ppermute | solution.py:561

commit v8 on v6

--- a/solution.py
+++ b/solution.py
@@ -24,7 +24,7 @@
 FIELDS = 8
 LANES = 128
 F32 = jnp.float32
-VMEM_LIMIT = 40 * 1024 * 1024
+VMEM_LIMIT = 24 * 1024 * 1024
 VM = pl.BlockSpec(memory_space=pltpu.VMEM)
 SM = pl.BlockSpec(memory_space=pltpu.SMEM)
 HB = pl.BlockSpec(memory_space=pltpu.HBM)

time: 55.8 us -> 55.8 us (level)
  no operation moved by 1% of the time
where the time goes in v8:
time: 55.8 us; the launch traced here: 55.4 us
  Pallas kernels  21.1 us (38%)
  starting transfers between devices  20.8 us (37%)
  waiting for transfers between devices  13.3 us (24%)
    ppermute x1, waiting for transfers between devices, per_device(): lh = lax.ppermute(mr, 'pts', RIGHT)  8.57 us
    ppermute x6, starting transfers between devices, band_parts(): lax.ppermute(x, 'band', [(i, i ^ k) for i in range(BANDS)])  7.82 us
    all_to_all x1, starting transfers between devices, per_device(): windows = lax.all_to_all(windows, ('band', 'pts'), 0, 0, tiled=True)  6.8 us
    ppermute x1, starting transfers between devices, per_device(): rh = lax.ppermute(ml, 'pts', LEFT)  6.08 us
    pallas_call x1, Pallas kernels, first_step(): pl.pallas_call(first_kernel, in_specs=[SM] + [VM] * 9, out_specs=[VM] * 2...  4.57 us
    pallas_call x1, Pallas kernels, pack(): pl.pallas_call(pack_kernel, in_specs=[HB], out_specs=[VM, VM], out_shape=...  4.33 us
    ppermute x6, waiting for transfers between devices, band_parts(): lax.ppermute(x, 'band', [(i, i ^ k) for i in range(BANDS)])  4.24 us
    pallas_call x1, Pallas kernels, second_step(): pl.pallas_call(second_kernel, in_specs=[SM] + [VM] * 10, out_specs=[VM] *...  3.03 us
  transfers between devices with their start and end apart: 9, of which 6 were waited for; matrix products, arithmetic and copies ran while one was open for 0% of the time, Pallas kernels for 10%

profile of v8, /device:TPU:0, one launch (start us, length us, event | category | flops | bytes accessed | tf_op | source)
XLA Modules:
  0.0 55.4 jit_solution(7148453939263049808)
XLA Ops:
  0.0 0.0 copy-start.3
  0.0 0.0 copy-start.1
  0.0 0.0 copy-start.2
  0.0 4.3 %pack.1 = (f32[2,9,9,16,128]{4,3,2,1,0:T(8,128)}, f32[2,9,9,16,128]{4,3,2,1,0:T(8,128)}) custom-call(f32[9,36,16,128]{3,2,1,0:T(8,128)} %bitcast.10), custom_call_target="tpu_custom_call" | custom-call | bytes 7500000 | tf_op jit(solution)/shard_map/pack/pallas_call | solution.py:133
  4.3 0.1 collective-permute-start
  4.4 6.1 %collective-permute-start.1 = (f32[2,9,9,16,128]{4,3,2,1,0:T(8,128)}, f32[2,9,9,16,128]{4,3,2,1,0:T(8,128)S(1)}, u32[]{:S(2)}, u32[]{:S(2)}) collective-permute-start(f32[2,9,9,16,128]{4,3,2,1,0:T(8,128)} %get-tuple-element.19.ml), channel_id=1, source_target_pairs={{1,0},{2,1},{3,2},{4,3},{5,4},{6,5},{7,6},{8,7},{9,8},{10,9},{11,1... | collective-permute-start | bytes 3981320 | tf_op jit(solution)/shard_map/ppermute | solution.py:577
  10.5 0.0 copy-done.3
  10.5 0.0 copy-done.1
  10.5 0.0 copy-done.2
  10.5 1.0 %forcing.1 = f32[128,2,128]{2,1,0:T(2,128)} custom-call(f32[32,128]{1,0:T(8,128)S(1)} %bitcast.9), custom_call_target="tpu_custom_call" | custom-call | bytes 2400000 | tf_op jit(solution)/shard_map/forcing/pallas_call | solution.py:169
  11.6 6.8 %all-to-all-start = ((f32[128,2,128]{2,1,0:T(2,128)}), f32[128,2,128]{2,1,0:T(2,128)S(1)}, u32[]{:S(2)}, u32[]{:S(2)}) async-start(f32[128,2,128]{2,1,0:T(2,128)} %forcing.1), calls=%async_computation | async-start | bytes 262144 | tf_op jit(solution)/shard_map/all_to_all | solution.py:575
  18.4 0.1 turns.1.t_ref
  18.5 0.1 pad_add_fusion.at
  18.6 8.6 %collective-permute-done.lh = f32[2,9,9,16,128]{4,3,2,1,0:T(8,128)S(1)} collective-permute-done((f32[2,9,9,16,128]{4,3,2,1,0:T(8,128)}, f32[2,9,9,16,128]{4,3,2,1,0:T(8,128)S(1)}, u32[]{:S(2)}, u32[]{:S(2)}) %collective-permute-start) | collective-permute-done | bytes 1327136 | tf_op jit(solution)/shard_map/ppermute | solution.py:576
  27.2 0.4 collective-permute-done.1.rh
  27.6 1.5 %align.1 = (f32[2,9,9,16,128]{4,3,2,1,0:T(8,128)S(1)}, f32[2,9,9,16,128]{4,3,2,1,0:T(8,128)S(1)}) custom-call(s32[2]{0:T(128)S(1)} %pad_add_fusion.at, f32[2,9,9,16,128]{4,3,2,1,0:T(8,128)S(1)} %collective-permute-done.lh, f32[2,9,9,16,128]{4,3,2,1,0:T(8,128)S(1)} %collective-permute-done.1.rh), custom_call_target="tpu_custom_call", output_to_operand_aliasing={{0}: (1, {}), {1}: (2, {})} | custom-call | bytes 3000000 | tf_op jit(solution)/shard_map/align/pallas_call | solution.py:290
  29.1 0.1 all-to-all-done.win
  29.2 0.0 copy-start
  29.2 1.7 %speeds.1 = (f32[9,8,16,128]{3,2,1,0:T(8,128)S(1)}, f32[2,8,16,128]{3,2,1,0:T(8,128)S(1)}, f32[2,8,16,128]{3,2,1,0:T(8,128)S(1)}, f32[8,16,128]{2,1,0:T(8,128)S(1)}, f32[2,16,128]{2,1,0:T(8,128)S(1)}) custom-call(s32[2]{0:T(128)S(1)} %pad_add_fusion.at, f32[128,2,128]{2,1,0:T(2,128)S(1)} %all-to-all-done.win, ...), custom_call_target="tpu_custom_call" | custom-call | bytes 6000000 | tf_op jit(solution)/shard_map/speeds/pallas_call | solution.py:231
  30.8 0.0 copy-done
  30.8 4.6 %first_step.1 = (f32[6,9,9,16,128]{4,3,2,1,0:T(8,128)S(1)}, f32[2,2,16,128]{3,2,1,0:T(8,128)S(1)}) custom-call(s32[2]{0:T(128)S(1)} %pad_add_fusion.at, f32[2,9,9,16,128]{4,3,2,1,0:T(8,128)S(1)} %get-tuple-element.20.after.lh, f32[2,9,9,16,128]{4,3,2,1,0:T(8,128)} %get-tuple-element.19.ml, f32[2,9,9,16,128]{4,3,2,1,0:T(8,128)S(1)} %copy-done, ...), custom_call_target="tpu_custom_call" | custom-call | bytes 15000000 | tf_op jit(solution)/shard_map/first_step/pallas_call | solution.py:403
  35.4 3.2 %collective-permute-start.4 = (f32[2,2,16,128]{3,2,1,0:T(8,128)S(1)}, f32[2,2,16,128]{3,2,1,0:T(8,128)S(1)}, u32[]{:S(2)}, u32[]{:S(2)}) collective-permute-start(f32[2,2,16,128]{3,2,1,0:T(8,128)S(1)} %get-tuple-element.27.m0), channel_id=1, source_target_pairs={{0,64},{32,96},{64,0},{96,32},{1,65},{33,97},{65,1},{97,33},{2,66}... | collective-permute-start | bytes 98312 | tf_op jit(solution)/shard_map/ppermute | solution.py:558
  38.6 1.1 %collective-permute-start.3 = (f32[2,2,16,128]{3,2,1,0:T(8,128)S(1)}, f32[2,2,16,128]{3,2,1,0:T(8,128)S(1)}, u32[]{:S(2)}, u32[]{:S(2)}) collective-permute-start(f32[2,2,16,128]{3,2,1,0:T(8,128)S(1)} %get-tuple-element.27.m0), channel_id=1, source_target_pairs={{0,96},{32,64},{64,32},{96,0},{1,97},{33,65},{65,33},{97,1},{2,98}... | collective-permute-start | bytes 98312 | tf_op jit(solution)/shard_map/ppermute | solution.py:558
  39.6 0.0 collective-permute-start.2
  39.7 1.0 %second_speeds.1.c_ref = f32[9,8,16,128]{3,2,1,0:T(8,128)S(1)} custom-call(s32[2]{0:T(128)S(1)} %pad_add_fusion.at, f32[2,16,128]{2,1,0:T(8,128)S(1)} %get-tuple-element.28.h_ref), custom_call_target="tpu_custom_call" | custom-call | bytes 4500000 | tf_op jit(solution)/shard_map/second_speeds/pallas_call | solution.py:307
  40.7 0.2 collective-permute-done.4.m3
  40.9 2.8 %collective-permute-done.3.m2 = f32[2,2,16,128]{3,2,1,0:T(8,128)S(1)} collective-permute-done((f32[2,2,16,128]{3,2,1,0:T(8,128)S(1)}, f32[2,2,16,128]{3,2,1,0:T(8,128)S(1)}, u32[]{:S(2)}, u32[]{:S(2)}) %collective-permute-start.3) | collective-permute-done | bytes 32800 | tf_op jit(solution)/shard_map/ppermute | solution.py:558
  43.7 0.0 collective-permute-done.2.m1
  43.7 3.0 %second_step.1 = (f32[4,9,9,16,128]{4,3,2,1,0:T(8,128)S(1)}, f32[2,16,128]{2,1,0:T(8,128)S(1)}) custom-call(s32[2]{0:T(128)S(1)} %pad_add_fusion.at, f32[6,9,9,16,128]{4,3,2,1,0:T(8,128)S(1)} %get-tuple-element.26.e_ref, f32[2,2,16,128]{3,2,1,0:T(8,128)S(1)} %get-tuple-element.27.m0, f32[2,2,16,128]{3,2,1,0:T(8,128)S(1)} %collective-permute-done.2.m1, ...), custom_call_target="tpu_custom_call" | custom-call | bytes 10500000 | tf_op jit(solution)/shard_map/second_step/pallas_call | solution.py:472
  46.7 1.5 %collective-permute-start.7 = (f32[2,16,128]{2,1,0:T(8,128)S(1)}, f32[2,16,128]{2,1,0:T(8,128)S(1)}, u32[]{:S(2)}, u32[]{:S(2)}) collective-permute-start(f32[2,16,128]{2,1,0:T(8,128)S(1)} %get-tuple-element.30.m0), channel_id=1, source_target_pairs={{0,64},{32,96},{64,0},{96,32},{1,65},{33,97},{65,1},{97,33},{2,66}... | collective-permute-start | bytes 49160 | tf_op jit(solution)/shard_map/ppermute | solution.py:558
  48.3 1.1 %collective-permute-start.6 = (f32[2,16,128]{2,1,0:T(8,128)S(1)}, f32[2,16,128]{2,1,0:T(8,128)S(1)}, u32[]{:S(2)}, u32[]{:S(2)}) collective-permute-start(f32[2,16,128]{2,1,0:T(8,128)S(1)} %get-tuple-element.30.m0), channel_id=1, source_target_pairs={{0,96},{32,64},{64,32},{96,0},{1,97},{33,65},{65,33},{97,1},{2,98}... | collective-permute-start | bytes 49160 | tf_op jit(solution)/shard_map/ppermute | solution.py:558
  49.4 0.9 %collective-permute-start.5 = (f32[2,16,128]{2,1,0:T(8,128)S(1)}, f32[2,16,128]{2,1,0:T(8,128)S(1)}, u32[]{:S(2)}, u32[]{:S(2)}) collective-permute-start(f32[2,16,128]{2,1,0:T(8,128)S(1)} %get-tuple-element.30.m0), channel_id=1, source_target_pairs={{0,32},{32,0},{64,96},{96,64},{1,33},{33,1},{65,97},{97,65},{2,34}... | collective-permute-start | bytes 49160 | tf_op jit(solution)/shard_map/ppermute | solution.py:558
  50.3 1.7 %unpack.1.e_ref = f32[9,36,16,128]{3,2,1,0:T(8,128)S(1)} custom-call(f32[4,9,9,16,128]{4,3,2,1,0:T(8,128)S(1)} %get-tuple-element.29.e_ref), custom_call_target="tpu_custom_call" | custom-call | bytes 6000000 | tf_op jit(solution)/shard_map/unpack/pallas_call | solution.py:503
  52.0 0.2 collective-permute-done.7.m3
  52.2 1.0 %collective-permute-done.6.m2 = f32[2,16,128]{2,1,0:T(8,128)S(1)} collective-permute-done((f32[2,16,128]{2,1,0:T(8,128)S(1)}, f32[2,16,128]{2,1,0:T(8,128)S(1)}, u32[]{:S(2)}, u32[]{:S(2)}) %collective-permute-start.6) | collective-permute-done | bytes 16416 | tf_op jit(solution)/shard_map/ppermute | solution.py:558
  53.2 0.0 collective-permute-done.5.m1
  53.2 2.2 %last_step.1 = f32[9,36,16,128]{3,2,1,0:T(8,128)} custom-call(s32[2]{0:T(128)S(1)} %pad_add_fusion.at, f32[9,36,16,128]{3,2,1,0:T(8,128)S(1)} %unpack.1.e_ref, f32[8,16,128]{2,1,0:T(8,128)S(1)} %get-tuple-element.25.w_ref, f32[2,16,128]{2,1,0:T(8,128)S(1)} %get-tuple-element.30.m0, f32[2,16,128]{2,1,0:T(8,128)S(1)} %collective-permute-done.5.m1, ...), custom_call_target="tpu_custom_call" | custom-call | bytes 4500000 | tf_op jit(solution)/shard_map/last_step/pallas_call | solution.py:536
  (2 shorter events, 0.0 us)
Async XLA Ops:
  0.0 10.5 %copy-start.3 = (s32[4,128]{1,0:T(4,128)S(1)}, s32[4,128]{1,0:T(4,128)}, u32[]{:S(2)}) copy-start(s32[4,128]{1,0:T(4,128)} %param.7) | copy-start | bytes 6148
  0.0 10.5 %copy-start.1 = (f32[2,3,4,128]{3,2,1,0:T(4,128)S(1)}, f32[2,3,4,128]{3,2,1,0:T(4,128)}, u32[]{:S(2)}) copy-start(f32[2,3,4,128]{3,2,1,0:T(4,128)} %param.5) | copy-start | bytes 36868
  0.0 10.5 %copy-start.2 = (f32[4,128]{1,0:T(4,128)S(1)}, f32[4,128]{1,0:T(4,128)}, u32[]{:S(2)}) copy-start(f32[4,128]{1,0:T(4,128)} %param.6) | copy-start | bytes 6148
  4.3 22.8 %collective-permute-start = (f32[2,9,9,16,128]{4,3,2,1,0:T(8,128)}, f32[2,9,9,16,128]{4,3,2,1,0:T(8,128)S(1)}, u32[]{:S(2)}, u32[]{:S(2)}) collective-permute-start(f32[2,9,9,16,128]{4,3,2,1,0:T(8,128)} %get-tuple-element.18.mr), channel_id=1, source_target_pairs={{0,1},{1,2},{2,3},{3,4},{4,5},{5,6},{6,7},{7,8},{8,9},{9,10},{10,1... | collective-permute-start | bytes 3981320 | tf_op jit(solution)/shard_map/ppermute | solution.py:576
  4.4 23.2 %collective-permute-start.1 = (f32[2,9,9,16,128]{4,3,2,1,0:T(8,128)}, f32[2,9,9,16,128]{4,3,2,1,0:T(8,128)S(1)}, u32[]{:S(2)}, u32[]{:S(2)}) collective-permute-start(f32[2,9,9,16,128]{4,3,2,1,0:T(8,128)} %get-tuple-element.19.ml), channel_id=1, source_target_pairs={{1,0},{2,1},{3,2},{4,3},{5,4},{6,5},{7,6},{8,7},{9,8},{10,9},{11,1... | collective-permute-start | bytes 3981320 | tf_op jit(solution)/shard_map/ppermute | solution.py:577
  11.6 17.6 %all-to-all-start = ((f32[128,2,128]{2,1,0:T(2,128)}), f32[128,2,128]{2,1,0:T(2,128)S(1)}, u32[]{:S(2)}, u32[]{:S(2)}) async-start(f32[128,2,128]{2,1,0:T(2,128)} %forcing.1), calls=%async_computation | async-start | bytes 262144 | tf_op jit(solution)/shard_map/all_to_all | solution.py:575
  29.2 1.7 %copy-start = (f32[2,9,9,16,128]{4,3,2,1,0:T(8,128)S(1)}, f32[2,9,9,16,128]{4,3,2,1,0:T(8,128)}, u32[]{:S(2)}) copy-start(f32[2,9,9,16,128]{4,3,2,1,0:T(8,128)} %get-tuple-element.18.mr) | copy-start | bytes 3981316
  35.4 5.5 %collective-permute-start.4 = (f32[2,2,16,128]{3,2,1,0:T(8,128)S(1)}, f32[2,2,16,128]{3,2,1,0:T(8,128)S(1)}, u32[]{:S(2)}, u32[]{:S(2)}) collective-permute-start(f32[2,2,16,128]{3,2,1,0:T(8,128)S(1)} %get-tuple-element.27.m0), channel_id=1, source_target_pairs={{0,64},{32,96},{64,0},{96,32},{1,65},{33,97},{65,1},{97,33},{2,66}... | collective-permute-start | bytes 98312 | tf_op jit(solution)/shard_map/ppermute | solution.py:558
  38.6 5.1 %collective-permute-start.3 = (f32[2,2,16,128]{3,2,1,0:T(8,128)S(1)}, f32[2,2,16,128]{3,2,1,0:T(8,128)S(1)}, u32[]{:S(2)}, u32[]{:S(2)}) collective-permute-start(f32[2,2,16,128]{3,2,1,0:T(8,128)S(1)} %get-tuple-element.27.m0), channel_id=1, source_target_pairs={{0,96},{32,64},{64,32},{96,0},{1,97},{33,65},{65,33},{97,1},{2,98}... | collective-permute-start | bytes 98312 | tf_op jit(solution)/shard_map/ppermute | solution.py:558
  39.6 4.0 %collective-permute-start.2 = (f32[2,2,16,128]{3,2,1,0:T(8,128)S(1)}, f32[2,2,16,128]{3,2,1,0:T(8,128)S(1)}, u32[]{:S(2)}, u32[]{:S(2)}) collective-permute-start(f32[2,2,16,128]{3,2,1,0:T(8,128)S(1)} %get-tuple-element.27.m0), channel_id=1, source_target_pairs={{0,32},{32,0},{64,96},{96,64},{1,33},{33,1},{65,97},{97,65},{2,34}... | collective-permute-start | bytes 98312 | tf_op jit(solution)/shard_map/ppermute | solution.py:558
  46.7 5.5 %collective-permute-start.7 = (f32[2,16,128]{2,1,0:T(8,128)S(1)}, f32[2,16,128]{2,1,0:T(8,128)S(1)}, u32[]{:S(2)}, u32[]{:S(2)}) collective-permute-start(f32[2,16,128]{2,1,0:T(8,128)S(1)} %get-tuple-element.30.m0), channel_id=1, source_target_pairs={{0,64},{32,96},{64,0},{96,32},{1,65},{33,97},{65,1},{97,33},{2,66}... | collective-permute-start | bytes 49160 | tf_op jit(solution)/shard_map/ppermute | solution.py:558
  48.3 4.9 %collective-permute-start.6 = (f32[2,16,128]{2,1,0:T(8,128)S(1)}, f32[2,16,128]{2,1,0:T(8,128)S(1)}, u32[]{:S(2)}, u32[]{:S(2)}) collective-permute-start(f32[2,16,128]{2,1,0:T(8,128)S(1)} %get-tuple-element.30.m0), channel_id=1, source_target_pairs={{0,96},{32,64},{64,32},{96,0},{1,97},{33,65},{65,33},{97,1},{2,98}... | collective-permute-start | bytes 49160 | tf_op jit(solution)/shard_map/ppermute | solution.py:558
  49.4 3.9 %collective-permute-start.5 = (f32[2,16,128]{2,1,0:T(8,128)S(1)}, f32[2,16,128]{2,1,0:T(8,128)S(1)}, u32[]{:S(2)}, u32[]{:S(2)}) collective-permute-start(f32[2,16,128]{2,1,0:T(8,128)S(1)} %get-tuple-element.30.m0), channel_id=1, source_target_pairs={{0,32},{32,0},{64,96},{96,64},{1,33},{33,1},{65,97},{97,65},{2,34}... | collective-permute-start | bytes 49160 | tf_op jit(solution)/shard_map/ppermute | solution.py:558
